TPU v7x, 32 devices: a whole 2x2x4 slice. The times are simulated.
32 devices in a mesh: lat: 16 (over z, y, core), lon: 2 (over x).
Axes of the slice: x: 2, y: 2, z: 4, core: 2. Of those that a mesh axis runs over, the one named last changes fastest.
Arguments:
- inputs: bfloat16 [1024, 128, 128], P('lat', 'lon'), may hold values from -6 to 6
- w_first: bfloat16 [221184], P(('lat', 'lon')), may hold values from -0.1875 to 0.1875
- w_second: bfloat16 [331776], P(('lat', 'lon')), may hold values from -0.15625 to 0.15625
- w_third: bfloat16 [331776], P(('lat', 'lon')), may hold values from -0.15625 to 0.15625
- cotangent: bfloat16 [512, 64, 192], P('lat', 'lon'), may hold values from -6 to 6
Outputs:
- features: bfloat16 [512, 64, 192], P('lat', 'lon')
- grad_input: bfloat16 [1024, 128, 128], P('lat', 'lon')
- grad_first: float32 [221184], P(('lat', 'lon'))
- grad_second: float32 [331776], P(('lat', 'lon'))
- grad_third: float32 [331776], P(('lat', 'lon'))
All inputs are finite; a program needn't handle non-finite values.
Results may differ from a plain program's by a relative error of at most 0.011.
Values may be sent and summed in bfloat16 or wider, within the bound.
No kernel may reach another device: no remote copies, remote signals or barrier semaphores. Data moves between devices by JAX's collectives and lax.ppermute only.
A program may use at most 64 MiB of HBM per device.

v0:
```python
import functools

import jax
import jax.numpy as jnp
from jax import lax
from jax.experimental import pallas as pl
from jax.experimental.pallas import tpu as pltpu
from jax.sharding import PartitionSpec as P

LOSS_CELLS = 1024
BOTH = ("lat", "lon")
F32 = jnp.float32
BF16 = jnp.bfloat16


class Slice:
    def __init__(self):
        lat, lon = lax.axis_size("lat"), lax.axis_size("lon")
        core = 2 if lat % 2 == 0 else 1
        near = 2 if (lat // core) % 2 == 0 else 1
        self.sizes = (lat // core // near, near, core, lon)
        self.count = lat * lon

    def coords(self, index):
        out = []
        for size in reversed(self.sizes):
            if isinstance(index, int):
                out.append(index % size)
                index = index // size
            else:
                out.append(lax.rem(index, size))
                index = lax.div(index, size)
        return tuple(reversed(out))

    def index(self, coords):
        total = 0
        for at, size in zip(coords, self.sizes):
            total = total * size + at
        return total

    def moved(self, coords, steps, sign=1):
        out = []
        for at, by, size in zip(coords, steps, self.sizes):
            to = at + sign * by + size
            out.append(to % size if isinstance(to, int) else lax.rem(to, size))
        return tuple(out)

    def send(self, value, steps):
        pairs = []
        for source in range(self.count):
            pairs.append((source, self.index(self.moved(self.coords(source), steps))))
        return lax.ppermute(value, BOTH, pairs)


def gathered(devices, shard):
    far, near, core, lon = devices.sizes
    line = jnp.stack([shard] + [devices.send(shard, (f, 0, 0, 0)) for f in range(1, far)])
    planes, parts = [], []
    for c in range(core):
        for n in range(near):
            for o in range(lon):
                if c:
                    plane = devices.send(planes[n * lon + o], (0, 0, c, 0))
                else:
                    plane = line if n == o == 0 else devices.send(line, (0, n, 0, o))
                planes.append(plane)
                parts.append((c, n, o))
    return planes, parts


def summed(devices, chunks):
    far, near, core, lon = devices.sizes

    def add(terms):
        total = terms[0].astype(F32)
        for term in terms[1:]:
            total = total + term.astype(F32)
        return total

    half = add([chunks[0]] + [devices.send(chunks[c], (0, 0, c, 0)) for c in range(1, core)])
    half = half.astype(BF16)
    terms = []
    for n in range(near):
        for o in range(lon):
            part = half[n * lon + o]
            terms.append(part if n == o == 0 else devices.send(part, (0, n, 0, o)))
    line = add(terms).astype(BF16)
    return add([line[0]] + [devices.send(line[f], (f, 0, 0, 0)) for f in range(1, far)])


def order(devices, sign):
    far, near, core, lon = devices.sizes
    me = lax.axis_index("lat") * lon + lax.axis_index("lon")
    mine = devices.coords(me)
    places = []
    for c in range(core):
        for n in range(near):
            for o in range(lon):
                for f in range(far):
                    places.append(devices.index(devices.moved(mine, (f, n, c, o), sign)))
    return jnp.stack(places)


def widened(block, low, high):
    count = lax.axis_size("lon")
    east = [(i, (i + 1) % count) for i in range(count)]
    west = [(i, (i - 1) % count) for i in range(count)]
    before = lax.ppermute(block[:, -low:], "lon", east)
    after = lax.ppermute(block[:, :high], "lon", west)
    block = jnp.concatenate([before, block, after], axis=1)
    count = lax.axis_size("lat")
    south = [(i, i + 1) for i in range(count - 1)]
    north = [(i + 1, i) for i in range(count - 1)]
    before = lax.ppermute(block[-low:], "lat", south)
    after = lax.ppermute(block[:high], "lat", north)
    return jnp.concatenate([before, block, after], axis=0)


LEFT = 16
ABOVE = 5
BELOW = 7
GUARD = 8
HALF = 64

FRINGE = (((0, 0, 0),), ((0, 1, 0),), ((0, 2, 0),), ((0, 0, 1), (0, 1, 1)), ((0, 2, 1), (1, 2, 1)))
MIDDLE = (((1, 0, 0),), ((1, 1, 0),), ((1, 2, 0),), ((1, 0, 1), (1, 1, 1)))
LAST = (((2, 0, 0),), ((2, 1, 0),), ((2, 2, 0),), ((2, 0, 1), (2, 1, 1)), ((2, 2, 1), None))
BLOCKS = FRINGE + MIDDLE + LAST


def low_lanes(rows):
    return lax.broadcasted_iota(jnp.int32, (rows, 128), 1) < HALF


def swapped(value):
    return pltpu.roll(value, HALF, 1)


def prepare(rows, cols, x_ref, c_ref, windows_ref, cot_ref, wide, cot_a, cot_b):
    pitch = cols + LEFT
    height = rows + ABOVE + BELOW
    span = wide.shape[0] // (2 * height + 4)
    wide[...] = jnp.zeros_like(wide)
    cot_a[...] = jnp.zeros_like(cot_a)
    cot_b[...] = jnp.zeros_like(cot_b)
    high, across = x_ref.shape[0], x_ref.shape[1]

    def spread(i, _):
        start = pl.multiple_of((i + 4) * span + 16, 8)
        wide[pl.ds(start, across), :] = x_ref[i].astype(F32)
        return 0

    lax.fori_loop(0, high, spread, 0)

    def window(k, _):
        for parity in range(2):
            row = 2 * (k - ABOVE) + 13 + parity
            for tap in range(3):
                base = row * span + 24 + tap
                mid = wide[pl.ds(base, cols, stride=2), :]
                before = wide[pl.ds(base - 16, 8, stride=2), :]
                after = wide[pl.ds(base - 2 * span + 2 * cols, 8, stride=2), :]
                lane = (3 * parity + tap) * 128
                cells = jnp.concatenate([after, before, mid], axis=0).astype(BF16)
                windows_ref[pl.ds(pl.multiple_of(k * pitch, 16), pitch), lane : lane + 128] = cells
        return 0

    lax.fori_loop(0, height, window, 0)
    for i in range(c_ref.shape[0]):
        value = c_ref[i].astype(F32)
        start = GUARD + (i - 2 + ABOVE) * pitch + LEFT - 2
        cot_a[start : start + value.shape[0], :] = value[:, :128]
        cot_b[start : start + value.shape[0], 0:HALF] = value[:, 128:]
    size = height * pitch
    cot_ref[:, :128] = cot_a[GUARD : GUARD + size, :].astype(BF16)
    part = cot_b[GUARD : GUARD + size, :]
    cot_ref[:, 128:] = jnp.where(low_lanes(size), part, swapped(part)).astype(BF16)


def level(
    shape,
    devices,
    parts,
    x_ref,
    c_ref,
    *refs,
):
    rows, cols, chan_in, mid, factor, whole = shape
    planes = refs[: len(parts)]
    (
        features_ref,
        input_ref,
        terms_ref,
        chunks,
        outgoing,
        in_sems,
        out_sems,
        flat,
        k_a,
        k_b,
        w_one,
        w_two,
        w_three,
        t_two,
        t_three,
        t_one,
        f_a,
        f_b,
        slope,
        win_one,
        win_two,
        win_delta,
        spread,
        image,
    ) = refs[len(parts) :]
    pitch = cols + LEFT
    height = rows + ABOVE + BELOW
    size = height * pitch
    far, near, core, lon = devices.sizes
    sections = ((0, chan_in), (1, mid), (2, mid))
    count = chunks.shape[0]
    share = [9 * c * mid // 128 // count for _, c in sections]
    begin = [0, share[0], share[0] + share[1]]

    lat_at = lax.axis_index("lat")
    mine = devices.coords(lat_at * lon + lax.axis_index("lon"))

    copies = []
    for place, (steps_at, plane) in enumerate(zip(parts, planes)):
        for f in range(plane.shape[0]):
            if whole:
                owner = 0
            else:
                c, n, o = steps_at
                owner = devices.index(devices.moved(mine, (f, n, c, o), -1))
            copy = pltpu.make_async_copy(
                plane.at[f], chunks.at[owner], in_sems.at[len(copies)]
            )
            copy.start()
            copies.append(copy)
    f_a[...] = jnp.zeros_like(f_a)
    f_b[...] = jnp.zeros_like(f_b)
    slope[...] = jnp.zeros_like(slope)
    for copy in copies:
        copy.wait()

    def unpack(which, channels):
        n = share[which]
        for k in range(count):
            flat[k * n : (k + 1) * n, :] = chunks[
                k, begin[which] // 16 * 16 : -(-(begin[which] + n) // 16) * 16, :
            ].astype(F32)[begin[which] % 16 : begin[which] % 16 + n]
        pairs = 9 * channels // 2
        step = 96

        def one(i, _):
            at = i * step
            first = flat[pl.ds(3 * at, step, stride=3), :]
            second = flat[pl.ds(3 * at + 1, step, stride=3), :]
            third = flat[pl.ds(3 * at + 2, step, stride=3), :]
            low = low_lanes(step)
            second_r, third_r = swapped(second), swapped(third)
            k_a[pl.ds(2 * at, step, stride=2), :] = first
            k_b[pl.ds(2 * at, step, stride=2), :] = jnp.where(low, second, second_r)
            k_a[pl.ds(2 * at + 1, step, stride=2), :] = jnp.where(low, second_r, third_r)
            k_b[pl.ds(2 * at + 1, step, stride=2), :] = jnp.where(low, third_r, third)
            return 0

        lax.fori_loop(0, pairs // step, one, 0)

    def tap_rows(tap, part):
        start = (3 * tap[0] + tap[1]) * mid + 128 * part
        return start, start + (HALF if part else 128)

    def forward(target):
        at = 0
        for block in BLOCKS:
            for tap in block:
                if tap is None:
                    target[at : at + HALF, :] = jnp.zeros((HALF, 256), BF16)
                    at += HALF
                    continue
                lo, hi = tap_rows(tap, tap[2])
                target[at : at + hi - lo, 0:128] = k_a[lo:hi, :].astype(BF16)
                target[at : at + hi - lo, 128:256] = k_b[lo:hi, :].astype(BF16)
                at += hi - lo

    def backward(target):
        low = low_lanes(mid)
        for i, block in enumerate(BLOCKS):
            values = []
            for tap in block:
                if tap is None:
                    values.append(jnp.zeros((mid, 128), F32))
                    continue
                lo = (3 * (2 - tap[0]) + 2 - tap[1]) * mid
                source = k_b if tap[2] else k_a
                values.append(source[lo : lo + mid, :])
            value = values[0] if len(values) == 1 else jnp.where(low, values[0], values[1])
            value = value.astype(BF16)
            target[0:mid, 128 * i : 128 * i + 128] = value
            target[mid:256, 128 * i : 128 * i + 128] = value[128:mid]

    unpack(0, chan_in)
    w_one[:, 0:128] = k_a[0 : 9 * chan_in, :].astype(BF16)
    w_one[:, 128:256] = k_b[0 : 9 * chan_in, :].astype(BF16)
    empty = jnp.zeros((chan_in, 128), F32)
    low_in = low_lanes(chan_in)
    phases = (
        ((1, 1), None, None, None),
        ((1, 2), (1, 0), None, None),
        ((2, 1), None, (0, 1), None),
        ((2, 2), (2, 0), (0, 2), (0, 0)),
    )
    for i, taps in enumerate(phases):
        a, b = [], []
        for tap in taps:
            if tap is None:
                a.append(empty)
                b.append(empty)
            else:
                lo = (3 * tap[0] + tap[1]) * chan_in
                a.append(k_a[lo : lo + chan_in, :])
                b.append(k_b[lo : lo + chan_in, :])
        blocks = (
            a[0],
            a[1],
            jnp.where(low_in, b[0], b[1]),
            a[2],
            a[3],
            jnp.where(low_in, b[2], b[3]),
        )
        for j, block in enumerate(blocks):
            t_one[chan_in * i : chan_in * (i + 1), 128 * j : 128 * j + 128] = block.astype(BF16)
    unpack(1, mid)
    forward(w_two)
    backward(t_two)
    unpack(2, mid)
    forward(w_three)
    backward(t_three)

    first_row = lat_at * rows
    bottom = lax.axis_size("lat") * rows - first_row
    low_cell = (jnp.maximum(-first_row, -ABOVE) + ABOVE) * pitch + 8
    high_cell = (jnp.minimum(bottom, rows + BELOW) + ABOVE) * pitch + 8

    def inside(start, n):
        cell = start + lax.broadcasted_iota(jnp.int32, (n, 128), 0)
        return (cell >= low_cell) & (cell < high_cell)

    def store(start, n, left, right, mask):
        if mask:
            keep = inside(start, n)
            left = jnp.where(keep, left, 0.0)
            right = jnp.where(keep, right, 0.0)
        at = pl.multiple_of(start + GUARD, 8)
        f_a[pl.ds(at, n), :] = left
        f_b[pl.ds(at, n), :] = right

    def windows(target, top, under):
        def one(i, _):
            cell = i * pitch
            q = cell + GUARD
            low = low_lanes(pitch)
            b_0, b_1, b_2 = (f_b[pl.ds(q + s, pitch), :] for s in (-1, 0, 1))
            b_3 = f_b[pl.ds(q + 1 + pitch, pitch), :]
            out = [f_a[pl.ds(q + s, pitch), :] for s in (-1, 0, 1)]
            out += [jnp.where(low, b_0, b_1), jnp.where(low, b_2, b_3)]
            at = pl.multiple_of(cell, 16)
            for j, value in enumerate(out):
                target[pl.ds(at, pitch), 128 * j : 128 * j + 128] = value.astype(BF16)
            return 0

        lax.fori_loop(top + ABOVE, under + ABOVE, one, 0)

    def convolve(source, weights, turned, halo, steps, finish):
        start = (ABOVE - halo) * pitch
        total = (rows + 1 + 2 * halo) * pitch + LEFT
        n = -(-total // steps // 16) * 16
        contract = (((1,), (1,)), ((), ())) if turned else (((1,), (0,)), ((), ()))

        def one(i, _):
            p = pl.multiple_of(start + i * n, 16)
            above = source[pl.ds(pl.multiple_of(p - pitch, 16), n), :]
            here = source[pl.ds(p, n), 0:512]
            below = source[pl.ds(pl.multiple_of(p + pitch, 16), n), :]
            value = lax.dot_general(
                jnp.concatenate([above, here, below], axis=1),
                weights[...],
                contract,
                preferred_element_type=F32,
            )
            finish(p, n, value)
            return 0

        lax.fori_loop(0, steps, one, 0)

    def own(ref, lanes, row_step=0, shift=0, offset=0):
        pieces = []
        for r in range(rows):
            at = offset + (ABOVE + r + row_step) * pitch + LEFT + shift
            pieces.append(ref[at : at + cols, lanes])
        return jnp.concatenate(pieces, axis=0)

    ALL = slice(0, 128)

    def turned_deltas():
        left = own(f_a, ALL, offset=GUARD)
        right = own(f_b, ALL, offset=GUARD)
        return jnp.concatenate([left.T, right.T], axis=0).astype(BF16)

    def pack(which, channels):
        step = 96

        def one(i, _):
            at = i * step
            even_a = k_a[pl.ds(2 * at, step, stride=2), :]
            even_b = k_b[pl.ds(2 * at, step, stride=2), :]
            odd_a = swapped(k_a[pl.ds(2 * at + 1, step, stride=2), :])
            odd_b = k_b[pl.ds(2 * at + 1, step, stride=2), :]
            low = low_lanes(step)
            flat[pl.ds(3 * at, step, stride=3), :] = even_a
            flat[pl.ds(3 * at + 1, step, stride=3), :] = jnp.where(low, even_b, odd_a)
            flat[pl.ds(3 * at + 2, step, stride=3), :] = jnp.where(low, odd_a, odd_b)
            return 0

        lax.fori_loop(0, 9 * channels // 2 // step, one, 0)
        n = share[which]
        for k in range(count):
            outgoing[k, begin[which] : begin[which] + n, :] = flat[k * n : (k + 1) * n, :]

    def field_grad(which, source):
        turned = turned_deltas()
        for a, blocks in enumerate((FRINGE, MIDDLE, LAST)):
            lanes = slice(0, 128 * len(blocks))
            product = lax.dot_general(
                turned,
                own(source, lanes, a - 1),
                (((1,), (0,)), ((), ())),
                preferred_element_type=F32,
            )
            product = product * factor
            for j, block in enumerate(blocks):
                left = product[0:128, 128 * j : 128 * j + 128].T
                right = product[128:256, 128 * j : 128 * j + 128].T
                at = 0
                for tap in block:
                    if tap is None:
                        continue
                    lo, hi = tap_rows(tap, tap[2])
                    k_a[lo:hi, :] = left[at : at + hi - lo]
                    k_b[lo:hi, :] = right[at : at + hi - lo]
                    at += hi - lo
        pack(which, mid)

    def convolve_first():
        halo, steps = 4, 4
        start = (ABOVE - halo) * pitch
        total = (rows + 1 + 2 * halo) * pitch + LEFT
        n = -(-total // steps // 16) * 16

        def one(i, _):
            p = pl.multiple_of(start + i * n, 16)
            above = x_ref[pl.ds(pl.multiple_of(p - pitch, 16), n), 384:768]
            here = x_ref[pl.ds(p, n), :]
            value = lax.dot_general(
                jnp.concatenate([above, here], axis=1),
                w_one[...],
                (((1,), (0,)), ((), ())),
                preferred_element_type=F32,
            )
            store(p, n, value[:, :128], value[:, 128:], True)
            return 0

        lax.fori_loop(0, steps, one, 0)

    convolve_first()
    windows(win_one, -4, rows + 6)

    def finish_two(p, n, value):
        s = jax.nn.sigmoid(value)
        active = value * s
        slope[pl.ds(p, n), :] = s + active * (1.0 - s)
        store(p, n, active[:, :128], active[:, 128:], True)

    convolve(win_one, w_two, False, 3, 4, finish_two)
    windows(win_two, -3, rows + 5)

    def finish_three(p, n, value):
        s = jax.nn.sigmoid(value)
        active = value * s
        delta = c_ref[pl.ds(p, n), :].astype(F32) * (s + active * (1.0 - s))
        store(p, n, delta[:, :128], delta[:, 128:], False)
        spread[pl.ds(p, n), :] = active

    convolve(win_two, w_three, False, 2, 4, finish_three)
    for r in range(rows):
        at = (ABOVE + r) * pitch + LEFT
        features_ref[r] = spread[at : at + cols, 0:mid].astype(BF16)
    field_grad(2, win_two)
    windows(win_delta, -2, rows + 4)

    def finish_delta(p, n, value):
        value = value * slope[pl.ds(p, n), :]
        store(p, n, value[:, :128], value[:, 128:], True)

    convolve(win_delta, t_three, True, 1, 4, finish_delta)
    field_grad(1, win_one)
    windows(win_delta, -1, rows + 3)

    def finish_back(p, n, value):
        store(p, n, value[:, :128], value[:, 128:], True)

    convolve(win_delta, t_two, True, 0, 4, finish_back)
    turned = turned_deltas()
    for a, (step, lanes) in enumerate(((-1, slice(384, 768)), (0, slice(0, 384)), (0, slice(384, 768)))):
        product = lax.dot_general(
            turned,
            own(x_ref, lanes, step),
            (((1,), (0,)), ((), ())),
            preferred_element_type=F32,
        )
        product = product * factor
        lo = 3 * a * chan_in
        k_a[lo : lo + 3 * chan_in, :] = product[0:128].T
        k_b[lo : lo + 3 * chan_in, :] = product[128:256].T
    pack(0, chan_in)

    sends = []
    for k in range(count):
        chunks[k] = outgoing[k].astype(BF16)
        place = 0
        if not whole:
            distance = tuple(
                lax.rem(to - at + by, by)
                for to, at, by in zip(devices.coords(k), mine, devices.sizes)
            )
            f, n, c, o = distance
            place = ((c * near + n) * lon + o) * far + f
        copy = pltpu.make_async_copy(chunks.at[k], terms_ref.at[place], out_sems.at[k])
        copy.start()
        sends.append(copy)

    low = low_lanes(rows * cols)

    def four(ref):
        return [own(ref, ALL, r, c, GUARD) for r, c in ((0, 0), (0, 1), (1, 0), (1, 1))]

    a, b = four(f_a), four(f_b)
    around = (a[0], a[1], jnp.where(low, b[0], b[1]), a[2], a[3], jnp.where(low, b[2], b[3]))
    around = jnp.concatenate([value.astype(BF16) for value in around], axis=1)
    for r in range(2):
        wide = 384 * (r + 1)
        product = lax.dot_general(
            around[:, :wide],
            t_one[2 * chan_in * r : 2 * chan_in * (r + 1), :wide],
            (((1,), (1,)), ((), ())),
            preferred_element_type=F32,
        )
        for i in range(rows):
            at = i * cols
            base = (2 * i + r) * 2 * cols
            for c in range(2):
                spread_in = product[at : at + cols, chan_in * c : chan_in * (c + 1)]
                image[pl.ds(base + c, cols, stride=2), :] = spread_in
    for i in range(2 * rows):
        input_ref[i] = image[2 * cols * i : 2 * cols * (i + 1), :].astype(BF16)
    for copy in sends:
        copy.wait()


VMEM = pl.BlockSpec(memory_space=pltpu.VMEM)
ANY = pl.BlockSpec(memory_space=pl.ANY)


def local(inputs, w_first, w_second, w_third, cotangent):
    devices = Slice()
    rows, cols, mid = cotangent.shape
    chan_in = inputs.shape[2]
    factor = 1.0 / LOSS_CELLS
    far, near, core, lon = devices.sizes
    held = (w_first.shape[0], w_second.shape[0], w_third.shape[0])
    shard = jnp.concatenate([w_first, w_second, w_third]).reshape(-1, 128)
    whole = any(n % 128 for n in held)
    if not whole:
        shard = jnp.pad(shard, ((0, -shard.shape[0] % 16), (0, 0)))
    planes, parts = gathered(devices, shard)
    if whole:
        chunks = jnp.stack(planes).reshape(devices.count, -1)
        chunks = jnp.take(chunks, jnp.argsort(order(devices, -1)), axis=0)
        pieces = jnp.split(chunks, (held[0], held[0] + held[1]), axis=1)
        chunks = jnp.concatenate([piece.reshape(-1) for piece in pieces])
        planes, parts = [chunks.reshape(1, -1, 128)], [(0, 0, 0)]
    count = 1 if whole else devices.count
    depth = planes[0].shape[1]

    wide_in = widened(inputs, 9, 10)
    wide_cot = widened(cotangent, 2, 3)
    size = (rows + ABOVE + BELOW) * (cols + LEFT)
    field = pltpu.VMEM((size + 2 * GUARD, 128), F32)
    tall = 2 * (rows + ABOVE + BELOW) + 4
    across = -(-(wide_in.shape[1] + 29) // 16) * 16
    padded, cot = pl.pallas_call(
        functools.partial(prepare, rows, cols),
        out_shape=(
            jax.ShapeDtypeStruct((size, 6 * chan_in), BF16),
            jax.ShapeDtypeStruct((size, 256), BF16),
        ),
        in_specs=[VMEM] * 2,
        out_specs=(VMEM, VMEM),
        scratch_shapes=[pltpu.VMEM((tall * across, 128), F32), field, field],
        compiler_params=pltpu.CompilerParams(vmem_limit_bytes=40 * 2**20),
        cost_estimate=pl.CostEstimate(flops=0, bytes_accessed=12 * 2**20, transcendentals=0),
    )(wide_in, wide_cot)

    cells = pltpu.VMEM((size, 640), BF16)
    shape = (rows, cols, chan_in, mid, factor, whole)
    features, grad_input, terms = pl.pallas_call(
        functools.partial(level, shape, devices, parts),
        out_shape=(
            jax.ShapeDtypeStruct((rows, cols, mid), BF16),
            jax.ShapeDtypeStruct((2 * rows, 2 * cols, chan_in), BF16),
            jax.ShapeDtypeStruct((count, depth, 128), BF16),
        ),
        in_specs=[VMEM] * 2 + [ANY] * len(planes),
        out_specs=(VMEM, VMEM, ANY),
        scratch_shapes=[
            pltpu.VMEM((count, depth, 128), BF16),
            pltpu.VMEM((count, depth, 128), F32),
            pltpu.SemaphoreType.DMA((count,)),
            pltpu.SemaphoreType.DMA((count,)),
            pltpu.VMEM((9 * mid * mid // 128, 128), F32),
            pltpu.VMEM((9 * mid, 128), F32),
            pltpu.VMEM((9 * mid, 128), F32),
            pltpu.VMEM((9 * chan_in, 256), BF16),
            pltpu.VMEM((128 * len(BLOCKS), 256), BF16),
            pltpu.VMEM((128 * len(BLOCKS), 256), BF16),
            pltpu.VMEM((256, 128 * len(BLOCKS)), BF16),
            pltpu.VMEM((256, 128 * len(BLOCKS)), BF16),
            pltpu.VMEM((4 * chan_in, 768), BF16),
            field,
            field,
            pltpu.VMEM((size, 256), F32),
            cells,
            cells,
            cells,
            pltpu.VMEM((size, 256), F32),
            pltpu.VMEM((4 * rows * cols, 128), F32),
        ],
        compiler_params=pltpu.CompilerParams(vmem_limit_bytes=60 * 2**20),
        cost_estimate=pl.CostEstimate(
            flops=6 * 10**9, bytes_accessed=16 * 2**20, transcendentals=10**6
        ),
    )(padded, cot, *planes)
    if whole:
        cuts = (held[0] * devices.count, (held[0] + held[1]) * devices.count)
        pieces = jnp.split(terms.reshape(-1), cuts)
        terms = [piece.reshape(devices.count, -1) for piece in pieces]
        terms = jnp.take(jnp.concatenate(terms, axis=1), order(devices, 1), axis=0)
    terms = terms.reshape(core, near * lon, far, -1, 128)
    total = summed(devices, terms).reshape(-1)[: sum(held)]
    grad_first, grad_second, grad_third = jnp.split(total, (held[0], held[0] + held[1]))
    return (features, grad_input, grad_first, grad_second, grad_third)


def solution(mesh):
    tile = P("lat", "lon", None)
    flat = P(("lat", "lon"))
    return jax.shard_map(
        local,
        mesh=mesh,
        in_specs=(tile, flat, flat, flat, tile),
        out_specs=(tile, tile, flat, flat, flat),
        check_vma=False,
    )
```

profile of v0, /device:TPU:0, one launch (start us, length us, event | category | flops | bytes accessed | tf_op | source)
XLA Modules:
  0.0 110.2 jit_solution(11349522908200742814)
XLA Ops:
  1.7 3.0 %collective-permute-start.4 = (bf16[32,2,192]{2,1,0:T(2,128)(2,1)S(1)}, bf16[32,2,192]{2,1,0:T(2,128)(2,1)S(1)}, u32[]{:S(2)}, u32[]{:S(2)}) collective-permute-start(bf16[32,2,192]{2,1,0:T(2,128)(2,1)S(1)} %slice.68), channel_id=1, source_target_pairs={{0,1},{1,0},{2,3},{3,2},{4,5},{5,4},{6,7},{7,6},{8,9},{9,8},{10,11... | collective-permute-start | bytes 73736 | tf_op jit(solution)/shard_map/ppermute | solution.py:108
  6.5 3.2 %collective-permute-start.9 = (bf16[224,128]{1,0:T(8,128)(2,1)S(1)}, bf16[224,128]{1,0:T(8,128)(2,1)S(1)}, u32[]{:S(2)}, u32[]{:S(2)}) collective-permute-start(bf16[224,128]{1,0:T(8,128)(2,1)S(1)} %get-tuple-element.26), channel_id=1, source_target_pairs={{0,16},{1,17},{2,18},{3,19},{4,20},{5,21},{6,22},{7,23},{8,24},{9,... | collective-permute-start | bytes 172040 | tf_op jit(solution)/shard_map/ppermute | solution.py:52
  9.7 1.6 %collective-permute-start.8 = (bf16[224,128]{1,0:T(8,128)(2,1)S(1)}, bf16[224,128]{1,0:T(8,128)(2,1)S(1)}, u32[]{:S(2)}, u32[]{:S(2)}) collective-permute-start(bf16[224,128]{1,0:T(8,128)(2,1)S(1)} %get-tuple-element.26), channel_id=1, source_target_pairs={{0,8},{1,9},{2,10},{3,11},{4,12},{5,13},{6,14},{7,15},{8,16},{9,17... | collective-permute-start | bytes 172040 | tf_op jit(solution)/shard_map/ppermute | solution.py:52
  11.3 2.2 %collective-permute-start.10 = (bf16[224,128]{1,0:T(8,128)(2,1)S(1)}, bf16[224,128]{1,0:T(8,128)(2,1)S(1)}, u32[]{:S(2)}, u32[]{:S(2)}) collective-permute-start(bf16[224,128]{1,0:T(8,128)(2,1)S(1)} %get-tuple-element.26), channel_id=1, source_target_pairs={{0,24},{1,25},{2,26},{3,27},{4,28},{5,29},{6,30},{7,31},{8,0},{9,1... | collective-permute-start | bytes 172040 | tf_op jit(solution)/shard_map/ppermute | solution.py:52
  15.6 1.6 %collective-permute-start.1 = (bf16[64,10,128]{2,1,0:T(8,128)(2,1)S(1)}, bf16[64,10,128]{2,1,0:T(8,128)(2,1)S(1)}, u32[]{:S(2)}, u32[]{:S(2)}) collective-permute-start(bf16[64,10,128]{2,1,0:T(8,128)(2,1)S(1)} %slice.65), channel_id=1, source_target_pairs={{0,1},{1,0},{2,3},{3,2},{4,5},{5,4},{6,7},{7,6},{8,9},{9,8},{10,11... | collective-permute-start | bytes 491528 | tf_op jit(solution)/shard_map/ppermute | solution.py:109
  20.4 5.5 %collective-permute-start.13 = (bf16[4,224,128]{2,1,0:T(8,128)(2,1)S(1)}, bf16[4,224,128]{2,1,0:T(8,128)(2,1)S(1)}, u32[]{:S(2)}, u32[]{:S(2)}) collective-permute-start(bf16[4,224,128]{2,1,0:T(8,128)(2,1)S(1)} %pad_maximum_fusion.2.refs_0_), channel_id=1, source_target_pairs={{0,5},{1,4},{2,7},{3,6},{4,1},{5,0},{6,3},{7,2},{8,13},{9,12},{10,... | collective-permute-start | bytes 688136 | tf_op jit(solution)/shard_map/ppermute | solution.py:52
  25.9 4.0 %collective-permute-done = bf16[64,9,128]{2,1,0:T(8,128)(2,1)S(1)} collective-permute-done((bf16[64,9,128]{2,1,0:T(8,128)(2,1)S(1)}, bf16[64,9,128]{2,1,0:T(8,128)(2,1)S(1)}, u32[]{:S(2)}, u32[]{:S(2)}) %collective-permute-start) | collective-permute-done | bytes 147488 | tf_op jit(solution)/shard_map/ppermute | solution.py:108
  29.9 1.4 %collective-permute-start.12 = (bf16[4,224,128]{2,1,0:T(8,128)(2,1)S(1)}, bf16[4,224,128]{2,1,0:T(8,128)(2,1)S(1)}, u32[]{:S(2)}, u32[]{:S(2)}) collective-permute-start(bf16[4,224,128]{2,1,0:T(8,128)(2,1)S(1)} %pad_maximum_fusion.2.refs_0_), channel_id=1, source_target_pairs={{0,4},{1,5},{2,6},{3,7},{4,0},{5,1},{6,2},{7,3},{8,12},{9,13},{10,... | collective-permute-start | bytes 688136 | tf_op jit(solution)/shard_map/ppermute | solution.py:52
  31.3 1.5 %collective-permute-start.11 = (bf16[4,224,128]{2,1,0:T(8,128)(2,1)S(1)}, bf16[4,224,128]{2,1,0:T(8,128)(2,1)S(1)}, u32[]{:S(2)}, u32[]{:S(2)}) collective-permute-start(bf16[4,224,128]{2,1,0:T(8,128)(2,1)S(1)} %pad_maximum_fusion.2.refs_0_), channel_id=1, source_target_pairs={{0,1},{1,0},{2,3},{3,2},{4,5},{5,4},{6,7},{7,6},{8,9},{9,8},{10,11... | collective-permute-start | bytes 688136 | tf_op jit(solution)/shard_map/ppermute | solution.py:52
  32.9 1.3 %collective-permute-start.2 = (bf16[9,83,128]{2,1,0:T(8,128)(2,1)S(1)}, bf16[9,83,128]{2,1,0:T(8,128)(2,1)S(1)}, u32[]{:S(2)}, u32[]{:S(2)}) collective-permute-start(bf16[9,83,128]{2,1,0:T(8,128)(2,1)S(1)} %pad_maximum_fusion.5), channel_id=1, source_target_pairs={{0,2},{2,4},{4,6},{6,8},{8,10},{10,12},{12,14},{14,16},{16,18},{18... | collective-permute-start | bytes 573704 | tf_op jit(solution)/shard_map/ppermute | solution.py:114
  35.7 1.9 %collective-permute-start.14 = (bf16[4,224,128]{2,1,0:T(8,128)(2,1)S(1)}, bf16[4,224,128]{2,1,0:T(8,128)(2,1)S(1)}, u32[]{:S(2)}, u32[]{:S(2)}) collective-permute-start(bf16[4,224,128]{2,1,0:T(8,128)(2,1)S(1)} %pad_maximum_fusion.2.refs_0_), channel_id=1, source_target_pairs={{0,2},{1,3},{2,0},{3,1},{4,6},{5,7},{6,4},{7,5},{8,10},{9,11},{10,... | collective-permute-start | bytes 688136 | tf_op jit(solution)/shard_map/ppermute | solution.py:52
  39.4 2.2 %shard_map.92 = (bf16[2112,768]{1,0:T(8,128)(2,1)S(1)}, bf16[2112,256]{1,0:T(8,128)(2,1)S(1)}) custom-call(bf16[83,83,128]{2,1,0:T(8,128)(2,1)S(1)} %pad_maximum_fusion.x_ref, bf16[37,37,192]{2,1,0:T(8,128)(2,1)S(1)} %pad_maximum_fusion.1.c_ref), custom_call_target="tpu_custom_call" | custom-call | bytes 12582912 | tf_op jit(solution)/shard_map/pallas_call | solution.py:603
  41.6 1.7 %copy-done = bf16[2112,768]{1,0:T(8,128)(2,1)} copy-done((bf16[2112,768]{1,0:T(8,128)(2,1)}, bf16[2112,768]{1,0:T(8,128)(2,1)S(1)}, u32[]{:S(2)}) %copy-start) | copy-done | bytes 3244056
  45.2 31.0 %shard_map.93 = (bf16[32,32,192]{2,1,0:T(8,128)(2,1)}, bf16[64,64,128]{2,1,0:T(8,128)(2,1)}, bf16[32,224,128]{2,1,0:T(8,128)(2,1)}) custom-call(bf16[2112,768]{1,0:T(8,128)(2,1)} %copy-done, bf16[2112,256]{1,0:T(8,128)(2,1)} %copy-done.1, bf16[4,224,128]{2,1,0:T(8,128)(2,1)} %copy-done.4, bf16[4,224,128]{2,1,0:T(8,128)(2,1)} %copy-done.7, ...), custom_call_target="tpu_custom_call" | custom-call | flops 6000000000 | bytes 16777216 | tf_op jit(solution)/shard_map/pallas_call | solution.py:618
  76.2 1.6 %fusion.6 = (bf16[16,224,128]{2,1,0:T(8,128)(2,1)S(1)}, bf16[16,224,128]{2,1,0:T(8,128)(2,1)S(1)}) fusion(bf16[32,224,128]{2,1,0:T(8,128)(2,1)} %get-tuple-element.14), kind=kLoop, calls=%fused_computation.31 | loop fusion | bytes 3670016 | tf_op jit(solution)/shard_map/slice | solution.py:80
  77.8 4.4 %collective-permute-start.18 = (bf16[4,4,224,128]{3,2,1,0:T(8,128)(2,1)S(1)}, bf16[4,4,224,128]{3,2,1,0:T(8,128)(2,1)S(1)}, u32[]{:S(2)}, u32[]{:S(2)}) collective-permute-start(bf16[4,4,224,128]{3,2,1,0:T(8,128)(2,1)S(1)} %bitcast.39), channel_id=1, source_target_pairs={{0,2},{1,3},{2,0},{3,1},{4,6},{5,7},{6,4},{7,5},{8,10},{9,11},{10,... | collective-permute-start | bytes 2752520 | tf_op jit(solution)/shard_map/ppermute | solution.py:52
  82.1 2.1 %collective-permute-done.18 = bf16[4,4,224,128]{3,2,1,0:T(8,128)(2,1)S(1)} collective-permute-done((bf16[4,4,224,128]{3,2,1,0:T(8,128)(2,1)S(1)}, bf16[4,4,224,128]{3,2,1,0:T(8,128)(2,1)S(1)}, u32[]{:S(2)}, u32[]{:S(2)}) %collective-permute-start.18) | collective-permute-done | bytes 917536 | tf_op jit(solution)/shard_map/ppermute | solution.py:52
  85.2 2.4 %collective-permute-start.21 = (bf16[4,224,128]{2,1,0:T(8,128)(2,1)S(1)}, bf16[4,224,128]{2,1,0:T(8,128)(2,1)S(1)}, u32[]{:S(2)}, u32[]{:S(2)}) collective-permute-start(bf16[4,224,128]{2,1,0:T(8,128)(2,1)S(1)} %get-tuple-element.18), channel_id=1, source_target_pairs={{0,5},{1,4},{2,7},{3,6},{4,1},{5,0},{6,3},{7,2},{8,13},{9,12},{10,... | collective-permute-start | bytes 688136 | tf_op jit(solution)/shard_map/ppermute | solution.py:52
  88.1 4.9 %collective-permute-done.19 = bf16[4,224,128]{2,1,0:T(8,128)(2,1)S(1)} collective-permute-done((bf16[4,224,128]{2,1,0:T(8,128)(2,1)S(1)}, bf16[4,224,128]{2,1,0:T(8,128)(2,1)S(1)}, u32[]{:S(2)}, u32[]{:S(2)}) %collective-permute-start.19) | collective-permute-done | bytes 229408 | tf_op jit(solution)/shard_map/ppermute | solution.py:52
  93.0 5.4 %collective-permute-done.21 = bf16[4,224,128]{2,1,0:T(8,128)(2,1)S(1)} collective-permute-done((bf16[4,224,128]{2,1,0:T(8,128)(2,1)S(1)}, bf16[4,224,128]{2,1,0:T(8,128)(2,1)S(1)}, u32[]{:S(2)}, u32[]{:S(2)}) %collective-permute-start.21) | collective-permute-done | bytes 229408 | tf_op jit(solution)/shard_map/ppermute | solution.py:52
  98.4 1.4 %collective-permute-done.20 = bf16[4,224,128]{2,1,0:T(8,128)(2,1)S(1)} collective-permute-done((bf16[4,224,128]{2,1,0:T(8,128)(2,1)S(1)}, bf16[4,224,128]{2,1,0:T(8,128)(2,1)S(1)}, u32[]{:S(2)}, u32[]{:S(2)}) %collective-permute-start.20) | collective-permute-done | bytes 229408 | tf_op jit(solution)/shard_map/ppermute | solution.py:52
  100.6 3.2 %collective-permute-start.24 = (bf16[224,128]{1,0:T(8,128)(2,1)S(1)}, bf16[224,128]{1,0:T(8,128)(2,1)S(1)}, u32[]{:S(2)}, u32[]{:S(2)}) collective-permute-start(bf16[224,128]{1,0:T(8,128)(2,1)S(1)} %get-tuple-element.21), channel_id=1, source_target_pairs={{0,24},{1,25},{2,26},{3,27},{4,28},{5,29},{6,30},{7,31},{8,0},{9,1... | collective-permute-start | bytes 172040 | tf_op jit(solution)/shard_map/ppermute | solution.py:52
  103.8 2.2 %collective-permute-done.22 = bf16[224,128]{1,0:T(8,128)(2,1)S(1)} collective-permute-done((bf16[224,128]{1,0:T(8,128)(2,1)S(1)}, bf16[224,128]{1,0:T(8,128)(2,1)S(1)}, u32[]{:S(2)}, u32[]{:S(2)}) %collective-permute-start.22) | collective-permute-done | bytes 57376 | tf_op jit(solution)/shard_map/ppermute | solution.py:52
  106.0 2.9 %collective-permute-done.23 = bf16[224,128]{1,0:T(8,128)(2,1)S(1)} collective-permute-done((bf16[224,128]{1,0:T(8,128)(2,1)S(1)}, bf16[224,128]{1,0:T(8,128)(2,1)S(1)}, u32[]{:S(2)}, u32[]{:S(2)}) %collective-permute-start.23) | collective-permute-done | bytes 57376 | tf_op jit(solution)/shard_map/ppermute | solution.py:52
  (73 shorter events, 16.8 us)
Async XLA Ops:
  1.7 13.8 %collective-permute-start.4 = (bf16[32,2,192]{2,1,0:T(2,128)(2,1)S(1)}, bf16[32,2,192]{2,1,0:T(2,128)(2,1)S(1)}, u32[]{:S(2)}, u32[]{:S(2)}) collective-permute-start(bf16[32,2,192]{2,1,0:T(2,128)(2,1)S(1)} %slice.68), channel_id=1, source_target_pairs={{0,1},{1,0},{2,3},{3,2},{4,5},{5,4},{6,7},{7,6},{8,9},{9,8},{10,11... | collective-permute-start | bytes 73736 | tf_op jit(solution)/shard_map/ppermute | solution.py:108
  5.6 11.5 %collective-permute-start.5 = (bf16[32,3,192]{2,1,0:T(4,128)(2,1)S(1)}, bf16[32,3,192]{2,1,0:T(4,128)(2,1)S(1)}, u32[]{:S(2)}, u32[]{:S(2)}) collective-permute-start(bf16[32,3,192]{2,1,0:T(4,128)(2,1)S(1)} %slice.69), channel_id=1, source_target_pairs={{0,1},{1,0},{2,3},{3,2},{4,5},{5,4},{6,7},{7,6},{8,9},{9,8},{10,11... | collective-permute-start | bytes 110600 | tf_op jit(solution)/shard_map/ppermute | solution.py:109
  6.5 11.2 %collective-permute-start.9 = (bf16[224,128]{1,0:T(8,128)(2,1)S(1)}, bf16[224,128]{1,0:T(8,128)(2,1)S(1)}, u32[]{:S(2)}, u32[]{:S(2)}) collective-permute-start(bf16[224,128]{1,0:T(8,128)(2,1)S(1)} %get-tuple-element.26), channel_id=1, source_target_pairs={{0,16},{1,17},{2,18},{3,19},{4,20},{5,21},{6,22},{7,23},{8,24},{9,... | collective-permute-start | bytes 172040 | tf_op jit(solution)/shard_map/ppermute | solution.py:52
  9.7 9.3 %collective-permute-start.8 = (bf16[224,128]{1,0:T(8,128)(2,1)S(1)}, bf16[224,128]{1,0:T(8,128)(2,1)S(1)}, u32[]{:S(2)}, u32[]{:S(2)}) collective-permute-start(bf16[224,128]{1,0:T(8,128)(2,1)S(1)} %get-tuple-element.26), channel_id=1, source_target_pairs={{0,8},{1,9},{2,10},{3,11},{4,12},{5,13},{6,14},{7,15},{8,16},{9,17... | collective-permute-start | bytes 172040 | tf_op jit(solution)/shard_map/ppermute | solution.py:52
  11.3 9.1 %collective-permute-start.10 = (bf16[224,128]{1,0:T(8,128)(2,1)S(1)}, bf16[224,128]{1,0:T(8,128)(2,1)S(1)}, u32[]{:S(2)}, u32[]{:S(2)}) collective-permute-start(bf16[224,128]{1,0:T(8,128)(2,1)S(1)} %get-tuple-element.26), channel_id=1, source_target_pairs={{0,24},{1,25},{2,26},{3,27},{4,28},{5,29},{6,30},{7,31},{8,0},{9,1... | collective-permute-start | bytes 172040 | tf_op jit(solution)/shard_map/ppermute | solution.py:52
  15.6 15.8 %collective-permute-start.1 = (bf16[64,10,128]{2,1,0:T(8,128)(2,1)S(1)}, bf16[64,10,128]{2,1,0:T(8,128)(2,1)S(1)}, u32[]{:S(2)}, u32[]{:S(2)}) collective-permute-start(bf16[64,10,128]{2,1,0:T(8,128)(2,1)S(1)} %slice.65), channel_id=1, source_target_pairs={{0,1},{1,0},{2,3},{3,2},{4,5},{5,4},{6,7},{7,6},{8,9},{9,8},{10,11... | collective-permute-start | bytes 491528 | tf_op jit(solution)/shard_map/ppermute | solution.py:109
  17.1 12.8 %collective-permute-start = (bf16[64,9,128]{2,1,0:T(8,128)(2,1)S(1)}, bf16[64,9,128]{2,1,0:T(8,128)(2,1)S(1)}, u32[]{:S(2)}, u32[]{:S(2)}) collective-permute-start(bf16[64,9,128]{2,1,0:T(8,128)(2,1)S(1)} %slice.64), channel_id=1, source_target_pairs={{0,1},{1,0},{2,3},{3,2},{4,5},{5,4},{6,7},{7,6},{8,9},{9,8},{10,11... | collective-permute-start | bytes 442376 | tf_op jit(solution)/shard_map/ppermute | solution.py:108
  17.7 15.2 %collective-permute-start.6 = (bf16[2,37,192]{2,1,0:T(8,128)(2,1)S(1)}, bf16[2,37,192]{2,1,0:T(8,128)(2,1)S(1)}, u32[]{:S(2)}, u32[]{:S(2)}) collective-permute-start(bf16[2,37,192]{2,1,0:T(8,128)(2,1)S(1)} %pad_maximum_fusion.8), channel_id=1, source_target_pairs={{0,2},{2,4},{4,6},{6,8},{8,10},{10,12},{12,14},{14,16},{16,18},{18... | collective-permute-start | bytes 85256 | tf_op jit(solution)/shard_map/ppermute | solution.py:114
  19.0 15.3 %collective-permute-start.7 = (bf16[3,37,192]{2,1,0:T(8,128)(2,1)S(1)}, bf16[3,37,192]{2,1,0:T(8,128)(2,1)S(1)}, u32[]{:S(2)}, u32[]{:S(2)}) collective-permute-start(bf16[3,37,192]{2,1,0:T(8,128)(2,1)S(1)} %pad_maximum_fusion.6), channel_id=1, source_target_pairs={{2,0},{4,2},{6,4},{8,6},{10,8},{12,10},{14,12},{16,14},{18,16},{20... | collective-permute-start | bytes 127880 | tf_op jit(solution)/shard_map/ppermute | solution.py:115
  20.4 15.3 %collective-permute-start.13 = (bf16[4,224,128]{2,1,0:T(8,128)(2,1)S(1)}, bf16[4,224,128]{2,1,0:T(8,128)(2,1)S(1)}, u32[]{:S(2)}, u32[]{:S(2)}) collective-permute-start(bf16[4,224,128]{2,1,0:T(8,128)(2,1)S(1)} %pad_maximum_fusion.2.refs_0_), channel_id=1, source_target_pairs={{0,5},{1,4},{2,7},{3,6},{4,1},{5,0},{6,3},{7,2},{8,13},{9,12},{10,... | collective-permute-start | bytes 688136 | tf_op jit(solution)/shard_map/ppermute | solution.py:52
  29.9 7.7 %collective-permute-start.12 = (bf16[4,224,128]{2,1,0:T(8,128)(2,1)S(1)}, bf16[4,224,128]{2,1,0:T(8,128)(2,1)S(1)}, u32[]{:S(2)}, u32[]{:S(2)}) collective-permute-start(bf16[4,224,128]{2,1,0:T(8,128)(2,1)S(1)} %pad_maximum_fusion.2.refs_0_), channel_id=1, source_target_pairs={{0,4},{1,5},{2,6},{3,7},{4,0},{5,1},{6,2},{7,3},{8,12},{9,13},{10,... | collective-permute-start | bytes 688136 | tf_op jit(solution)/shard_map/ppermute | solution.py:52
  31.3 6.4 %collective-permute-start.11 = (bf16[4,224,128]{2,1,0:T(8,128)(2,1)S(1)}, bf16[4,224,128]{2,1,0:T(8,128)(2,1)S(1)}, u32[]{:S(2)}, u32[]{:S(2)}) collective-permute-start(bf16[4,224,128]{2,1,0:T(8,128)(2,1)S(1)} %pad_maximum_fusion.2.refs_0_), channel_id=1, source_target_pairs={{0,1},{1,0},{2,3},{3,2},{4,5},{5,4},{6,7},{7,6},{8,9},{9,8},{10,11... | collective-permute-start | bytes 688136 | tf_op jit(solution)/shard_map/ppermute | solution.py:52
  32.9 5.3 %collective-permute-start.2 = (bf16[9,83,128]{2,1,0:T(8,128)(2,1)S(1)}, bf16[9,83,128]{2,1,0:T(8,128)(2,1)S(1)}, u32[]{:S(2)}, u32[]{:S(2)}) collective-permute-start(bf16[9,83,128]{2,1,0:T(8,128)(2,1)S(1)} %pad_maximum_fusion.5), channel_id=1, source_target_pairs={{0,2},{2,4},{4,6},{6,8},{8,10},{10,12},{12,14},{14,16},{16,18},{18... | collective-permute-start | bytes 573704 | tf_op jit(solution)/shard_map/ppermute | solution.py:114
  35.7 8.5 %collective-permute-start.14 = (bf16[4,224,128]{2,1,0:T(8,128)(2,1)S(1)}, bf16[4,224,128]{2,1,0:T(8,128)(2,1)S(1)}, u32[]{:S(2)}, u32[]{:S(2)}) collective-permute-start(bf16[4,224,128]{2,1,0:T(8,128)(2,1)S(1)} %pad_maximum_fusion.2.refs_0_), channel_id=1, source_target_pairs={{0,2},{1,3},{2,0},{3,1},{4,6},{5,7},{6,4},{7,5},{8,10},{9,11},{10,... | collective-permute-start | bytes 688136 | tf_op jit(solution)/shard_map/ppermute | solution.py:52
  37.7 6.5 %collective-permute-start.17 = (bf16[4,224,128]{2,1,0:T(8,128)(2,1)S(1)}, bf16[4,224,128]{2,1,0:T(8,128)(2,1)S(1)}, u32[]{:S(2)}, u32[]{:S(2)}) collective-permute-start(bf16[4,224,128]{2,1,0:T(8,128)(2,1)S(1)} %collective-permute-done.13.refs_3_), channel_id=1, source_target_pairs={{0,2},{1,3},{2,0},{3,1},{4,6},{5,7},{6,4},{7,5},{8,10},{9,11},{10,... | collective-permute-start | bytes 688136 | tf_op jit(solution)/shard_map/ppermute | solution.py:52
  37.8 6.5 %collective-permute-start.16 = (bf16[4,224,128]{2,1,0:T(8,128)(2,1)S(1)}, bf16[4,224,128]{2,1,0:T(8,128)(2,1)S(1)}, u32[]{:S(2)}, u32[]{:S(2)}) collective-permute-start(bf16[4,224,128]{2,1,0:T(8,128)(2,1)S(1)} %collective-permute-done.12.refs_2_), channel_id=1, source_target_pairs={{0,2},{1,3},{2,0},{3,1},{4,6},{5,7},{6,4},{7,5},{8,10},{9,11},{10,... | collective-permute-start | bytes 688136 | tf_op jit(solution)/shard_map/ppermute | solution.py:52
  38.2 6.1 %collective-permute-start.15 = (bf16[4,224,128]{2,1,0:T(8,128)(2,1)S(1)}, bf16[4,224,128]{2,1,0:T(8,128)(2,1)S(1)}, u32[]{:S(2)}, u32[]{:S(2)}) collective-permute-start(bf16[4,224,128]{2,1,0:T(8,128)(2,1)S(1)} %collective-permute-done.11.refs_1_), channel_id=1, source_target_pairs={{0,2},{1,3},{2,0},{3,1},{4,6},{5,7},{6,4},{7,5},{8,10},{9,11},{10,... | collective-permute-start | bytes 688136 | tf_op jit(solution)/shard_map/ppermute | solution.py:52
  77.8 6.5 %collective-permute-start.18 = (bf16[4,4,224,128]{3,2,1,0:T(8,128)(2,1)S(1)}, bf16[4,4,224,128]{3,2,1,0:T(8,128)(2,1)S(1)}, u32[]{:S(2)}, u32[]{:S(2)}) collective-permute-start(bf16[4,4,224,128]{3,2,1,0:T(8,128)(2,1)S(1)} %bitcast.39), channel_id=1, source_target_pairs={{0,2},{1,3},{2,0},{3,1},{4,6},{5,7},{6,4},{7,5},{8,10},{9,11},{10,... | collective-permute-start | bytes 2752520 | tf_op jit(solution)/shard_map/ppermute | solution.py:52
  84.5 8.5 %collective-permute-start.19 = (bf16[4,224,128]{2,1,0:T(8,128)(2,1)S(1)}, bf16[4,224,128]{2,1,0:T(8,128)(2,1)S(1)}, u32[]{:S(2)}, u32[]{:S(2)}) collective-permute-start(bf16[4,224,128]{2,1,0:T(8,128)(2,1)S(1)} %get-tuple-element.17), channel_id=1, source_target_pairs={{0,1},{1,0},{2,3},{3,2},{4,5},{5,4},{6,7},{7,6},{8,9},{9,8},{10,11... | collective-permute-start | bytes 688136 | tf_op jit(solution)/shard_map/ppermute | solution.py:52
  85.2 13.3 %collective-permute-start.21 = (bf16[4,224,128]{2,1,0:T(8,128)(2,1)S(1)}, bf16[4,224,128]{2,1,0:T(8,128)(2,1)S(1)}, u32[]{:S(2)}, u32[]{:S(2)}) collective-permute-start(bf16[4,224,128]{2,1,0:T(8,128)(2,1)S(1)} %get-tuple-element.18), channel_id=1, source_target_pairs={{0,5},{1,4},{2,7},{3,6},{4,1},{5,0},{6,3},{7,2},{8,13},{9,12},{10,... | collective-permute-start | bytes 688136 | tf_op jit(solution)/shard_map/ppermute | solution.py:52
  87.6 12.2 %collective-permute-start.20 = (bf16[4,224,128]{2,1,0:T(8,128)(2,1)S(1)}, bf16[4,224,128]{2,1,0:T(8,128)(2,1)S(1)}, u32[]{:S(2)}, u32[]{:S(2)}) collective-permute-start(bf16[4,224,128]{2,1,0:T(8,128)(2,1)S(1)} %get-tuple-element.19), channel_id=1, source_target_pairs={{0,4},{1,5},{2,6},{3,7},{4,0},{5,1},{6,2},{7,3},{8,12},{9,13},{10,... | collective-permute-start | bytes 688136 | tf_op jit(solution)/shard_map/ppermute | solution.py:52
  100.0 6.1 %collective-permute-start.22 = (bf16[224,128]{1,0:T(8,128)(2,1)S(1)}, bf16[224,128]{1,0:T(8,128)(2,1)S(1)}, u32[]{:S(2)}, u32[]{:S(2)}) collective-permute-start(bf16[224,128]{1,0:T(8,128)(2,1)S(1)} %get-tuple-element.20), channel_id=1, source_target_pairs={{0,8},{1,9},{2,10},{3,11},{4,12},{5,13},{6,14},{7,15},{8,16},{9,17... | collective-permute-start | bytes 172040 | tf_op jit(solution)/shard_map/ppermute | solution.py:52
  100.6 5.4 %collective-permute-start.24 = (bf16[224,128]{1,0:T(8,128)(2,1)S(1)}, bf16[224,128]{1,0:T(8,128)(2,1)S(1)}, u32[]{:S(2)}, u32[]{:S(2)}) collective-permute-start(bf16[224,128]{1,0:T(8,128)(2,1)S(1)} %get-tuple-element.21), channel_id=1, source_target_pairs={{0,24},{1,25},{2,26},{3,27},{4,28},{5,29},{6,30},{7,31},{8,0},{9,1... | collective-permute-start | bytes 172040 | tf_op jit(solution)/shard_map/ppermute | solution.py:52
  103.8 5.1 %collective-permute-start.23 = (bf16[224,128]{1,0:T(8,128)(2,1)S(1)}, bf16[224,128]{1,0:T(8,128)(2,1)S(1)}, u32[]{:S(2)}, u32[]{:S(2)}) collective-permute-start(bf16[224,128]{1,0:T(8,128)(2,1)S(1)} %get-tuple-element.22), channel_id=1, source_target_pairs={{0,16},{1,17},{2,18},{3,19},{4,20},{5,21},{6,22},{7,23},{8,24},{9,... | collective-permute-start | bytes 172040 | tf_op jit(solution)/shard_map/ppermute | solution.py:52
  (13 other events, 84.6 us)
where the time goes:
time: 111 us; the launch traced here: 110 us
  starting transfers between devices  40.1 us (36%)
  Pallas kernels  33.1 us (30%)
  waiting for transfers between devices  23.1 us (21%)
  local copies, waits for them, and re-layouts  10.5 us (9%)
  other arithmetic  2.41 us (2%)
    pallas_call x1, Pallas kernels, local(): pl.pallas_call(functools.partial(level, shape, devices, parts), out_shape...  31 us
    ppermute x17, starting transfers between devices, send(): return lax.ppermute(value, BOTH, pairs)  29.7 us
    ppermute x17, waiting for transfers between devices, send(): return lax.ppermute(value, BOTH, pairs)  19 us
    ppermute x2, waiting for transfers between devices, widened(): before = lax.ppermute(block[:, -low:], 'lon', east)  4.05 us
    unnamed x24, local copies, waits for them, and re-layouts  3.63 us
    ppermute x2, starting transfers between devices, widened(): before = lax.ppermute(block[:, -low:], 'lon', east)  3.54 us
    ppermute x2, starting transfers between devices, widened(): before = lax.ppermute(block[-low:], 'lat', south)  2.59 us
    ppermute x2, starting transfers between devices, widened(): after = lax.ppermute(block[:high], 'lat', north)  2.58 us
  transfers between devices with their start and end apart: 25, of which 8 were waited for; matrix products, arithmetic and copies ran while one was open for 4% of the time, Pallas kernels for 2%

commit v1 on v0

v1 whole, which is shorter than its diff:
```python
import functools

import jax
import jax.numpy as jnp
from jax import lax
from jax.experimental import pallas as pl
from jax.experimental.pallas import tpu as pltpu
from jax.sharding import PartitionSpec as P

LOSS_CELLS = 1024
LAT = ("chip", "core")
BOTH = ("chip", "core", "lon")
F32 = jnp.float32
BF16 = jnp.bfloat16


class Slice:
    def __init__(self):
        chip, core, lon = (lax.axis_size(axis) for axis in BOTH)
        near = 2 if chip % 2 == 0 else 1
        self.sizes = (chip // near, near, core, lon)
        self.count = chip * core * lon

    def place(self):
        lat = lax.axis_index("chip") * self.sizes[2] + lax.axis_index("core")
        return lat, self.coords(lat * self.sizes[3] + lax.axis_index("lon"))

    def coords(self, index):
        out = []
        for size in reversed(self.sizes):
            if isinstance(index, int):
                out.append(index % size)
                index = index // size
            else:
                out.append(lax.rem(index, size))
                index = lax.div(index, size)
        return tuple(reversed(out))

    def index(self, coords):
        total = 0
        for at, size in zip(coords, self.sizes):
            total = total * size + at
        return total

    def moved(self, coords, steps, sign=1):
        out = []
        for at, by, size in zip(coords, steps, self.sizes):
            to = at + sign * by + size
            out.append(to % size if isinstance(to, int) else lax.rem(to, size))
        return tuple(out)

    def send(self, value, steps):
        pairs = []
        for source in range(self.count):
            pairs.append((source, self.index(self.moved(self.coords(source), steps))))
        return lax.ppermute(value, BOTH, pairs)


def gathered(devices, shard):
    far, near, core, lon = devices.sizes
    line = jnp.stack([shard] + [devices.send(shard, (f, 0, 0, 0)) for f in range(1, far)])
    planes, parts = [], []
    for c in range(core):
        for n in range(near):
            for o in range(lon):
                if c:
                    plane = devices.send(planes[n * lon + o], (0, 0, c, 0))
                else:
                    plane = line if n == o == 0 else devices.send(line, (0, n, 0, o))
                planes.append(plane)
                parts.append((c, n, o))
    return planes, parts


def halved(devices, chunks):
    half = chunks[0].astype(F32)
    for c in range(1, chunks.shape[0]):
        half = half + devices.send(chunks[c], (0, 0, c, 0)).astype(F32)
    return half.astype(BF16)


def summed(half, size):
    half = lax.all_to_all(half, ("chip", "lon"), 0, 0, tiled=True)
    return jnp.sum(half.astype(F32), axis=0).reshape(-1)[:size]


def order(devices, sign):
    far, near, core, lon = devices.sizes
    mine = devices.place()[1]
    places = []
    for c in range(core):
        for n in range(near):
            for o in range(lon):
                for f in range(far):
                    places.append(devices.index(devices.moved(mine, (f, n, c, o), sign)))
    return jnp.stack(places)


def owners(devices):
    far, near, core, lon = devices.sizes
    at = devices.place()[1][2]
    places = []
    for c in range(core):
        for f in range(far):
            for n in range(near):
                for o in range(lon):
                    places.append(devices.index((f, n, lax.rem(at + c, core), o)))
    return jnp.stack(places)


def passed(devices, half):
    far, near, core, lon = devices.sizes

    def add(terms):
        total = terms[0].astype(F32)
        for term in terms[1:]:
            total = total + term.astype(F32)
        return total

    half = half.reshape(near * lon, far, *half.shape[1:])
    terms = []
    for n in range(near):
        for o in range(lon):
            part = half[n * lon + o]
            terms.append(part if n == o == 0 else devices.send(part, (0, n, 0, o)))
    line = add(terms).astype(BF16)
    return add([line[0]] + [devices.send(line[f], (f, 0, 0, 0)) for f in range(1, far)])


WEST, EAST = 9, 10
BEFORE, AFTER = 2, 3
CORNER = 16


def strips(rows, cols):
    side, at = [], 0
    for inputs, cots in ((WEST, BEFORE), (EAST, AFTER)):
        columns = [at + 2 * rows * j for j in range(inputs)]
        at += 2 * rows * inputs
        parts = [[at + rows * (cots * part + j) for j in range(cots)] for part in range(2)]
        at += 2 * rows * cots
        side.append((columns, parts))
    return side, at


def edges(rows, cols, inputs, cots):
    places = [0, 2 * cols * inputs]
    places.append(places[-1] + CORNER * (WEST + EAST))
    places.append(places[-1] + 2 * cots * cols)
    places.append(places[-1] + 2 * CORNER * (BEFORE + AFTER))
    return places


def halves(value):
    return value[..., :128], jnp.concatenate([value[..., 128:], value[..., 128:]], axis=-1)


def pack_sides(rows, cols, x_ref, c_ref, side_ref, parts_ref, strip):
    west, east = strips(rows, cols)[0]

    def columns(value, wanted, places):
        high = value.shape[0]
        strip[: high * CORNER, :] = value.astype(F32).reshape(high * CORNER, 128)
        for j, place in zip(wanted, places):
            side_ref[place : place + high, :] = strip[pl.ds(j, high, stride=CORNER), :].astype(BF16)

    columns(x_ref[:, 2 * cols - CORNER :, :], range(CORNER - WEST, CORNER), west[0])
    columns(x_ref[:, :CORNER, :], range(EAST), east[0])
    parts = halves(c_ref[...])
    for part in range(2):
        parts_ref[part] = parts[part]
        columns(parts[part][:, cols - CORNER :], range(CORNER - BEFORE, CORNER), west[1][part])
        columns(parts[part][:, :CORNER], range(AFTER), east[1][part])


def pack_edges(rows, cols, x_ref, parts_ref, side_ref, south_ref, north_ref):
    side = strips(rows, cols)[0]
    for ref, inputs, cots, last in (
        (south_ref, WEST, BEFORE, True),
        (north_ref, EAST, AFTER, False),
    ):
        at = edges(rows, cols, inputs, cots)
        first = 2 * rows - inputs if last else 0
        for i in range(inputs):
            ref[at[0] + 2 * cols * i : at[0] + 2 * cols * (i + 1), :] = x_ref[first + i]
        first = 2 * rows - CORNER if last else 0
        to = at[1]
        for columns, _ in side:
            for place in columns:
                ref[to : to + CORNER, :] = side_ref[place + first : place + first + CORNER, :]
                to += CORNER
        first = rows - cots if last else 0
        to = at[2]
        for part in range(2):
            for i in range(cots):
                ref[to : to + cols, :] = parts_ref[part, first + i]
                to += cols
        first = rows - CORNER if last else 0
        for part in range(2):
            for _, parts in side:
                for place in parts[part]:
                    ref[to : to + CORNER, :] = side_ref[place + first : place + first + CORNER, :]
                    to += CORNER


def sideways(rows, cols, packed):
    count = lax.axis_size("lon")
    east = [(i, (i + 1) % count) for i in range(count)]
    west = [(i, (i - 1) % count) for i in range(count)]
    if count == 2:
        return lax.ppermute(packed, "lon", east)
    cut = strips(rows, cols)[0][1][0][0]
    before = lax.ppermute(packed[:cut], "lon", east)
    after = lax.ppermute(packed[cut:], "lon", west)
    return jnp.concatenate([before, after], axis=0)


def lengthways(south, north):
    count = lax.axis_size("chip") * lax.axis_size("core")
    down = [(i, i + 1) for i in range(count - 1)]
    up = [(i + 1, i) for i in range(count - 1)]
    return lax.ppermute(south, LAT, down), lax.ppermute(north, LAT, up)


LEFT = 16
ABOVE = 5
BELOW = 7
GUARD = 8
HALF = 64

FRINGE = (((0, 0, 0),), ((0, 1, 0),), ((0, 2, 0),), ((0, 0, 1), (0, 1, 1)), ((0, 2, 1), (1, 2, 1)))
MIDDLE = (((1, 0, 0),), ((1, 1, 0),), ((1, 2, 0),), ((1, 0, 1), (1, 1, 1)))
LAST = (((2, 0, 0),), ((2, 1, 0),), ((2, 2, 0),), ((2, 0, 1), (2, 1, 1)), ((2, 2, 1), None))
BLOCKS = FRINGE + MIDDLE + LAST


def low_lanes(rows):
    return lax.broadcasted_iota(jnp.int32, (rows, 128), 1) < HALF


def swapped(value):
    return pltpu.roll(value, HALF, 1)


def prepare(
    rows, cols, x_ref, parts_ref, side_ref, south_ref, north_ref, windows_ref, cot_ref, wide, cots
):
    pitch = cols + LEFT
    height = rows + ABOVE + BELOW
    size = height * pitch
    span = 2 * cols + 48
    base_row, base_col = 20, 24
    wide[...] = jnp.zeros_like(wide)
    cots[...] = jnp.zeros_like(cots)
    side = strips(rows, cols)[0]
    columns = [*range(-WEST, 0), *range(2 * cols, 2 * cols + EAST)]

    def at(i, j):
        return (i + base_row) * span + base_col + j

    def own(i, _):
        wide[pl.ds(pl.multiple_of(at(i, 0), 8), 2 * cols), :] = x_ref[i].astype(F32)
        return 0

    lax.fori_loop(0, 2 * rows, own, 0)
    for j, place in zip(columns, side[0][0] + side[1][0]):
        strip = side_ref[place : place + 2 * rows, :].astype(F32)
        wide[pl.ds(at(0, j), 2 * rows, stride=span), :] = strip
    for ref, inputs, cotangents, top, above in (
        (south_ref, WEST, BEFORE, -WEST, True),
        (north_ref, EAST, AFTER, 2 * rows, False),
    ):
        places = edges(rows, cols, inputs, cotangents)
        for i in range(inputs):
            edge = ref[2 * cols * i : 2 * cols * (i + 1), :].astype(F32)
            wide[at(top + i, 0) : at(top + i, 0) + 2 * cols, :] = edge
        first = -CORNER if above else 2 * rows
        for k, j in enumerate(columns):
            place = places[1] + CORNER * k
            corner = ref[place : place + CORNER, :].astype(F32)
            wide[pl.ds(at(first, j), CORNER, stride=span), :] = corner

    def window(k, _):
        for parity in range(2):
            row = 2 * (k - ABOVE) + parity + base_row
            for tap in range(3):
                base = row * span + base_col - 1 + tap
                mid = wide[pl.ds(base, cols, stride=2), :]
                before = wide[pl.ds(base - 16, 8, stride=2), :]
                after = wide[pl.ds(base - 2 * span + 2 * cols, 8, stride=2), :]
                lane = (3 * parity + tap) * 128
                cells = jnp.concatenate([after, before, mid], axis=0).astype(BF16)
                windows_ref[pl.ds(pl.multiple_of(k * pitch, 16), pitch), lane : lane + 128] = cells
        return 0

    lax.fori_loop(0, height, window, 0)

    def cell(i, j):
        return GUARD + (i + ABOVE) * pitch + LEFT + j

    columns = [*range(-BEFORE, 0), *range(cols, cols + AFTER)]
    for part in range(2):
        for i in range(rows):
            cots[cell(i, 0) : cell(i, cols), :] = parts_ref[part, i].astype(F32)
        for j, place in zip(columns, side[0][1][part] + side[1][1][part]):
            strip = side_ref[place : place + rows, :].astype(F32)
            cots[pl.ds(cell(0, j), rows, stride=pitch), :] = strip
        for ref, inputs, cotangents, above in (
            (south_ref, WEST, BEFORE, True),
            (north_ref, EAST, AFTER, False),
        ):
            places = edges(rows, cols, inputs, cotangents)
            for i in range(cotangents):
                place = places[2] + cols * (cotangents * part + i)
                to = cell(i - cotangents if above else rows + i, 0)
                cots[to : to + cols, :] = ref[place : place + cols, :].astype(F32)
            for k, j in enumerate(columns):
                place = places[3] + CORNER * (len(columns) * part + k)
                corner = ref[place : place + CORNER, :].astype(F32)
                if above:
                    corner = corner[CORNER - 8 :]
                else:
                    corner = corner[:8]
                for i in range(cotangents):
                    to = cell(i - cotangents if above else rows + i, j)
                    line = 8 - cotangents + i if above else i
                    cots[to : to + 1, :] = corner[line : line + 1]
        cot_ref[:, 128 * part : 128 * part + 128] = cots[GUARD : GUARD + size, :].astype(BF16)


def level(shape, devices, parts, second, names, *refs):
    rows, cols, chan_in, mid, factor, whole = shape
    refs = dict(zip(names, refs))
    x_ref, terms_ref = refs["x"], refs["terms"]
    flat, k_a, k_b, f_a, f_b = (refs[name] for name in ("flat", "k_a", "k_b", "f_a", "f_b"))
    win_delta, t_one, t_two = (refs[name] for name in ("win_delta", "t_one", "t_two"))
    pitch = cols + LEFT
    height = rows + ABOVE + BELOW
    size = height * pitch
    far, near, core, lon = devices.sizes
    count = 1 if whole else devices.count
    share = [9 * c * mid // 128 // count for c in (chan_in, mid, mid)]
    begin = [0, share[0], share[0] + share[1]]
    lat_at, mine = devices.place()
    f_a[...] = jnp.zeros_like(f_a)
    f_b[...] = jnp.zeros_like(f_b)

    def unpack(which, channels):
        n = share[which]
        for i, (c, m, o) in enumerate(parts):
            plane = refs["plane", i]
            for f in range(plane.shape[0]):
                owner = 0 if whole else devices.index(devices.moved(mine, (f, m, c, o), -1))
                lo = begin[which] // 16 * 16
                hi = -(-(begin[which] + n) // 16) * 16
                value = plane[f, lo:hi, :].astype(F32)
                flat[pl.ds(owner * n, n), :] = value[begin[which] - lo : begin[which] - lo + n]
        pairs = 9 * channels // 2
        step = 96

        def one(i, _):
            at = i * step
            first = flat[pl.ds(3 * at, step, stride=3), :]
            second = flat[pl.ds(3 * at + 1, step, stride=3), :]
            third = flat[pl.ds(3 * at + 2, step, stride=3), :]
            low = low_lanes(step)
            second_r, third_r = swapped(second), swapped(third)
            k_a[pl.ds(2 * at, step, stride=2), :] = first
            k_b[pl.ds(2 * at, step, stride=2), :] = jnp.where(low, second, second_r)
            k_a[pl.ds(2 * at + 1, step, stride=2), :] = jnp.where(low, second_r, third_r)
            k_b[pl.ds(2 * at + 1, step, stride=2), :] = jnp.where(low, third_r, third)
            return 0

        lax.fori_loop(0, pairs // step, one, 0)

    def tap_rows(tap, part):
        start = (3 * tap[0] + tap[1]) * mid + 128 * part
        return start, start + (HALF if part else 128)

    def forward(target):
        at = 0
        for block in BLOCKS:
            for tap in block:
                if tap is None:
                    target[at : at + HALF, :] = jnp.zeros((HALF, 256), BF16)
                    at += HALF
                    continue
                lo, hi = tap_rows(tap, tap[2])
                target[at : at + hi - lo, 0:128] = k_a[lo:hi, :].astype(BF16)
                target[at : at + hi - lo, 128:256] = k_b[lo:hi, :].astype(BF16)
                at += hi - lo

    def backward(target):
        low = low_lanes(mid)
        for i, block in enumerate(BLOCKS):
            values = []
            for tap in block:
                if tap is None:
                    values.append(jnp.zeros((mid, 128), F32))
                    continue
                lo = (3 * (2 - tap[0]) + 2 - tap[1]) * mid
                source = k_b if tap[2] else k_a
                values.append(source[lo : lo + mid, :])
            value = values[0] if len(values) == 1 else jnp.where(low, values[0], values[1])
            value = value.astype(BF16)
            target[0:mid, 128 * i : 128 * i + 128] = value
            target[mid:256, 128 * i : 128 * i + 128] = value[128:mid]

    def load_kernels():
        unpack(0, chan_in)
        refs["w_one"][:, 0:128] = k_a[0 : 9 * chan_in, :].astype(BF16)
        refs["w_one"][:, 128:256] = k_b[0 : 9 * chan_in, :].astype(BF16)
        empty = jnp.zeros((chan_in, 128), F32)
        low_in = low_lanes(chan_in)
        phases = (
            ((1, 1), None, None, None),
            ((1, 2), (1, 0), None, None),
            ((2, 1), None, (0, 1), None),
            ((2, 2), (2, 0), (0, 2), (0, 0)),
        )
        for i, taps in enumerate(phases):
            a, b = [], []
            for tap in taps:
                if tap is None:
                    a.append(empty)
                    b.append(empty)
                else:
                    lo = (3 * tap[0] + tap[1]) * chan_in
                    a.append(k_a[lo : lo + chan_in, :])
                    b.append(k_b[lo : lo + chan_in, :])
            blocks = (
                a[0],
                a[1],
                jnp.where(low_in, b[0], b[1]),
                a[2],
                a[3],
                jnp.where(low_in, b[2], b[3]),
            )
            for j, block in enumerate(blocks):
                t_one[chan_in * i : chan_in * (i + 1), 128 * j : 128 * j + 128] = block.astype(BF16)
        unpack(1, mid)
        forward(refs["w_two"])
        backward(t_two)
        unpack(2, mid)
        forward(refs["w_three"])
        backward(refs["t_three"])

    first_row = lat_at * rows
    bottom = lax.axis_size("chip") * core * rows - first_row
    low_cell = (jnp.maximum(-first_row, -ABOVE) + ABOVE) * pitch + 8
    high_cell = (jnp.minimum(bottom, rows + BELOW) + ABOVE) * pitch + 8

    def inside(start, n):
        cell = start + lax.broadcasted_iota(jnp.int32, (n, 128), 0)
        return (cell >= low_cell) & (cell < high_cell)

    def store(start, n, left, right, mask):
        if mask:
            keep = inside(start, n)
            left = jnp.where(keep, left, 0.0)
            right = jnp.where(keep, right, 0.0)
        at = pl.multiple_of(start + GUARD, 8)
        f_a[pl.ds(at, n), :] = left
        f_b[pl.ds(at, n), :] = right

    def windows(target, top, under):
        def one(i, _):
            cell = i * pitch
            q = cell + GUARD
            low = low_lanes(pitch)
            b_0, b_1, b_2 = (f_b[pl.ds(q + s, pitch), :] for s in (-1, 0, 1))
            b_3 = f_b[pl.ds(q + 1 + pitch, pitch), :]
            out = [f_a[pl.ds(q + s, pitch), :] for s in (-1, 0, 1)]
            out += [jnp.where(low, b_0, b_1), jnp.where(low, b_2, b_3)]
            at = pl.multiple_of(cell, 16)
            for j, value in enumerate(out):
                target[pl.ds(at, pitch), 128 * j : 128 * j + 128] = value.astype(BF16)
            return 0

        lax.fori_loop(top + ABOVE, under + ABOVE, one, 0)

    def convolve(source, weights, turned, halo, steps, finish):
        start = (ABOVE - halo) * pitch
        total = (rows + 1 + 2 * halo) * pitch + LEFT
        n = -(-total // steps // 16) * 16
        contract = (((1,), (1,)), ((), ())) if turned else (((1,), (0,)), ((), ()))

        def one(i, _):
            p = pl.multiple_of(start + i * n, 16)
            above = source[pl.ds(pl.multiple_of(p - pitch, 16), n), :]
            here = source[pl.ds(p, n), 0:512]
            below = source[pl.ds(pl.multiple_of(p + pitch, 16), n), :]
            value = lax.dot_general(
                jnp.concatenate([above, here, below], axis=1),
                weights[...],
                contract,
                preferred_element_type=F32,
            )
            finish(p, n, value)
            return 0

        lax.fori_loop(0, steps, one, 0)

    def own(ref, lanes, row_step=0, shift=0, offset=0):
        pieces = []
        for r in range(rows):
            at = offset + (ABOVE + r + row_step) * pitch + LEFT + shift
            pieces.append(ref[at : at + cols, lanes])
        return jnp.concatenate(pieces, axis=0)

    ALL = slice(0, 128)

    def turned_deltas():
        left = own(f_a, ALL, offset=GUARD)
        right = own(f_b, ALL, offset=GUARD)
        return jnp.concatenate([left.T, right.T], axis=0).astype(BF16)

    def pack(which, channels, first=0):
        step = 96

        def one(i, _):
            at = i * step
            even_a = k_a[pl.ds(2 * at, step, stride=2), :]
            even_b = k_b[pl.ds(2 * at, step, stride=2), :]
            odd_a = swapped(k_a[pl.ds(2 * at + 1, step, stride=2), :])
            odd_b = k_b[pl.ds(2 * at + 1, step, stride=2), :]
            low = low_lanes(step)
            flat[pl.ds(3 * at, step, stride=3), :] = even_a
            flat[pl.ds(3 * at + 1, step, stride=3), :] = jnp.where(low, even_b, odd_a)
            flat[pl.ds(3 * at + 2, step, stride=3), :] = jnp.where(low, odd_a, odd_b)
            return 0

        lax.fori_loop(0, 9 * channels // 2 // step, one, 0)
        n = share[which]
        for k in range(count):
            refs["chunk"][k, first : first + n, :] = flat[k * n : (k + 1) * n, :]

    def hand_over():
        for k in range(count):
            f, m, c, o = devices.coords(k)
            place, side = 0, 0
            if not whole:
                side = lax.rem(c - mine[2] + core, core)
                place = (f * near + m) * lon + o
                if not second:
                    away = zip(devices.coords(k), mine, devices.sizes)
                    f, m, c, o = (lax.rem(to - at + by, by) for to, at, by in away)
                    place = (m * lon + o) * far + f
            terms_ref[side, place] = refs["chunk"][k].astype(BF16)

    def field_grad(which, source, first):
        turned = turned_deltas()
        for a, blocks in enumerate((FRINGE, MIDDLE, LAST)):
            lanes = slice(0, 128 * len(blocks))
            product = lax.dot_general(
                turned,
                own(source, lanes, a - 1),
                (((1,), (0,)), ((), ())),
                preferred_element_type=F32,
            )
            product = product * factor
            for j, block in enumerate(blocks):
                left = product[0:128, 128 * j : 128 * j + 128].T
                right = product[128:256, 128 * j : 128 * j + 128].T
                at = 0
                for tap in block:
                    if tap is None:
                        continue
                    lo, hi = tap_rows(tap, tap[2])
                    k_a[lo:hi, :] = left[at : at + hi - lo]
                    k_b[lo:hi, :] = right[at : at + hi - lo]
                    at += hi - lo
        pack(which, mid, first)

    def forward_pass():
        load_kernels()
        win_one, win_two, slope, spread, c_ref = (
            refs[name] for name in ("win_one", "win_two", "slope", "spread", "c")
        )
        slope[...] = jnp.zeros_like(slope)

        def convolve_first():
            halo, steps = 4, 4
            start = (ABOVE - halo) * pitch
            total = (rows + 1 + 2 * halo) * pitch + LEFT
            n = -(-total // steps // 16) * 16

            def one(i, _):
                p = pl.multiple_of(start + i * n, 16)
                above = x_ref[pl.ds(pl.multiple_of(p - pitch, 16), n), 384:768]
                here = x_ref[pl.ds(p, n), :]
                value = lax.dot_general(
                    jnp.concatenate([above, here], axis=1),
                    refs["w_one"][...],
                    (((1,), (0,)), ((), ())),
                    preferred_element_type=F32,
                )
                store(p, n, value[:, :128], value[:, 128:], True)
                return 0

            lax.fori_loop(0, steps, one, 0)

        convolve_first()
        windows(win_one, -4, rows + 6)

        def finish_two(p, n, value):
            s = jax.nn.sigmoid(value)
            active = value * s
            slope[pl.ds(p, n), :] = s + active * (1.0 - s)
            store(p, n, active[:, :128], active[:, 128:], True)

        convolve(win_one, refs["w_two"], False, 3, 4, finish_two)
        windows(win_two, -3, rows + 5)

        def finish_three(p, n, value):
            s = jax.nn.sigmoid(value)
            active = value * s
            delta = c_ref[pl.ds(p, n), :].astype(F32) * (s + active * (1.0 - s))
            store(p, n, delta[:, :128], delta[:, 128:], False)
            spread[pl.ds(p, n), :] = active

        convolve(win_two, refs["w_three"], False, 2, 4, finish_three)
        for r in range(rows):
            at = (ABOVE + r) * pitch + LEFT
            refs["features"][r] = spread[at : at + cols, 0:mid].astype(BF16)
        field_grad(2, win_two, share[1])
        windows(win_delta, -2, rows + 4)

        def finish_delta(p, n, value):
            value = value * slope[pl.ds(p, n), :]
            store(p, n, value[:, :128], value[:, 128:], True)

        convolve(win_delta, refs["t_three"], True, 1, 4, finish_delta)
        field_grad(1, win_one, 0)
        hand_over()
        windows(win_delta, -1, rows + 3)

    def backward_pass():
        def finish_back(p, n, value):
            store(p, n, value[:, :128], value[:, 128:], True)

        convolve(win_delta, t_two, True, 0, 4, finish_back)
        turned = turned_deltas()
        for a, (step, lanes) in enumerate(((-1, slice(384, 768)), (0, slice(0, 384)), (0, slice(384, 768)))):
            product = lax.dot_general(
                turned,
                own(x_ref, lanes, step),
                (((1,), (0,)), ((), ())),
                preferred_element_type=F32,
            )
            product = product * factor
            lo = 3 * a * chan_in
            k_a[lo : lo + 3 * chan_in, :] = product[0:128].T
            k_b[lo : lo + 3 * chan_in, :] = product[128:256].T
        pack(0, chan_in)
        hand_over()

        low = low_lanes(rows * cols)

        def four(ref):
            return [own(ref, ALL, r, c, GUARD) for r, c in ((0, 0), (0, 1), (1, 0), (1, 1))]

        a, b = four(f_a), four(f_b)
        around = (a[0], a[1], jnp.where(low, b[0], b[1]), a[2], a[3], jnp.where(low, b[2], b[3]))
        around = jnp.concatenate([value.astype(BF16) for value in around], axis=1)
        for r in range(2):
            wide = 384 * (r + 1)
            product = lax.dot_general(
                around[:, :wide],
                t_one[2 * chan_in * r : 2 * chan_in * (r + 1), :wide],
                (((1,), (1,)), ((), ())),
                preferred_element_type=F32,
            )
            for i in range(rows):
                at = i * cols
                base = (2 * i + r) * 2 * cols
                for c in range(2):
                    spread_in = product[at : at + cols, chan_in * c : chan_in * (c + 1)]
                    refs["image"][pl.ds(base + c, cols, stride=2), :] = spread_in
        for i in range(2 * rows):
            refs["grad_input"][i] = refs["image"][2 * cols * i : 2 * cols * (i + 1), :].astype(BF16)

    if second:
        backward_pass()
    else:
        forward_pass()


VMEM = pl.BlockSpec(memory_space=pltpu.VMEM)
ANY = pl.BlockSpec(memory_space=pl.ANY)


def local(inputs, w_first, w_second, w_third, cotangent):
    devices = Slice()
    rows, cols, mid = cotangent.shape
    chan_in = inputs.shape[2]
    factor = 1.0 / LOSS_CELLS
    far, near, core, lon = devices.sizes
    held = (w_first.shape[0], w_second.shape[0], w_third.shape[0])
    shard = jnp.concatenate([w_first, w_second, w_third]).reshape(-1, 128)
    whole = any(n % 128 for n in held)
    if not whole:
        shard = jnp.pad(shard, ((0, -shard.shape[0] % 16), (0, 0)))
    planes, parts = gathered(devices, shard)
    if whole:
        chunks = jnp.stack(planes).reshape(devices.count, -1)
        chunks = jnp.take(chunks, jnp.argsort(order(devices, -1)), axis=0)
        pieces = jnp.split(chunks, (held[0], held[0] + held[1]), axis=1)
        chunks = jnp.concatenate([piece.reshape(-1) for piece in pieces])
        planes, parts = [chunks.reshape(1, -1, 128)], [(0, 0, 0)]
    count = 1 if whole else devices.count
    depth = planes[0].shape[1]

    packed_rows = strips(rows, cols)[1]
    packed, split_cot = pl.pallas_call(
        functools.partial(pack_sides, rows, cols),
        out_shape=(
            jax.ShapeDtypeStruct((packed_rows, 128), BF16),
            jax.ShapeDtypeStruct((2, rows, cols, 128), BF16),
        ),
        in_specs=[VMEM] * 2,
        out_specs=(VMEM, VMEM),
        scratch_shapes=[pltpu.VMEM((2 * rows * CORNER, 128), F32)],
        compiler_params=pltpu.CompilerParams(vmem_limit_bytes=16 * 2**20),
        cost_estimate=pl.CostEstimate(flops=0, bytes_accessed=3 * 2**20, transcendentals=0),
    )(inputs, cotangent)
    side = sideways(rows, cols, packed)
    south, north = pl.pallas_call(
        functools.partial(pack_edges, rows, cols),
        out_shape=(
            jax.ShapeDtypeStruct((edges(rows, cols, WEST, BEFORE)[-1], 128), BF16),
            jax.ShapeDtypeStruct((edges(rows, cols, EAST, AFTER)[-1], 128), BF16),
        ),
        in_specs=[VMEM] * 3,
        out_specs=(VMEM, VMEM),
        compiler_params=pltpu.CompilerParams(vmem_limit_bytes=16 * 2**20),
        cost_estimate=pl.CostEstimate(flops=0, bytes_accessed=3 * 2**20, transcendentals=0),
    )(inputs, split_cot, side)
    south, north = lengthways(south, north)
    size = (rows + ABOVE + BELOW) * (cols + LEFT)
    padded, cot = pl.pallas_call(
        functools.partial(prepare, rows, cols),
        out_shape=(
            jax.ShapeDtypeStruct((size, 6 * chan_in), BF16),
            jax.ShapeDtypeStruct((size, 256), BF16),
        ),
        in_specs=[VMEM] * 5,
        out_specs=(VMEM, VMEM),
        scratch_shapes=[
            pltpu.VMEM(((2 * rows + 40) * (2 * cols + 48), 128), F32),
            pltpu.VMEM((size + 2 * GUARD, 128), F32),
        ],
        compiler_params=pltpu.CompilerParams(vmem_limit_bytes=40 * 2**20),
        cost_estimate=pl.CostEstimate(flops=0, bytes_accessed=12 * 2**20, transcendentals=0),
    )(inputs, split_cot, side, south, north)

    deep = -(-(2 * held[1]) // 2048) * 16, -(-held[0] // 2048) * 16
    if whole:
        deep = 2 * held[1] * devices.count // 128, held[0] * devices.count // 128
    sides = 1 if whole else core
    field_shape = (size + 2 * GUARD, 128)
    shape = (rows, cols, chan_in, mid, factor, whole)
    wide = 128 * len(BLOCKS)
    shared = {
        "flat": ((9 * mid * mid // 128, 128), F32),
        "k_a": ((9 * mid, 128), F32),
        "k_b": ((9 * mid, 128), F32),
        "f_a": (field_shape, F32),
        "f_b": (field_shape, F32),
    }

    def call(second, ins, outs, scratch):
        scratch = {**scratch, **shared}
        names = list(ins) + list(outs) + list(scratch)
        results = pl.pallas_call(
            functools.partial(level, shape, devices, () if second else parts, second, names),
            out_shape=[jax.ShapeDtypeStruct(*out) for out in outs.values()],
            in_specs=[VMEM] * len(ins),
            out_specs=[VMEM] * len(outs),
            scratch_shapes=[pltpu.VMEM(*kind) for kind in scratch.values()],
            compiler_params=pltpu.CompilerParams(vmem_limit_bytes=40 * 2**20),
            cost_estimate=pl.CostEstimate(
                flops=2 * 10**9 if second else 5 * 10**9,
                bytes_accessed=12 * 2**20,
                transcendentals=10**6,
            ),
        )(*ins.values())
        return dict(zip(outs, results))

    ins = {"x": padded, "c": cot}
    for i, plane in enumerate(planes):
        ins["plane", i] = plane
    done = call(
        False,
        ins,
        {
            "features": ((rows, cols, mid), BF16),
            "terms": ((sides, count // sides, deep[0], 128), BF16),
            "win_delta": ((size, 640), BF16),
            "t_one": ((4 * chan_in, 768), BF16),
            "t_two": ((256, wide), BF16),
        },
        {
            "chunk": ((count, deep[0], 128), F32),
            "w_one": ((9 * chan_in, 256), BF16),
            "w_two": ((wide, 256), BF16),
            "w_three": ((wide, 256), BF16),
            "t_three": ((256, wide), BF16),
            "slope": ((size, 256), F32),
            "spread": ((size, 256), F32),
            "win_one": ((size, 640), BF16),
            "win_two": ((size, 640), BF16),
        },
    )
    features = done["features"]

    def reduced(terms, places, *sizes):
        if whole:
            cuts = [sum(sizes[:i]) * devices.count for i in range(1, len(sizes))]
            pieces = jnp.split(terms.reshape(-1), cuts)
            terms = [piece.reshape(devices.count, -1) for piece in pieces]
            terms = jnp.take(jnp.concatenate(terms, axis=1), places, axis=0)
            terms = terms.reshape(core, devices.count // core, 1, -1)
        return halved(devices, terms)

    upper = reduced(done["terms"], order(devices, 1), held[1], held[2])
    upper, win_delta = lax.optimization_barrier((upper, done["win_delta"]))
    done["win_delta"] = win_delta
    upper = passed(devices, upper).reshape(-1)
    grad_second, grad_third = upper[: held[1]], upper[held[1] : held[1] + held[2]]
    done = call(
        True,
        {"x": padded, **{name: done[name] for name in ("win_delta", "t_one", "t_two")}},
        {
            "grad_input": ((2 * rows, 2 * cols, chan_in), BF16),
            "terms": ((sides, count // sides, deep[1], 128), BF16),
        },
        {
            "chunk": ((count, deep[1], 128), F32),
            "image": ((4 * rows * cols, 128), F32),
        },
    )
    lower = reduced(done["terms"], owners(devices), held[0])
    grad_first = summed(lower, held[0])
    return (features, done["grad_input"], grad_first, grad_second, grad_third)


def solution(mesh):
    lat, lon = mesh.shape["lat"], mesh.shape["lon"]
    core = 2 if lat % 2 == 0 else 1
    chips = jax.sharding.Mesh(mesh.devices.reshape(lat // core, core, lon), BOTH)
    tile = P(LAT, "lon", None)
    flat = P(BOTH)
    return jax.shard_map(
        local,
        mesh=chips,
        in_specs=(tile, flat, flat, flat, tile),
        out_specs=(tile, tile, flat, flat, flat),
        check_vma=False,
    )
```

time: 111 us -> 95.7 us (0.86)
  local copies, waits for them, and re-layouts: 10.5 us -> 3.66 us
  starting transfers between devices: 40.1 us -> 33.3 us
  waiting for transfers between devices: 23.1 us -> 26.7 us
  Pallas kernels: 33.1 us -> 29.6 us
  other arithmetic: 2.41 us -> 1.17 us
    all_to_all x0 -> x1, waiting for transfers between devices: none -> 7.79 us  [summed(): half = lax.all_to_all(half, ('chip', 'lon'), 0, 0, tiled=True)]
    ppermute x17 -> x18, starting transfers between devices: 29.7 us -> 23.2 us  [send(): return lax.ppermute(value, BOTH, pairs)]
    ppermute x8 -> x3, starting transfers between devices: 10.4 us -> 5.59 us  [the longest x1 3 us: sideways(): return lax.ppermute(packed, 'lon', east)]
    all_to_all x0 -> x1, starting transfers between devices: none -> 4.45 us  [summed(): half = lax.all_to_all(half, ('chip', 'lon'), 0, 0, tiled=True)]
    slice x5 -> x3, local copies, waits for them, and re-layouts: 5.58 us -> 1.29 us  [the longest x1 0.64 us: local(): upper[held[1]:held[1] + held[2]]]
    pallas_call x1 -> x4, Pallas kernels: 31 us -> 27.3 us  [the longest x2 26.8 us: call(): pl.pallas_call(functools.partial(level, shape, devices, () if second else...]
    ppermute x17 -> x18, waiting for transfers between devices: 19 us -> 16.3 us  [send(): return lax.ppermute(value, BOTH, pairs)]
    ppermute x8 -> x3, waiting for transfers between devices: 4.07 us -> 2.59 us  [the longest x1 2.59 us: sideways(): return lax.ppermute(packed, 'lon', east)]
  transfers between devices with their start and end apart: 25 -> 22, of which waited for: 8 -> 7; matrix products, arithmetic and copies ran while one was open for 4% -> 2% of each run, Pallas kernels for 2% -> 9%
where the time goes in v1:
time: 95.7 us; the launch traced here: 95.3 us
  starting transfers between devices  33.3 us (35%)
  Pallas kernels  29.6 us (31%)
  waiting for transfers between devices  26.7 us (28%)
  local copies, waits for them, and re-layouts  3.66 us (4%)
  other arithmetic  1.17 us (1%)
    pallas_call x2, Pallas kernels, call(): pl.pallas_call(functools.partial(level, shape, devices, () if second else...  26.8 us
    ppermute x18, starting transfers between devices, send(): return lax.ppermute(value, BOTH, pairs)  23.2 us
    ppermute x18, waiting for transfers between devices, send(): return lax.ppermute(value, BOTH, pairs)  16.3 us
    all_to_all x1, waiting for transfers between devices, summed(): half = lax.all_to_all(half, ('chip', 'lon'), 0, 0, tiled=True)  7.79 us
    all_to_all x1, starting transfers between devices, summed(): half = lax.all_to_all(half, ('chip', 'lon'), 0, 0, tiled=True)  4.45 us
    ppermute x1, starting transfers between devices, sideways(): return lax.ppermute(packed, 'lon', east)  3 us
    ppermute x2, starting transfers between devices, lengthways(): return (lax.ppermute(south, LAT, down), lax.ppermute(north, LAT, up))  2.59 us
    ppermute x1, waiting for transfers between devices, sideways(): return lax.ppermute(packed, 'lon', east)  2.59 us
  transfers between devices with their start and end apart: 22, of which 7 were waited for; matrix products, arithmetic and copies ran while one was open for 2% of the time, Pallas kernels for 9%

profile of v1, /device:TPU:0, one launch (start us, length us, event | category | flops | bytes accessed | tf_op | source)
XLA Modules:
  0.0 95.3 jit_solution(12126387565424405670)
XLA Ops:
  3.4 3.0 %collective-permute-start = (bf16[1536,128]{1,0:T(8,128)(2,1)S(1)}, bf16[1536,128]{1,0:T(8,128)(2,1)S(1)}, u32[]{:S(2)}, u32[]{:S(2)}) collective-permute-start(bf16[1536,128]{1,0:T(8,128)(2,1)S(1)} %get-tuple-element.21), channel_id=1, source_target_pairs={{0,1},{1,0},{2,3},{3,2},{4,5},{5,4},{6,7},{7,6},{8,9},{9,8},{10,11... | collective-permute-start | bytes 1179656 | tf_op jit(solution)/shard_map/ppermute | solution.py:211
  6.4 2.7 %collective-permute-start.4 = (bf16[224,128]{1,0:T(8,128)(2,1)S(1)}, bf16[224,128]{1,0:T(8,128)(2,1)S(1)}, u32[]{:S(2)}, u32[]{:S(2)}) collective-permute-start(bf16[224,128]{1,0:T(8,128)(2,1)S(1)} %get-tuple-element.44), channel_id=1, source_target_pairs={{0,16},{1,17},{2,18},{3,19},{4,20},{5,21},{6,22},{7,23},{8,24},{9,... | collective-permute-start | bytes 172040 | tf_op jit(solution)/shard_map/ppermute | solution.py:56
  9.1 1.6 %collective-permute-start.3 = (bf16[224,128]{1,0:T(8,128)(2,1)S(1)}, bf16[224,128]{1,0:T(8,128)(2,1)S(1)}, u32[]{:S(2)}, u32[]{:S(2)}) collective-permute-start(bf16[224,128]{1,0:T(8,128)(2,1)S(1)} %get-tuple-element.44), channel_id=1, source_target_pairs={{0,8},{1,9},{2,10},{3,11},{4,12},{5,13},{6,14},{7,15},{8,16},{9,17... | collective-permute-start | bytes 172040 | tf_op jit(solution)/shard_map/ppermute | solution.py:56
  10.7 2.2 %collective-permute-start.5 = (bf16[224,128]{1,0:T(8,128)(2,1)S(1)}, bf16[224,128]{1,0:T(8,128)(2,1)S(1)}, u32[]{:S(2)}, u32[]{:S(2)}) collective-permute-start(bf16[224,128]{1,0:T(8,128)(2,1)S(1)} %get-tuple-element.44), channel_id=1, source_target_pairs={{0,24},{1,25},{2,26},{3,27},{4,28},{5,29},{6,30},{7,31},{8,0},{9,1... | collective-permute-start | bytes 172040 | tf_op jit(solution)/shard_map/ppermute | solution.py:56
  12.9 2.6 %collective-permute-done.side_ref = bf16[1536,128]{1,0:T(8,128)(2,1)S(1)} collective-permute-done((bf16[1536,128]{1,0:T(8,128)(2,1)S(1)}, bf16[1536,128]{1,0:T(8,128)(2,1)S(1)}, u32[]{:S(2)}, u32[]{:S(2)}) %collective-permute-start) | collective-permute-done | bytes 393248 | tf_op jit(solution)/shard_map/ppermute | solution.py:211
  15.6 1.3 %collective-permute-start.1 = (bf16[1168,128]{1,0:T(8,128)(2,1)S(1)}, bf16[1168,128]{1,0:T(8,128)(2,1)S(1)}, u32[]{:S(2)}, u32[]{:S(2)}) collective-permute-start(bf16[1168,128]{1,0:T(8,128)(2,1)S(1)} %get-tuple-element.22), channel_id=1, source_target_pairs={{0,2},{2,4},{4,6},{6,8},{8,10},{10,12},{12,14},{14,16},{16,18},{18... | collective-permute-start | bytes 897032 | tf_op jit(solution)/shard_map/ppermute | solution.py:222
  16.9 3.4 %collective-permute-start.8 = (bf16[4,224,128]{2,1,0:T(8,128)(2,1)S(1)}, bf16[4,224,128]{2,1,0:T(8,128)(2,1)S(1)}, u32[]{:S(2)}, u32[]{:S(2)}) collective-permute-start(bf16[4,224,128]{2,1,0:T(8,128)(2,1)S(1)} %pad_maximum_fusion.refs_2_), channel_id=1, source_target_pairs={{0,5},{1,4},{2,7},{3,6},{4,1},{5,0},{6,3},{7,2},{8,13},{9,12},{10,... | collective-permute-start | bytes 688136 | tf_op jit(solution)/shard_map/ppermute | solution.py:56
  21.0 1.3 %collective-permute-start.2 = (bf16[1296,128]{1,0:T(8,128)(2,1)S(1)}, bf16[1296,128]{1,0:T(8,128)(2,1)S(1)}, u32[]{:S(2)}, u32[]{:S(2)}) collective-permute-start(bf16[1296,128]{1,0:T(8,128)(2,1)S(1)} %get-tuple-element.23), channel_id=1, source_target_pairs={{2,0},{4,2},{6,4},{8,6},{10,8},{12,10},{14,12},{16,14},{18,16},{20... | collective-permute-start | bytes 995336 | tf_op jit(solution)/shard_map/ppermute | solution.py:222
  22.2 3.5 %collective-permute-done.8.refs_5_ = bf16[4,224,128]{2,1,0:T(8,128)(2,1)S(1)} collective-permute-done((bf16[4,224,128]{2,1,0:T(8,128)(2,1)S(1)}, bf16[4,224,128]{2,1,0:T(8,128)(2,1)S(1)}, u32[]{:S(2)}, u32[]{:S(2)}) %collective-permute-start.8) | collective-permute-done | bytes 229408 | tf_op jit(solution)/shard_map/ppermute | solution.py:56
  25.8 2.0 %collective-permute-start.9 = (bf16[4,224,128]{2,1,0:T(8,128)(2,1)S(1)}, bf16[4,224,128]{2,1,0:T(8,128)(2,1)S(1)}, u32[]{:S(2)}, u32[]{:S(2)}) collective-permute-start(bf16[4,224,128]{2,1,0:T(8,128)(2,1)S(1)} %pad_maximum_fusion.refs_2_), channel_id=1, source_target_pairs={{0,2},{1,3},{2,0},{3,1},{4,6},{5,7},{6,4},{7,5},{8,10},{9,11},{10,... | collective-permute-start | bytes 688136 | tf_op jit(solution)/shard_map/ppermute | solution.py:56
  27.8 7.1 %collective-permute-done.7.refs_4_ = bf16[4,224,128]{2,1,0:T(8,128)(2,1)S(1)} collective-permute-done((bf16[4,224,128]{2,1,0:T(8,128)(2,1)S(1)}, bf16[4,224,128]{2,1,0:T(8,128)(2,1)S(1)}, u32[]{:S(2)}, u32[]{:S(2)}) %collective-permute-start.7) | collective-permute-done | bytes 229408 | tf_op jit(solution)/shard_map/ppermute | solution.py:56
  34.8 1.6 %collective-permute-start.12 = (bf16[4,224,128]{2,1,0:T(8,128)(2,1)S(1)}, bf16[4,224,128]{2,1,0:T(8,128)(2,1)S(1)}, u32[]{:S(2)}, u32[]{:S(2)}) collective-permute-start(bf16[4,224,128]{2,1,0:T(8,128)(2,1)S(1)} %collective-permute-done.8.refs_5_), channel_id=1, source_target_pairs={{0,2},{1,3},{2,0},{3,1},{4,6},{5,7},{6,4},{7,5},{8,10},{9,11},{10,... | collective-permute-start | bytes 688136 | tf_op jit(solution)/shard_map/ppermute | solution.py:56
  37.0 2.3 %shard_map.94 = (bf16[2112,768]{1,0:T(8,128)(2,1)S(1)}, bf16[2112,256]{1,0:T(8,128)(2,1)S(1)}) custom-call(bf16[64,64,128]{2,1,0:T(8,128)(2,1)S(1)} %copy-done.1, bf16[2,32,32,128]{3,2,1,0:T(8,128)(2,1)S(1)} %get-tuple-element.20.parts_ref, bf16[1536,128]{1,0:T(8,128)(2,1)S(1)} %collective-permute-done.side_ref, ...), custom_call_target="tpu_custom_call" | custom-call | bytes 12582912 | tf_op jit(solution)/shard_map/pallas_call | solution.py:741
  39.3 20.7 %shard_map.95 = (bf16[32,32,192]{2,1,0:T(8,128)(2,1)}, bf16[2,16,176,128]{3,2,1,0:T(8,128)(2,1)S(1)}, bf16[2112,640]{1,0:T(8,128)(2,1)S(1)}, bf16[512,768]{1,0:T(8,128)(2,1)S(1)}, bf16[256,1792]{1,0:T(8,128)(2,1)S(1)}) custom-call(bf16[2112,768]{1,0:T(8,128)(2,1)S(1)} %get-tuple-element.24.refs_0_, bf16[2112,256]{1,0:T(8,128)(2,1)S(1)} %get-tuple-element.25.refs_1_, ...), custom_call_target="tpu_custom_call" | custom-call | flops 5000000000 | bytes 12582912 | tf_op jit(solution)/shard_map/pallas_call | solution.py:775
  60.2 2.1 %collective-permute-done.13 = bf16[16,176,128]{2,1,0:T(8,128)(2,1)S(1)} collective-permute-done((bf16[16,176,128]{2,1,0:T(8,128)(2,1)S(1)}, bf16[16,176,128]{2,1,0:T(8,128)(2,1)S(1)}, u32[]{:S(2)}, u32[]{:S(2)}) %collective-permute-start.13) | collective-permute-done | bytes 720928 | tf_op jit(solution)/shard_map/ppermute | solution.py:56
  62.6 1.6 %collective-permute-start.15 = (bf16[4,176,128]{2,1,0:T(8,128)(2,1)S(1)}, bf16[4,176,128]{2,1,0:T(8,128)(2,1)S(1)}, u32[]{:S(2)}, u32[]{:S(2)}) collective-permute-start(bf16[4,176,128]{2,1,0:T(8,128)(2,1)S(1)} %get-tuple-element.35), channel_id=1, source_target_pairs={{0,1},{1,0},{2,3},{3,2},{4,5},{5,4},{6,7},{7,6},{8,9},{9,8},{10,11... | collective-permute-start | bytes 540680 | tf_op jit(solution)/shard_map/ppermute | solution.py:56
  64.1 2.1 %collective-permute-start.17 = (bf16[4,176,128]{2,1,0:T(8,128)(2,1)S(1)}, bf16[4,176,128]{2,1,0:T(8,128)(2,1)S(1)}, u32[]{:S(2)}, u32[]{:S(2)}) collective-permute-start(bf16[4,176,128]{2,1,0:T(8,128)(2,1)S(1)} %get-tuple-element.36), channel_id=1, source_target_pairs={{0,5},{1,4},{2,7},{3,6},{4,1},{5,0},{6,3},{7,2},{8,13},{9,12},{10,... | collective-permute-start | bytes 540680 | tf_op jit(solution)/shard_map/ppermute | solution.py:56
  66.3 6.1 %shard_map.96 = (bf16[64,64,128]{2,1,0:T(8,128)(2,1)}, bf16[2,16,64,128]{3,2,1,0:T(8,128)(2,1)S(1)}) custom-call(bf16[2112,768]{1,0:T(8,128)(2,1)S(1)} %get-tuple-element.24.refs_0_, bf16[2112,640]{1,0:T(8,128)(2,1)S(1)} %get-tuple-element.29.refs_1_, bf16[512,768]{1,0:T(8,128)(2,1)S(1)} %get-tuple-element.30.refs_2_, ...), custom_call_target="tpu_custom_call" | custom-call | flops 2000000000 | bytes 12582912 | tf_op jit(solution)/shard_map/pallas_call | solution.py:775
  72.5 2.2 %collective-permute-done.17 = bf16[4,176,128]{2,1,0:T(8,128)(2,1)S(1)} collective-permute-done((bf16[4,176,128]{2,1,0:T(8,128)(2,1)S(1)}, bf16[4,176,128]{2,1,0:T(8,128)(2,1)S(1)}, u32[]{:S(2)}, u32[]{:S(2)}) %collective-permute-start.17) | collective-permute-done | bytes 180256 | tf_op jit(solution)/shard_map/ppermute | solution.py:56
  74.8 1.4 %collective-permute-done.16 = bf16[4,176,128]{2,1,0:T(8,128)(2,1)S(1)} collective-permute-done((bf16[4,176,128]{2,1,0:T(8,128)(2,1)S(1)}, bf16[4,176,128]{2,1,0:T(8,128)(2,1)S(1)}, u32[]{:S(2)}, u32[]{:S(2)}) %collective-permute-start.16) | collective-permute-done | bytes 180256 | tf_op jit(solution)/shard_map/ppermute | solution.py:56
  76.3 1.6 %collective-permute-start.18 = (bf16[176,128]{1,0:T(8,128)(2,1)S(1)}, bf16[176,128]{1,0:T(8,128)(2,1)S(1)}, u32[]{:S(2)}, u32[]{:S(2)}) collective-permute-start(bf16[176,128]{1,0:T(8,128)(2,1)S(1)} %get-tuple-element.38), channel_id=1, source_target_pairs={{0,8},{1,9},{2,10},{3,11},{4,12},{5,13},{6,14},{7,15},{8,16},{9,17... | collective-permute-start | bytes 135176 | tf_op jit(solution)/shard_map/ppermute | solution.py:56
  77.9 2.2 %collective-permute-start.20 = (bf16[176,128]{1,0:T(8,128)(2,1)S(1)}, bf16[176,128]{1,0:T(8,128)(2,1)S(1)}, u32[]{:S(2)}, u32[]{:S(2)}) collective-permute-start(bf16[176,128]{1,0:T(8,128)(2,1)S(1)} %get-tuple-element.39), channel_id=1, source_target_pairs={{0,24},{1,25},{2,26},{3,27},{4,28},{5,29},{6,30},{7,31},{8,0},{9,1... | collective-permute-start | bytes 135176 | tf_op jit(solution)/shard_map/ppermute | solution.py:56
  81.7 4.5 %all-to-all-start = ((bf16[16,64,128]{2,1,0:T(8,128)(2,1)}), bf16[16,64,128]{2,1,0:T(8,128)(2,1)S(1)}, u32[]{:S(2)}, u32[]{:S(2)}) async-start(bf16[16,64,128]{2,1,0:T(8,128)(2,1)} %fusion.1), calls=%async_computation | async-start | bytes 524288 | tf_op jit(solution)/shard_map/all_to_all | solution.py:83
  86.9 7.8 %all-to-all-done = bf16[16,64,128]{2,1,0:T(8,128)(2,1)S(1)} async-done(((bf16[16,64,128]{2,1,0:T(8,128)(2,1)}), bf16[16,64,128]{2,1,0:T(8,128)(2,1)S(1)}, u32[]{:S(2)}, u32[]{:S(2)}) %all-to-all-start) | async-done | bytes 262176 | tf_op jit(solution)/shard_map/all_to_all | solution.py:83
  (51 shorter events, 7.6 us)
Async XLA Ops:
  2.9 3.5 %copy-start.5 = (bf16[6912]{0:T(1024)(128)(2,1)S(1)}, bf16[6912]{0:T(1024)(128)(2,1)}, u32[]{:S(2)}) copy-start(bf16[6912]{0:T(1024)(128)(2,1)} %param.6) | copy-start | bytes 41476
  3.4 33.6 %copy-start.1 = (bf16[64,64,128]{2,1,0:T(8,128)(2,1)S(1)}, bf16[64,64,128]{2,1,0:T(8,128)(2,1)}, u32[]{:S(2)}) copy-start(bf16[64,64,128]{2,1,0:T(8,128)(2,1)} %x_ref.5) | copy-start | bytes 3145732
  3.4 12.1 %collective-permute-start = (bf16[1536,128]{1,0:T(8,128)(2,1)S(1)}, bf16[1536,128]{1,0:T(8,128)(2,1)S(1)}, u32[]{:S(2)}, u32[]{:S(2)}) collective-permute-start(bf16[1536,128]{1,0:T(8,128)(2,1)S(1)} %get-tuple-element.21), channel_id=1, source_target_pairs={{0,1},{1,0},{2,3},{3,2},{4,5},{5,4},{6,7},{7,6},{8,9},{9,8},{10,11... | collective-permute-start | bytes 1179656 | tf_op jit(solution)/shard_map/ppermute | solution.py:211
  6.4 10.4 %collective-permute-start.4 = (bf16[224,128]{1,0:T(8,128)(2,1)S(1)}, bf16[224,128]{1,0:T(8,128)(2,1)S(1)}, u32[]{:S(2)}, u32[]{:S(2)}) collective-permute-start(bf16[224,128]{1,0:T(8,128)(2,1)S(1)} %get-tuple-element.44), channel_id=1, source_target_pairs={{0,16},{1,17},{2,18},{3,19},{4,20},{5,21},{6,22},{7,23},{8,24},{9,... | collective-permute-start | bytes 172040 | tf_op jit(solution)/shard_map/ppermute | solution.py:56
  9.1 7.8 %collective-permute-start.3 = (bf16[224,128]{1,0:T(8,128)(2,1)S(1)}, bf16[224,128]{1,0:T(8,128)(2,1)S(1)}, u32[]{:S(2)}, u32[]{:S(2)}) collective-permute-start(bf16[224,128]{1,0:T(8,128)(2,1)S(1)} %get-tuple-element.44), channel_id=1, source_target_pairs={{0,8},{1,9},{2,10},{3,11},{4,12},{5,13},{6,14},{7,15},{8,16},{9,17... | collective-permute-start | bytes 172040 | tf_op jit(solution)/shard_map/ppermute | solution.py:56
  10.7 6.2 %collective-permute-start.5 = (bf16[224,128]{1,0:T(8,128)(2,1)S(1)}, bf16[224,128]{1,0:T(8,128)(2,1)S(1)}, u32[]{:S(2)}, u32[]{:S(2)}) collective-permute-start(bf16[224,128]{1,0:T(8,128)(2,1)S(1)} %get-tuple-element.44), channel_id=1, source_target_pairs={{0,24},{1,25},{2,26},{3,27},{4,28},{5,29},{6,30},{7,31},{8,0},{9,1... | collective-permute-start | bytes 172040 | tf_op jit(solution)/shard_map/ppermute | solution.py:56
  15.6 20.9 %collective-permute-start.1 = (bf16[1168,128]{1,0:T(8,128)(2,1)S(1)}, bf16[1168,128]{1,0:T(8,128)(2,1)S(1)}, u32[]{:S(2)}, u32[]{:S(2)}) collective-permute-start(bf16[1168,128]{1,0:T(8,128)(2,1)S(1)} %get-tuple-element.22), channel_id=1, source_target_pairs={{0,2},{2,4},{4,6},{6,8},{8,10},{10,12},{12,14},{14,16},{16,18},{18... | collective-permute-start | bytes 897032 | tf_op jit(solution)/shard_map/ppermute | solution.py:222
  16.9 8.8 %collective-permute-start.8 = (bf16[4,224,128]{2,1,0:T(8,128)(2,1)S(1)}, bf16[4,224,128]{2,1,0:T(8,128)(2,1)S(1)}, u32[]{:S(2)}, u32[]{:S(2)}) collective-permute-start(bf16[4,224,128]{2,1,0:T(8,128)(2,1)S(1)} %pad_maximum_fusion.refs_2_), channel_id=1, source_target_pairs={{0,5},{1,4},{2,7},{3,6},{4,1},{5,0},{6,3},{7,2},{8,13},{9,12},{10,... | collective-permute-start | bytes 688136 | tf_op jit(solution)/shard_map/ppermute | solution.py:56
  20.3 14.5 %collective-permute-start.7 = (bf16[4,224,128]{2,1,0:T(8,128)(2,1)S(1)}, bf16[4,224,128]{2,1,0:T(8,128)(2,1)S(1)}, u32[]{:S(2)}, u32[]{:S(2)}) collective-permute-start(bf16[4,224,128]{2,1,0:T(8,128)(2,1)S(1)} %pad_maximum_fusion.refs_2_), channel_id=1, source_target_pairs={{0,4},{1,5},{2,6},{3,7},{4,0},{5,1},{6,2},{7,3},{8,12},{9,13},{10,... | collective-permute-start | bytes 688136 | tf_op jit(solution)/shard_map/ppermute | solution.py:56
  20.3 16.1 %collective-permute-start.6 = (bf16[4,224,128]{2,1,0:T(8,128)(2,1)S(1)}, bf16[4,224,128]{2,1,0:T(8,128)(2,1)S(1)}, u32[]{:S(2)}, u32[]{:S(2)}) collective-permute-start(bf16[4,224,128]{2,1,0:T(8,128)(2,1)S(1)} %pad_maximum_fusion.refs_2_), channel_id=1, source_target_pairs={{0,1},{1,0},{2,3},{3,2},{4,5},{5,4},{6,7},{7,6},{8,9},{9,8},{10,11... | collective-permute-start | bytes 688136 | tf_op jit(solution)/shard_map/ppermute | solution.py:56
  21.0 16.0 %collective-permute-start.2 = (bf16[1296,128]{1,0:T(8,128)(2,1)S(1)}, bf16[1296,128]{1,0:T(8,128)(2,1)S(1)}, u32[]{:S(2)}, u32[]{:S(2)}) collective-permute-start(bf16[1296,128]{1,0:T(8,128)(2,1)S(1)} %get-tuple-element.23), channel_id=1, source_target_pairs={{2,0},{4,2},{6,4},{8,6},{10,8},{12,10},{14,12},{16,14},{18,16},{20... | collective-permute-start | bytes 995336 | tf_op jit(solution)/shard_map/ppermute | solution.py:222
  25.8 13.5 %collective-permute-start.9 = (bf16[4,224,128]{2,1,0:T(8,128)(2,1)S(1)}, bf16[4,224,128]{2,1,0:T(8,128)(2,1)S(1)}, u32[]{:S(2)}, u32[]{:S(2)}) collective-permute-start(bf16[4,224,128]{2,1,0:T(8,128)(2,1)S(1)} %pad_maximum_fusion.refs_2_), channel_id=1, source_target_pairs={{0,2},{1,3},{2,0},{3,1},{4,6},{5,7},{6,4},{7,5},{8,10},{9,11},{10,... | collective-permute-start | bytes 688136 | tf_op jit(solution)/shard_map/ppermute | solution.py:56
  34.8 4.5 %collective-permute-start.12 = (bf16[4,224,128]{2,1,0:T(8,128)(2,1)S(1)}, bf16[4,224,128]{2,1,0:T(8,128)(2,1)S(1)}, u32[]{:S(2)}, u32[]{:S(2)}) collective-permute-start(bf16[4,224,128]{2,1,0:T(8,128)(2,1)S(1)} %collective-permute-done.8.refs_5_), channel_id=1, source_target_pairs={{0,2},{1,3},{2,0},{3,1},{4,6},{5,7},{6,4},{7,5},{8,10},{9,11},{10,... | collective-permute-start | bytes 688136 | tf_op jit(solution)/shard_map/ppermute | solution.py:56
  36.4 2.9 %collective-permute-start.11 = (bf16[4,224,128]{2,1,0:T(8,128)(2,1)S(1)}, bf16[4,224,128]{2,1,0:T(8,128)(2,1)S(1)}, u32[]{:S(2)}, u32[]{:S(2)}) collective-permute-start(bf16[4,224,128]{2,1,0:T(8,128)(2,1)S(1)} %collective-permute-done.7.refs_4_), channel_id=1, source_target_pairs={{0,2},{1,3},{2,0},{3,1},{4,6},{5,7},{6,4},{7,5},{8,10},{9,11},{10,... | collective-permute-start | bytes 688136 | tf_op jit(solution)/shard_map/ppermute | solution.py:56
  36.4 2.9 %collective-permute-start.10 = (bf16[4,224,128]{2,1,0:T(8,128)(2,1)S(1)}, bf16[4,224,128]{2,1,0:T(8,128)(2,1)S(1)}, u32[]{:S(2)}, u32[]{:S(2)}) collective-permute-start(bf16[4,224,128]{2,1,0:T(8,128)(2,1)S(1)} %collective-permute-done.6.refs_3_), channel_id=1, source_target_pairs={{0,2},{1,3},{2,0},{3,1},{4,6},{5,7},{6,4},{7,5},{8,10},{9,11},{10,... | collective-permute-start | bytes 688136 | tf_op jit(solution)/shard_map/ppermute | solution.py:56
  60.1 2.3 %collective-permute-start.13 = (bf16[16,176,128]{2,1,0:T(8,128)(2,1)S(1)}, bf16[16,176,128]{2,1,0:T(8,128)(2,1)S(1)}, u32[]{:S(2)}, u32[]{:S(2)}) collective-permute-start(bf16[16,176,128]{2,1,0:T(8,128)(2,1)S(1)} %slice_bitcast_fusion), channel_id=1, source_target_pairs={{0,2},{1,3},{2,0},{3,1},{4,6},{5,7},{6,4},{7,5},{8,10},{9,11},{10,... | collective-permute-start | bytes 2162696 | tf_op jit(solution)/shard_map/ppermute | solution.py:56
  62.6 10.0 %collective-permute-start.15 = (bf16[4,176,128]{2,1,0:T(8,128)(2,1)S(1)}, bf16[4,176,128]{2,1,0:T(8,128)(2,1)S(1)}, u32[]{:S(2)}, u32[]{:S(2)}) collective-permute-start(bf16[4,176,128]{2,1,0:T(8,128)(2,1)S(1)} %get-tuple-element.35), channel_id=1, source_target_pairs={{0,1},{1,0},{2,3},{3,2},{4,5},{5,4},{6,7},{7,6},{8,9},{9,8},{10,11... | collective-permute-start | bytes 540680 | tf_op jit(solution)/shard_map/ppermute | solution.py:56
  64.1 10.7 %collective-permute-start.17 = (bf16[4,176,128]{2,1,0:T(8,128)(2,1)S(1)}, bf16[4,176,128]{2,1,0:T(8,128)(2,1)S(1)}, u32[]{:S(2)}, u32[]{:S(2)}) collective-permute-start(bf16[4,176,128]{2,1,0:T(8,128)(2,1)S(1)} %get-tuple-element.36), channel_id=1, source_target_pairs={{0,5},{1,4},{2,7},{3,6},{4,1},{5,0},{6,3},{7,2},{8,13},{9,12},{10,... | collective-permute-start | bytes 540680 | tf_op jit(solution)/shard_map/ppermute | solution.py:56
  66.2 9.9 %collective-permute-start.16 = (bf16[4,176,128]{2,1,0:T(8,128)(2,1)S(1)}, bf16[4,176,128]{2,1,0:T(8,128)(2,1)S(1)}, u32[]{:S(2)}, u32[]{:S(2)}) collective-permute-start(bf16[4,176,128]{2,1,0:T(8,128)(2,1)S(1)} %get-tuple-element.37), channel_id=1, source_target_pairs={{0,4},{1,5},{2,6},{3,7},{4,0},{5,1},{6,2},{7,3},{8,12},{9,13},{10,... | collective-permute-start | bytes 540680 | tf_op jit(solution)/shard_map/ppermute | solution.py:56
  72.5 8.5 %collective-permute-start.14 = (bf16[16,64,128]{2,1,0:T(8,128)(2,1)S(1)}, bf16[16,64,128]{2,1,0:T(8,128)(2,1)S(1)}, u32[]{:S(2)}, u32[]{:S(2)}) collective-permute-start(bf16[16,64,128]{2,1,0:T(8,128)(2,1)S(1)} %slice_bitcast_fusion.1), channel_id=1, source_target_pairs={{0,2},{1,3},{2,0},{3,1},{4,6},{5,7},{6,4},{7,5},{8,10},{9,11},{10,... | collective-permute-start | bytes 786440 | tf_op jit(solution)/shard_map/ppermute | solution.py:56
  76.3 9.9 %collective-permute-start.18 = (bf16[176,128]{1,0:T(8,128)(2,1)S(1)}, bf16[176,128]{1,0:T(8,128)(2,1)S(1)}, u32[]{:S(2)}, u32[]{:S(2)}) collective-permute-start(bf16[176,128]{1,0:T(8,128)(2,1)S(1)} %get-tuple-element.38), channel_id=1, source_target_pairs={{0,8},{1,9},{2,10},{3,11},{4,12},{5,13},{6,14},{7,15},{8,16},{9,17... | collective-permute-start | bytes 135176 | tf_op jit(solution)/shard_map/ppermute | solution.py:56
  77.9 8.3 %collective-permute-start.20 = (bf16[176,128]{1,0:T(8,128)(2,1)S(1)}, bf16[176,128]{1,0:T(8,128)(2,1)S(1)}, u32[]{:S(2)}, u32[]{:S(2)}) collective-permute-start(bf16[176,128]{1,0:T(8,128)(2,1)S(1)} %get-tuple-element.39), channel_id=1, source_target_pairs={{0,24},{1,25},{2,26},{3,27},{4,28},{5,29},{6,30},{7,31},{8,0},{9,1... | collective-permute-start | bytes 135176 | tf_op jit(solution)/shard_map/ppermute | solution.py:56
  80.1 6.1 %collective-permute-start.19 = (bf16[176,128]{1,0:T(8,128)(2,1)S(1)}, bf16[176,128]{1,0:T(8,128)(2,1)S(1)}, u32[]{:S(2)}, u32[]{:S(2)}) collective-permute-start(bf16[176,128]{1,0:T(8,128)(2,1)S(1)} %get-tuple-element.40), channel_id=1, source_target_pairs={{0,16},{1,17},{2,18},{3,19},{4,20},{5,21},{6,22},{7,23},{8,24},{9,... | collective-permute-start | bytes 135176 | tf_op jit(solution)/shard_map/ppermute | solution.py:56
  81.7 13.0 %all-to-all-start = ((bf16[16,64,128]{2,1,0:T(8,128)(2,1)}), bf16[16,64,128]{2,1,0:T(8,128)(2,1)S(1)}, u32[]{:S(2)}, u32[]{:S(2)}) async-start(bf16[16,64,128]{2,1,0:T(8,128)(2,1)} %fusion.1), calls=%async_computation | async-start | bytes 524288 | tf_op jit(solution)/shard_map/all_to_all | solution.py:83
  (4 other events, 9.2 us)

commit v2 on v1

--- a/solution.py
+++ b/solution.py
@@ -45,8 +45,17 @@
     def moved(self, coords, steps, sign=1):
         out = []
         for at, by, size in zip(coords, steps, self.sizes):
-            to = at + sign * by + size
-            out.append(to % size if isinstance(to, int) else lax.rem(to, size))
+            if size & (size - 1) == 0:
+                out.append(at ^ by)
+            else:
+                to = at + sign * by + size
+                out.append(to % size if isinstance(to, int) else lax.rem(to, size))
+        return tuple(out)
+
+    def apart(self, coords, origin):
+        out = []
+        for to, at, size in zip(coords, origin, self.sizes):
+            out.append(at ^ to if size & (size - 1) == 0 else lax.rem(to - at + size, size))
         return tuple(out)
 
     def send(self, value, steps):
@@ -56,20 +65,30 @@
         return lax.ppermute(value, BOTH, pairs)
 
 
-def gathered(devices, shard):
+def lined(devices, shard):
+    far = devices.sizes[0]
+    return jnp.stack([shard] + [devices.send(shard, (f, 0, 0, 0)) for f in range(1, far)])
+
+
+def spread(devices, line):
     far, near, core, lon = devices.sizes
-    line = jnp.stack([shard] + [devices.send(shard, (f, 0, 0, 0)) for f in range(1, far)])
-    planes, parts = [], []
+    planes = []
+    for n in range(near):
+        for o in range(lon):
+            planes.append(line if n == o == 0 else devices.send(line, (0, n, 0, o)))
+    return planes
+
+
+def shared_out(devices, planes):
+    far, near, core, lon = devices.sizes
+    out, parts = [], []
     for c in range(core):
         for n in range(near):
             for o in range(lon):
-                if c:
-                    plane = devices.send(planes[n * lon + o], (0, 0, c, 0))
-                else:
-                    plane = line if n == o == 0 else devices.send(line, (0, n, 0, o))
-                planes.append(plane)
+                plane = planes[n * lon + o]
+                out.append(devices.send(plane, (0, 0, c, 0)) if c else plane)
                 parts.append((c, n, o))
-    return planes, parts
+    return out, parts
 
 
 def halved(devices, chunks):
@@ -77,11 +96,6 @@
     for c in range(1, chunks.shape[0]):
         half = half + devices.send(chunks[c], (0, 0, c, 0)).astype(F32)
     return half.astype(BF16)
-
-
-def summed(half, size):
-    half = lax.all_to_all(half, ("chip", "lon"), 0, 0, tiled=True)
-    return jnp.sum(half.astype(F32), axis=0).reshape(-1)[:size]
 
 
 def order(devices, sign):
@@ -96,35 +110,27 @@
     return jnp.stack(places)
 
 
-def owners(devices):
+def total_of(terms):
+    total = terms[0].astype(F32)
+    for term in terms[1:]:
+        total = total + term.astype(F32)
+    return total
+
+
+def planar(devices, half):
     far, near, core, lon = devices.sizes
-    at = devices.place()[1][2]
-    places = []
-    for c in range(core):
-        for f in range(far):
-            for n in range(near):
-                for o in range(lon):
-                    places.append(devices.index((f, n, lax.rem(at + c, core), o)))
-    return jnp.stack(places)
-
-
-def passed(devices, half):
-    far, near, core, lon = devices.sizes
-
-    def add(terms):
-        total = terms[0].astype(F32)
-        for term in terms[1:]:
-            total = total + term.astype(F32)
-        return total
-
     half = half.reshape(near * lon, far, *half.shape[1:])
     terms = []
     for n in range(near):
         for o in range(lon):
             part = half[n * lon + o]
             terms.append(part if n == o == 0 else devices.send(part, (0, n, 0, o)))
-    line = add(terms).astype(BF16)
-    return add([line[0]] + [devices.send(line[f], (f, 0, 0, 0)) for f in range(1, far)])
+    return total_of(terms).astype(BF16)
+
+
+def linear(devices, line):
+    far = devices.sizes[0]
+    return total_of([line[0]] + [devices.send(line[f], (f, 0, 0, 0)) for f in range(1, far)])
 
 
 WEST, EAST = 9, 10
@@ -132,31 +138,23 @@
 CORNER = 16
 
 
-def strips(rows, cols):
+def strips(inputs_high, cots_high):
     side, at = [], 0
     for inputs, cots in ((WEST, BEFORE), (EAST, AFTER)):
-        columns = [at + 2 * rows * j for j in range(inputs)]
-        at += 2 * rows * inputs
-        parts = [[at + rows * (cots * part + j) for j in range(cots)] for part in range(2)]
-        at += 2 * rows * cots
+        columns = [at + inputs_high * j for j in range(inputs)]
+        at += inputs_high * inputs
+        parts = [[at + cots_high * (cots * part + j) for j in range(cots)] for part in range(2)]
+        at += 2 * cots_high * cots
         side.append((columns, parts))
     return side, at
 
 
-def edges(rows, cols, inputs, cots):
-    places = [0, 2 * cols * inputs]
-    places.append(places[-1] + CORNER * (WEST + EAST))
-    places.append(places[-1] + 2 * cots * cols)
-    places.append(places[-1] + 2 * CORNER * (BEFORE + AFTER))
-    return places
-
-
 def halves(value):
     return value[..., :128], jnp.concatenate([value[..., 128:], value[..., 128:]], axis=-1)
 
 
-def pack_sides(rows, cols, x_ref, c_ref, side_ref, parts_ref, strip):
-    west, east = strips(rows, cols)[0]
+def pack_sides(rows, cols, x_ref, c_ref, side_ref, south_ref, north_ref, strip):
+    west, east = strips(2 * rows, rows)[0]
 
     def columns(value, wanted, places):
         high = value.shape[0]
@@ -168,48 +166,38 @@
     columns(x_ref[:, :CORNER, :], range(EAST), east[0])
     parts = halves(c_ref[...])
     for part in range(2):
-        parts_ref[part] = parts[part]
         columns(parts[part][:, cols - CORNER :], range(CORNER - BEFORE, CORNER), west[1][part])
         columns(parts[part][:, :CORNER], range(AFTER), east[1][part])
-
-
-def pack_edges(rows, cols, x_ref, parts_ref, side_ref, south_ref, north_ref):
-    side = strips(rows, cols)[0]
-    for ref, inputs, cots, last in (
-        (south_ref, WEST, BEFORE, True),
-        (north_ref, EAST, AFTER, False),
+    for ref, inputs, cots, x_row, c_row in (
+        (south_ref, WEST, BEFORE, 2 * rows - WEST, rows - BEFORE),
+        (north_ref, EAST, AFTER, 0, 0),
     ):
-        at = edges(rows, cols, inputs, cots)
-        first = 2 * rows - inputs if last else 0
         for i in range(inputs):
-            ref[at[0] + 2 * cols * i : at[0] + 2 * cols * (i + 1), :] = x_ref[first + i]
-        first = 2 * rows - CORNER if last else 0
-        to = at[1]
-        for columns, _ in side:
-            for place in columns:
-                ref[to : to + CORNER, :] = side_ref[place + first : place + first + CORNER, :]
-                to += CORNER
-        first = rows - cots if last else 0
-        to = at[2]
+            ref[2 * cols * i : 2 * cols * (i + 1), :] = x_ref[x_row + i]
+        at = 2 * cols * inputs
         for part in range(2):
             for i in range(cots):
-                ref[to : to + cols, :] = parts_ref[part, first + i]
-                to += cols
-        first = rows - CORNER if last else 0
+                ref[at : at + cols, :] = parts[part][c_row + i]
+                at += cols
+
+
+def pack_corners(rows, side_ref, lower_ref, upper_ref):
+    for side, corner in zip(strips(2 * rows, rows)[0], strips(CORNER, CORNER)[0]):
+        strip = [(2 * rows, *pair) for pair in zip(side[0], corner[0])]
         for part in range(2):
-            for _, parts in side:
-                for place in parts[part]:
-                    ref[to : to + CORNER, :] = side_ref[place + first : place + first + CORNER, :]
-                    to += CORNER
-
-
-def sideways(rows, cols, packed):
+            strip += [(rows, *pair) for pair in zip(side[1][part], corner[1][part])]
+        for high, place, to in strip:
+            end = place + high
+            lower_ref[to : to + CORNER, :] = side_ref[end - CORNER : end, :]
+            upper_ref[to : to + CORNER, :] = side_ref[place : place + CORNER, :]
+
+
+def sideways(packed, cut):
     count = lax.axis_size("lon")
     east = [(i, (i + 1) % count) for i in range(count)]
     west = [(i, (i - 1) % count) for i in range(count)]
     if count == 2:
         return lax.ppermute(packed, "lon", east)
-    cut = strips(rows, cols)[0][1][0][0]
     before = lax.ppermute(packed[:cut], "lon", east)
     after = lax.ppermute(packed[cut:], "lon", west)
     return jnp.concatenate([before, after], axis=0)
@@ -243,7 +231,8 @@
 
 
 def prepare(
-    rows, cols, x_ref, parts_ref, side_ref, south_ref, north_ref, windows_ref, cot_ref, wide, cots
+    rows, cols, x_ref, c_ref, side_ref, south_ref, north_ref, lower_ref, upper_ref,
+    windows_ref, cot_ref, wide, cots,
 ):
     pitch = cols + LEFT
     height = rows + ABOVE + BELOW
@@ -252,7 +241,8 @@
     base_row, base_col = 20, 24
     wide[...] = jnp.zeros_like(wide)
     cots[...] = jnp.zeros_like(cots)
-    side = strips(rows, cols)[0]
+    side = strips(2 * rows, rows)[0]
+    corners = strips(CORNER, CORNER)[0]
     columns = [*range(-WEST, 0), *range(2 * cols, 2 * cols + EAST)]
 
     def at(i, j):
@@ -266,18 +256,15 @@
     for j, place in zip(columns, side[0][0] + side[1][0]):
         strip = side_ref[place : place + 2 * rows, :].astype(F32)
         wide[pl.ds(at(0, j), 2 * rows, stride=span), :] = strip
-    for ref, inputs, cotangents, top, above in (
-        (south_ref, WEST, BEFORE, -WEST, True),
-        (north_ref, EAST, AFTER, 2 * rows, False),
+    for ref, corner_ref, inputs, top, first in (
+        (south_ref, lower_ref, WEST, -WEST, -CORNER),
+        (north_ref, upper_ref, EAST, 2 * rows, 2 * rows),
     ):
-        places = edges(rows, cols, inputs, cotangents)
         for i in range(inputs):
             edge = ref[2 * cols * i : 2 * cols * (i + 1), :].astype(F32)
             wide[at(top + i, 0) : at(top + i, 0) + 2 * cols, :] = edge
-        first = -CORNER if above else 2 * rows
-        for k, j in enumerate(columns):
-            place = places[1] + CORNER * k
-            corner = ref[place : place + CORNER, :].astype(F32)
+        for place, j in zip(corners[0][0] + corners[1][0], columns):
+            corner = corner_ref[place : place + CORNER, :].astype(F32)
             wide[pl.ds(at(first, j), CORNER, stride=span), :] = corner
 
     def window(k, _):
@@ -299,32 +286,28 @@
         return GUARD + (i + ABOVE) * pitch + LEFT + j
 
     columns = [*range(-BEFORE, 0), *range(cols, cols + AFTER)]
+    parts = halves(c_ref[...])
     for part in range(2):
         for i in range(rows):
-            cots[cell(i, 0) : cell(i, cols), :] = parts_ref[part, i].astype(F32)
+            cots[cell(i, 0) : cell(i, cols), :] = parts[part][i].astype(F32)
         for j, place in zip(columns, side[0][1][part] + side[1][1][part]):
             strip = side_ref[place : place + rows, :].astype(F32)
             cots[pl.ds(cell(0, j), rows, stride=pitch), :] = strip
-        for ref, inputs, cotangents, above in (
-            (south_ref, WEST, BEFORE, True),
-            (north_ref, EAST, AFTER, False),
+        for ref, corner_ref, inputs, count, above in (
+            (south_ref, lower_ref, WEST, BEFORE, True),
+            (north_ref, upper_ref, EAST, AFTER, False),
         ):
-            places = edges(rows, cols, inputs, cotangents)
-            for i in range(cotangents):
-                place = places[2] + cols * (cotangents * part + i)
-                to = cell(i - cotangents if above else rows + i, 0)
+            first = -count if above else rows
+            for i in range(count):
+                place = 2 * cols * inputs + cols * (count * part + i)
+                to = cell(first + i, 0)
                 cots[to : to + cols, :] = ref[place : place + cols, :].astype(F32)
-            for k, j in enumerate(columns):
-                place = places[3] + CORNER * (len(columns) * part + k)
-                corner = ref[place : place + CORNER, :].astype(F32)
-                if above:
-                    corner = corner[CORNER - 8 :]
-                else:
-                    corner = corner[:8]
-                for i in range(cotangents):
-                    to = cell(i - cotangents if above else rows + i, j)
-                    line = 8 - cotangents + i if above else i
-                    cots[to : to + 1, :] = corner[line : line + 1]
+            for place, j in zip(corners[0][1][part] + corners[1][1][part], columns):
+                corner = corner_ref[place : place + CORNER, :].astype(F32)
+                corner = corner[CORNER - 8 :] if above else corner[:8]
+                for i in range(count):
+                    line = 8 - count + i if above else i
+                    cots[cell(first + i, j) : cell(first + i, j) + 1, :] = corner[line : line + 1]
         cot_ref[:, 128 * part : 128 * part + 128] = cots[GUARD : GUARD + size, :].astype(BF16)
 
 
@@ -356,7 +339,7 @@
                 value = plane[f, lo:hi, :].astype(F32)
                 flat[pl.ds(owner * n, n), :] = value[begin[which] - lo : begin[which] - lo + n]
         pairs = 9 * channels // 2
-        step = 96
+        step = 288
 
         def one(i, _):
             at = i * step
@@ -464,20 +447,22 @@
         f_b[pl.ds(at, n), :] = right
 
     def windows(target, top, under):
+        wide = -(-(under - top) * pitch // 6 // 16) * 16
+
         def one(i, _):
-            cell = i * pitch
+            cell = (top + ABOVE) * pitch + i * wide
             q = cell + GUARD
-            low = low_lanes(pitch)
-            b_0, b_1, b_2 = (f_b[pl.ds(q + s, pitch), :] for s in (-1, 0, 1))
-            b_3 = f_b[pl.ds(q + 1 + pitch, pitch), :]
-            out = [f_a[pl.ds(q + s, pitch), :] for s in (-1, 0, 1)]
+            low = low_lanes(wide)
+            b_0, b_1, b_2 = (f_b[pl.ds(q + s, wide), :] for s in (-1, 0, 1))
+            b_3 = f_b[pl.ds(q + 1 + pitch, wide), :]
+            out = [f_a[pl.ds(q + s, wide), :] for s in (-1, 0, 1)]
             out += [jnp.where(low, b_0, b_1), jnp.where(low, b_2, b_3)]
             at = pl.multiple_of(cell, 16)
             for j, value in enumerate(out):
-                target[pl.ds(at, pitch), 128 * j : 128 * j + 128] = value.astype(BF16)
+                target[pl.ds(at, wide), 128 * j : 128 * j + 128] = value.astype(BF16)
             return 0
 
-        lax.fori_loop(top + ABOVE, under + ABOVE, one, 0)
+        lax.fori_loop(0, 6, one, 0)
 
     def convolve(source, weights, turned, halo, steps, finish):
         start = (ABOVE - halo) * pitch
@@ -516,7 +501,7 @@
         return jnp.concatenate([left.T, right.T], axis=0).astype(BF16)
 
     def pack(which, channels, first=0):
-        step = 96
+        step = 288
 
         def one(i, _):
             at = i * step
@@ -540,12 +525,8 @@
             f, m, c, o = devices.coords(k)
             place, side = 0, 0
             if not whole:
-                side = lax.rem(c - mine[2] + core, core)
-                place = (f * near + m) * lon + o
-                if not second:
-                    away = zip(devices.coords(k), mine, devices.sizes)
-                    f, m, c, o = (lax.rem(to - at + by, by) for to, at, by in away)
-                    place = (m * lon + o) * far + f
+                f, m, side, o = devices.apart(devices.coords(k), mine)
+                place = (m * lon + o) * far + f
             terms_ref[side, place] = refs["chunk"][k].astype(BF16)
 
     def field_grad(which, source, first):
@@ -580,7 +561,7 @@
         slope[...] = jnp.zeros_like(slope)
 
         def convolve_first():
-            halo, steps = 4, 4
+            halo, steps = 4, 2
             start = (ABOVE - halo) * pitch
             total = (rows + 1 + 2 * halo) * pitch + LEFT
             n = -(-total // steps // 16) * 16
@@ -609,7 +590,7 @@
             slope[pl.ds(p, n), :] = s + active * (1.0 - s)
             store(p, n, active[:, :128], active[:, 128:], True)
 
-        convolve(win_one, refs["w_two"], False, 3, 4, finish_two)
+        convolve(win_one, refs["w_two"], False, 3, 2, finish_two)
         windows(win_two, -3, rows + 5)
 
         def finish_three(p, n, value):
@@ -619,7 +600,7 @@
             store(p, n, delta[:, :128], delta[:, 128:], False)
             spread[pl.ds(p, n), :] = active
 
-        convolve(win_two, refs["w_three"], False, 2, 4, finish_three)
+        convolve(win_two, refs["w_three"], False, 2, 2, finish_three)
         for r in range(rows):
             at = (ABOVE + r) * pitch + LEFT
             refs["features"][r] = spread[at : at + cols, 0:mid].astype(BF16)
@@ -630,7 +611,7 @@
             value = value * slope[pl.ds(p, n), :]
             store(p, n, value[:, :128], value[:, 128:], True)
 
-        convolve(win_delta, refs["t_three"], True, 1, 4, finish_delta)
+        convolve(win_delta, refs["t_three"], True, 1, 2, finish_delta)
         field_grad(1, win_one, 0)
         hand_over()
         windows(win_delta, -1, rows + 3)
@@ -639,7 +620,7 @@
         def finish_back(p, n, value):
             store(p, n, value[:, :128], value[:, 128:], True)
 
-        convolve(win_delta, t_two, True, 0, 4, finish_back)
+        convolve(win_delta, t_two, True, 0, 2, finish_back)
         turned = turned_deltas()
         for a, (step, lanes) in enumerate(((-1, slice(384, 768)), (0, slice(0, 384)), (0, slice(384, 768)))):
             product = lax.dot_general(
@@ -701,42 +682,40 @@
     whole = any(n % 128 for n in held)
     if not whole:
         shard = jnp.pad(shard, ((0, -shard.shape[0] % 16), (0, 0)))
-    planes, parts = gathered(devices, shard)
-    if whole:
-        chunks = jnp.stack(planes).reshape(devices.count, -1)
-        chunks = jnp.take(chunks, jnp.argsort(order(devices, -1)), axis=0)
-        pieces = jnp.split(chunks, (held[0], held[0] + held[1]), axis=1)
-        chunks = jnp.concatenate([piece.reshape(-1) for piece in pieces])
-        planes, parts = [chunks.reshape(1, -1, 128)], [(0, 0, 0)]
     count = 1 if whole else devices.count
-    depth = planes[0].shape[1]
-
-    packed_rows = strips(rows, cols)[1]
-    packed, split_cot = pl.pallas_call(
+
+    side_rows, corner_rows = strips(2 * rows, rows)[1], strips(CORNER, CORNER)[1]
+    south_rows = 2 * cols * (WEST + BEFORE)
+    north_rows = 2 * cols * (EAST + AFTER)
+    cost = pl.CostEstimate(flops=0, bytes_accessed=3 * 2**20, transcendentals=0)
+    params = pltpu.CompilerParams(vmem_limit_bytes=16 * 2**20)
+
+    def buffers(*sizes):
+        return [jax.ShapeDtypeStruct((n, 128), BF16) for n in sizes]
+
+    side, south, north = pl.pallas_call(
         functools.partial(pack_sides, rows, cols),
-        out_shape=(
-            jax.ShapeDtypeStruct((packed_rows, 128), BF16),
-            jax.ShapeDtypeStruct((2, rows, cols, 128), BF16),
-        ),
+        out_shape=buffers(side_rows, south_rows, north_rows),
         in_specs=[VMEM] * 2,
-        out_specs=(VMEM, VMEM),
+        out_specs=[VMEM] * 3,
         scratch_shapes=[pltpu.VMEM((2 * rows * CORNER, 128), F32)],
-        compiler_params=pltpu.CompilerParams(vmem_limit_bytes=16 * 2**20),
-        cost_estimate=pl.CostEstimate(flops=0, bytes_accessed=3 * 2**20, transcendentals=0),
+        compiler_params=params,
+        cost_estimate=cost,
     )(inputs, cotangent)
-    side = sideways(rows, cols, packed)
-    south, north = pl.pallas_call(
-        functools.partial(pack_edges, rows, cols),
-        out_shape=(
-            jax.ShapeDtypeStruct((edges(rows, cols, WEST, BEFORE)[-1], 128), BF16),
-            jax.ShapeDtypeStruct((edges(rows, cols, EAST, AFTER)[-1], 128), BF16),
-        ),
-        in_specs=[VMEM] * 3,
-        out_specs=(VMEM, VMEM),
-        compiler_params=pltpu.CompilerParams(vmem_limit_bytes=16 * 2**20),
-        cost_estimate=pl.CostEstimate(flops=0, bytes_accessed=3 * 2**20, transcendentals=0),
-    )(inputs, split_cot, side)
+    line = lined(devices, shard)
     south, north = lengthways(south, north)
+    side = sideways(side, strips(2 * rows, rows)[0][1][0][0])
+    lower, upper = pl.pallas_call(
+        functools.partial(pack_corners, rows),
+        out_shape=buffers(corner_rows, corner_rows),
+        in_specs=[VMEM],
+        out_specs=[VMEM] * 2,
+        compiler_params=params,
+        cost_estimate=cost,
+    )(side)
+    lower, upper = lengthways(lower, upper)
+    line, south, north, side = lax.optimization_barrier((line, south, north, side))
+    planes = spread(devices, line)
     size = (rows + ABOVE + BELOW) * (cols + LEFT)
     padded, cot = pl.pallas_call(
         functools.partial(prepare, rows, cols),
@@ -744,7 +723,7 @@
             jax.ShapeDtypeStruct((size, 6 * chan_in), BF16),
             jax.ShapeDtypeStruct((size, 256), BF16),
         ),
-        in_specs=[VMEM] * 5,
+        in_specs=[VMEM] * 7,
         out_specs=(VMEM, VMEM),
         scratch_shapes=[
             pltpu.VMEM(((2 * rows + 40) * (2 * cols + 48), 128), F32),
@@ -752,8 +731,16 @@
         ],
         compiler_params=pltpu.CompilerParams(vmem_limit_bytes=40 * 2**20),
         cost_estimate=pl.CostEstimate(flops=0, bytes_accessed=12 * 2**20, transcendentals=0),
-    )(inputs, split_cot, side, south, north)
-
+    )(inputs, cotangent, side, south, north, lower, upper)
+
+    planes[1:], padded, cot = lax.optimization_barrier((planes[1:], padded, cot))
+    planes, parts = shared_out(devices, planes)
+    if whole:
+        chunks = jnp.stack(planes).reshape(devices.count, -1)
+        chunks = jnp.take(chunks, jnp.argsort(order(devices, -1)), axis=0)
+        pieces = jnp.split(chunks, (held[0], held[0] + held[1]), axis=1)
+        chunks = jnp.concatenate([piece.reshape(-1) for piece in pieces])
+        planes, parts = [chunks.reshape(1, -1, 128)], [(0, 0, 0)]
     deep = -(-(2 * held[1]) // 2048) * 16, -(-held[0] // 2048) * 16
     if whole:
         deep = 2 * held[1] * devices.count // 128, held[0] * devices.count // 128
@@ -814,20 +801,19 @@
     )
     features = done["features"]
 
-    def reduced(terms, places, *sizes):
+    def reduced(terms, *sizes):
         if whole:
             cuts = [sum(sizes[:i]) * devices.count for i in range(1, len(sizes))]
             pieces = jnp.split(terms.reshape(-1), cuts)
             terms = [piece.reshape(devices.count, -1) for piece in pieces]
-            terms = jnp.take(jnp.concatenate(terms, axis=1), places, axis=0)
+            terms = jnp.take(jnp.concatenate(terms, axis=1), order(devices, 1), axis=0)
             terms = terms.reshape(core, devices.count // core, 1, -1)
         return halved(devices, terms)
 
-    upper = reduced(done["terms"], order(devices, 1), held[1], held[2])
+    upper = reduced(done["terms"], held[1], held[2])
     upper, win_delta = lax.optimization_barrier((upper, done["win_delta"]))
     done["win_delta"] = win_delta
-    upper = passed(devices, upper).reshape(-1)
-    grad_second, grad_third = upper[: held[1]], upper[held[1] : held[1] + held[2]]
+    upper = planar(devices, upper)
     done = call(
         True,
         {"x": padded, **{name: done[name] for name in ("win_delta", "t_one", "t_two")}},
@@ -840,8 +826,18 @@
             "image": ((4 * rows * cols, 128), F32),
         },
     )
-    lower = reduced(done["terms"], owners(devices), held[0])
-    grad_first = summed(lower, held[0])
+    upper, lower = lax.optimization_barrier((upper, reduced(done["terms"], held[0])))
+    lower = planar(devices, lower)
+    cut = upper.shape[-2] if not whole else 0
+    total = linear(devices, jnp.concatenate([upper, lower], axis=-1 if whole else -2))
+    if whole:
+        grad_second, grad_third, grad_first = jnp.split(
+            total.reshape(-1), (held[1], held[1] + held[2])
+        )
+    else:
+        grad_first = total[cut:].reshape(-1)[: held[0]]
+        total = total[:cut].reshape(-1)
+        grad_second, grad_third = total[: held[1]], total[held[1] : held[1] + held[2]]
     return (features, done["grad_input"], grad_first, grad_second, grad_third)
 
 

time: 95.7 us -> 90.9 us (0.950)
  starting transfers between devices: 33.3 us -> 40.4 us
  waiting for transfers between devices: 26.7 us -> 19.7 us
  Pallas kernels: 29.6 us -> 24.7 us
    all_to_all x1 -> x0, waiting for transfers between devices: 7.79 us -> none  [summed(): half = lax.all_to_all(half, ('chip', 'lon'), 0, 0, tiled=True)]
    ppermute x18 -> x21, starting transfers between devices: 23.2 us -> 30.5 us  [send(): return lax.ppermute(value, BOTH, pairs)]
    pallas_call x2, Pallas kernels: 26.8 us -> 21.9 us  [call(): pl.pallas_call(functools.partial(level, shape, devices, () if second else...]
    all_to_all x1 -> x0, starting transfers between devices: 4.45 us -> none  [summed(): half = lax.all_to_all(half, ('chip', 'lon'), 0, 0, tiled=True)]
    ppermute x2 -> x4, starting transfers between devices: 2.59 us -> 6.91 us  [lengthways(): return (lax.ppermute(south, LAT, down), lax.ppermute(north, LAT, up))]
    ppermute x18 -> x21, waiting for transfers between devices: 16.3 us -> 19.7 us  [send(): return lax.ppermute(value, BOTH, pairs)]
    ppermute x1, waiting for transfers between devices: 2.59 us -> 0.01 us  [sideways(): return lax.ppermute(packed, 'lon', east)]
    unnamed x12 -> x8, local copies, waits for them, and re-layouts: 2.28 us -> 2.27 us
  transfers between devices with their start and end apart: 22 -> 26, of which waited for: 7 -> 14; matrix products, arithmetic and copies ran while one was open for 2% -> 1% of each run, Pallas kernels for 9% -> 9%
where the time goes in v2:
time: 90.9 us; the launch traced here: 90.6 us
  starting transfers between devices  40.4 us (44%)
  Pallas kernels  24.7 us (27%)
  waiting for transfers between devices  19.7 us (22%)
  local copies, waits for them, and re-layouts  3.65 us (4%)
  other arithmetic  1.25 us (1%)
    ppermute x21, starting transfers between devices, send(): return lax.ppermute(value, BOTH, pairs)  30.5 us
    pallas_call x2, Pallas kernels, call(): pl.pallas_call(functools.partial(level, shape, devices, () if second else...  21.9 us
    ppermute x21, waiting for transfers between devices, send(): return lax.ppermute(value, BOTH, pairs)  19.7 us
    ppermute x4, starting transfers between devices, lengthways(): return (lax.ppermute(south, LAT, down), lax.ppermute(north, LAT, up))  6.91 us
    ppermute x1, starting transfers between devices, sideways(): return lax.ppermute(packed, 'lon', east)  3 us
    pallas_call x1, Pallas kernels, local(): pl.pallas_call(functools.partial(prepare, rows, cols), out_shape=(jax.Sha...  2.36 us
    unnamed x8, local copies, waits for them, and re-layouts  2.27 us
  transfers between devices with their start and end apart: 26, of which 14 were waited for; matrix products, arithmetic and copies ran while one was open for 1% of the time, Pallas kernels for 9%

profile of v2, /device:TPU:0, one launch (start us, length us, event | category | flops | bytes accessed | tf_op | source)
XLA Modules:
  0.0 90.6 jit_solution(3180355398000673658)
XLA Ops:
  3.4 3.0 %collective-permute-start.5 = (bf16[1536,128]{1,0:T(8,128)(2,1)S(1)}, bf16[1536,128]{1,0:T(8,128)(2,1)S(1)}, u32[]{:S(2)}, u32[]{:S(2)}) collective-permute-start(bf16[1536,128]{1,0:T(8,128)(2,1)S(1)} %get-tuple-element.34), channel_id=1, source_target_pairs={{0,1},{1,0},{2,3},{3,2},{4,5},{5,4},{6,7},{7,6},{8,9},{9,8},{10,11... | collective-permute-start | bytes 1179656 | tf_op jit(solution)/shard_map/ppermute | solution.py:200
  7.1 2.7 %collective-permute-start.1 = (bf16[224,128]{1,0:T(8,128)(2,1)S(1)}, bf16[224,128]{1,0:T(8,128)(2,1)S(1)}, u32[]{:S(2)}, u32[]{:S(2)}) collective-permute-start(bf16[224,128]{1,0:T(8,128)(2,1)S(1)} %get-tuple-element.71), channel_id=1, source_target_pairs={{0,16},{1,17},{2,18},{3,19},{4,20},{5,21},{6,22},{7,23},{8,24},{9,... | collective-permute-start | bytes 172040 | tf_op jit(solution)/shard_map/ppermute | solution.py:65
  11.1 3.0 %collective-permute-start.3 = (bf16[704,128]{1,0:T(8,128)(2,1)S(1)}, bf16[704,128]{1,0:T(8,128)(2,1)S(1)}, u32[]{:S(2)}, u32[]{:S(2)}) collective-permute-start(bf16[704,128]{1,0:T(8,128)(2,1)S(1)} %get-tuple-element.32), channel_id=1, source_target_pairs={{0,2},{2,4},{4,6},{6,8},{8,10},{10,12},{12,14},{14,16},{16,18},{18... | collective-permute-start | bytes 540680 | tf_op jit(solution)/shard_map/ppermute | solution.py:210
  14.1 1.6 %collective-permute-start = (bf16[224,128]{1,0:T(8,128)(2,1)S(1)}, bf16[224,128]{1,0:T(8,128)(2,1)S(1)}, u32[]{:S(2)}, u32[]{:S(2)}) collective-permute-start(bf16[224,128]{1,0:T(8,128)(2,1)S(1)} %get-tuple-element.71), channel_id=1, source_target_pairs={{0,8},{1,9},{2,10},{3,11},{4,12},{5,13},{6,14},{7,15},{8,0},{9,1},... | collective-permute-start | bytes 172040 | tf_op jit(solution)/shard_map/ppermute | solution.py:65
  15.8 2.3 %collective-permute-start.2 = (bf16[224,128]{1,0:T(8,128)(2,1)S(1)}, bf16[224,128]{1,0:T(8,128)(2,1)S(1)}, u32[]{:S(2)}, u32[]{:S(2)}) collective-permute-start(bf16[224,128]{1,0:T(8,128)(2,1)S(1)} %get-tuple-element.71), channel_id=1, source_target_pairs={{0,24},{1,25},{2,26},{3,27},{4,28},{5,29},{6,30},{7,31},{8,16},{9,... | collective-permute-start | bytes 172040 | tf_op jit(solution)/shard_map/ppermute | solution.py:65
  18.8 3.4 %collective-permute-done.2 = bf16[224,128]{1,0:T(8,128)(2,1)S(1)} collective-permute-done((bf16[224,128]{1,0:T(8,128)(2,1)S(1)}, bf16[224,128]{1,0:T(8,128)(2,1)S(1)}, u32[]{:S(2)}, u32[]{:S(2)}) %collective-permute-start.2) | collective-permute-done | bytes 57376 | tf_op jit(solution)/shard_map/ppermute | solution.py:65
  22.3 1.5 %collective-permute-start.8 = (bf16[4,224,128]{2,1,0:T(8,128)(2,1)S(1)}, bf16[4,224,128]{2,1,0:T(8,128)(2,1)S(1)}, u32[]{:S(2)}, u32[]{:S(2)}) collective-permute-start(bf16[4,224,128]{2,1,0:T(8,128)(2,1)S(1)} %pad_maximum_fusion.refs_2_), channel_id=1, source_target_pairs={{0,5},{1,4},{2,7},{3,6},{4,1},{5,0},{6,3},{7,2},{8,13},{9,12},{10,... | collective-permute-start | bytes 688136 | tf_op jit(solution)/shard_map/ppermute | solution.py:65
  24.4 1.5 %collective-permute-start.6 = (bf16[4,224,128]{2,1,0:T(8,128)(2,1)S(1)}, bf16[4,224,128]{2,1,0:T(8,128)(2,1)S(1)}, u32[]{:S(2)}, u32[]{:S(2)}) collective-permute-start(bf16[4,224,128]{2,1,0:T(8,128)(2,1)S(1)} %pad_maximum_fusion.refs_2_), channel_id=1, source_target_pairs={{0,1},{1,0},{2,3},{3,2},{4,5},{5,4},{6,7},{7,6},{8,9},{9,8},{10,11... | collective-permute-start | bytes 688136 | tf_op jit(solution)/shard_map/ppermute | solution.py:65
  28.5 8.2 %collective-permute-start.11 = (bf16[4,224,128]{2,1,0:T(8,128)(2,1)S(1)}, bf16[4,224,128]{2,1,0:T(8,128)(2,1)S(1)}, u32[]{:S(2)}, u32[]{:S(2)}) collective-permute-start(bf16[4,224,128]{2,1,0:T(8,128)(2,1)S(1)} %pad_maximum_fusion.refs_2_), channel_id=1, source_target_pairs={{0,2},{1,3},{2,0},{3,1},{4,6},{5,7},{6,4},{7,5},{8,10},{9,11},{10,... | collective-permute-start | bytes 688136 | tf_op jit(solution)/shard_map/ppermute | solution.py:65
  36.7 2.4 %shard_map.94 = (bf16[2112,768]{1,0:T(8,128)(2,1)S(1)}, bf16[2112,256]{1,0:T(8,128)(2,1)S(1)}) custom-call(bf16[64,64,128]{2,1,0:T(8,128)(2,1)S(1)} %copy-done.1, bf16[32,32,192]{2,1,0:T(8,128)(2,1)S(1)} %copy-done.3, bf16[1536,128]{1,0:T(8,128)(2,1)S(1)} %collective-permute-done.5.side_ref, bf16[704,128]{1,0:T(8,128)(2,1)S(1)} %collective-permute-done.3.south_ref, ...), custom_call_target="tpu_custom_call" | custom-call | bytes 12582912 | tf_op jit(solution)/shard_map/pallas_call | solution.py:720
  41.3 16.4 %shard_map.95 = (bf16[32,32,192]{2,1,0:T(8,128)(2,1)}, bf16[2,16,176,128]{3,2,1,0:T(8,128)(2,1)S(1)}, bf16[2112,640]{1,0:T(8,128)(2,1)S(1)}, bf16[512,768]{1,0:T(8,128)(2,1)S(1)}, bf16[256,1792]{1,0:T(8,128)(2,1)S(1)}) custom-call(bf16[2112,768]{1,0:T(8,128)(2,1)S(1)} %get-tuple-element.43.refs_0_, bf16[2112,256]{1,0:T(8,128)(2,1)S(1)} %get-tuple-element.44.refs_1_, ...), custom_call_target="tpu_custom_call" | custom-call | flops 5000000000 | bytes 12582912 | tf_op jit(solution)/shard_map/pallas_call | solution.py:762
  58.1 2.0 %collective-permute-done.15 = bf16[16,176,128]{2,1,0:T(8,128)(2,1)S(1)} collective-permute-done((bf16[16,176,128]{2,1,0:T(8,128)(2,1)S(1)}, bf16[16,176,128]{2,1,0:T(8,128)(2,1)S(1)}, u32[]{:S(2)}, u32[]{:S(2)}) %collective-permute-start.15) | collective-permute-done | bytes 720928 | tf_op jit(solution)/shard_map/ppermute | solution.py:65
  60.3 1.4 %collective-permute-start.16 = (bf16[4,176,128]{2,1,0:T(8,128)(2,1)S(1)}, bf16[4,176,128]{2,1,0:T(8,128)(2,1)S(1)}, u32[]{:S(2)}, u32[]{:S(2)}) collective-permute-start(bf16[4,176,128]{2,1,0:T(8,128)(2,1)S(1)} %get-tuple-element.59), channel_id=1, source_target_pairs={{0,1},{1,0},{2,3},{3,2},{4,5},{5,4},{6,7},{7,6},{8,9},{9,8},{10,11... | collective-permute-start | bytes 540680 | tf_op jit(solution)/shard_map/ppermute | solution.py:65
  61.7 2.7 %collective-permute-start.18 = (bf16[4,176,128]{2,1,0:T(8,128)(2,1)S(1)}, bf16[4,176,128]{2,1,0:T(8,128)(2,1)S(1)}, u32[]{:S(2)}, u32[]{:S(2)}) collective-permute-start(bf16[4,176,128]{2,1,0:T(8,128)(2,1)S(1)} %get-tuple-element.60), channel_id=1, source_target_pairs={{0,5},{1,4},{2,7},{3,6},{4,1},{5,0},{6,3},{7,2},{8,13},{9,12},{10,... | collective-permute-start | bytes 540680 | tf_op jit(solution)/shard_map/ppermute | solution.py:65
  64.4 5.5 %shard_map.96 = (bf16[64,64,128]{2,1,0:T(8,128)(2,1)}, bf16[2,16,64,128]{3,2,1,0:T(8,128)(2,1)S(1)}) custom-call(bf16[2112,768]{1,0:T(8,128)(2,1)S(1)} %get-tuple-element.43.refs_0_, bf16[2112,640]{1,0:T(8,128)(2,1)S(1)} %get-tuple-element.51.refs_1_, bf16[512,768]{1,0:T(8,128)(2,1)S(1)} %get-tuple-element.52.refs_2_, ...), custom_call_target="tpu_custom_call" | custom-call | flops 2000000000 | bytes 12582912 | tf_op jit(solution)/shard_map/pallas_call | solution.py:762
  69.9 3.2 %collective-permute-done.18 = bf16[4,176,128]{2,1,0:T(8,128)(2,1)S(1)} collective-permute-done((bf16[4,176,128]{2,1,0:T(8,128)(2,1)S(1)}, bf16[4,176,128]{2,1,0:T(8,128)(2,1)S(1)}, u32[]{:S(2)}, u32[]{:S(2)}) %collective-permute-start.18) | collective-permute-done | bytes 180256 | tf_op jit(solution)/shard_map/ppermute | solution.py:65
  73.1 1.4 %collective-permute-done.17 = bf16[4,176,128]{2,1,0:T(8,128)(2,1)S(1)} collective-permute-done((bf16[4,176,128]{2,1,0:T(8,128)(2,1)S(1)}, bf16[4,176,128]{2,1,0:T(8,128)(2,1)S(1)}, u32[]{:S(2)}, u32[]{:S(2)}) %collective-permute-start.17) | collective-permute-done | bytes 180256 | tf_op jit(solution)/shard_map/ppermute | solution.py:65
  74.7 1.4 %collective-permute-start.20 = (bf16[4,64,128]{2,1,0:T(8,128)(2,1)S(1)}, bf16[4,64,128]{2,1,0:T(8,128)(2,1)S(1)}, u32[]{:S(2)}, u32[]{:S(2)}) collective-permute-start(bf16[4,64,128]{2,1,0:T(8,128)(2,1)S(1)} %get-tuple-element.62), channel_id=1, source_target_pairs={{0,1},{1,0},{2,3},{3,2},{4,5},{5,4},{6,7},{7,6},{8,9},{9,8},{10,11... | collective-permute-start | bytes 196616 | tf_op jit(solution)/shard_map/ppermute | solution.py:65
  76.5 1.7 %collective-permute-start.21 = (bf16[4,64,128]{2,1,0:T(8,128)(2,1)S(1)}, bf16[4,64,128]{2,1,0:T(8,128)(2,1)S(1)}, u32[]{:S(2)}, u32[]{:S(2)}) collective-permute-start(bf16[4,64,128]{2,1,0:T(8,128)(2,1)S(1)} %get-tuple-element.64), channel_id=1, source_target_pairs={{0,4},{1,5},{2,6},{3,7},{4,0},{5,1},{6,2},{7,3},{8,12},{9,13},{10,... | collective-permute-start | bytes 196616 | tf_op jit(solution)/shard_map/ppermute | solution.py:65
  79.0 2.3 %collective-permute-done.22 = bf16[4,64,128]{2,1,0:T(8,128)(2,1)S(1)} collective-permute-done((bf16[4,64,128]{2,1,0:T(8,128)(2,1)S(1)}, bf16[4,64,128]{2,1,0:T(8,128)(2,1)S(1)}, u32[]{:S(2)}, u32[]{:S(2)}) %collective-permute-start.22) | collective-permute-done | bytes 65568 | tf_op jit(solution)/shard_map/ppermute | solution.py:65
  81.6 1.9 %collective-permute-start.25 = (bf16[240,128]{1,0:T(8,128)(2,1)S(1)}, bf16[240,128]{1,0:T(8,128)(2,1)S(1)}, u32[]{:S(2)}, u32[]{:S(2)}) collective-permute-start(bf16[240,128]{1,0:T(8,128)(2,1)S(1)} %get-tuple-element.66), channel_id=1, source_target_pairs={{0,24},{1,25},{2,26},{3,27},{4,28},{5,29},{6,30},{7,31},{8,16},{9,... | collective-permute-start | bytes 184328 | tf_op jit(solution)/shard_map/ppermute | solution.py:65
  83.5 1.6 %collective-permute-start.24 = (bf16[240,128]{1,0:T(8,128)(2,1)S(1)}, bf16[240,128]{1,0:T(8,128)(2,1)S(1)}, u32[]{:S(2)}, u32[]{:S(2)}) collective-permute-start(bf16[240,128]{1,0:T(8,128)(2,1)S(1)} %get-tuple-element.67), channel_id=1, source_target_pairs={{0,16},{1,17},{2,18},{3,19},{4,20},{5,21},{6,22},{7,23},{8,24},{9,... | collective-permute-start | bytes 184328 | tf_op jit(solution)/shard_map/ppermute | solution.py:65
  86.4 1.4 %collective-permute-done.25 = bf16[240,128]{1,0:T(8,128)(2,1)S(1)} collective-permute-done((bf16[240,128]{1,0:T(8,128)(2,1)S(1)}, bf16[240,128]{1,0:T(8,128)(2,1)S(1)}, u32[]{:S(2)}, u32[]{:S(2)}) %collective-permute-start.25) | collective-permute-done | bytes 61472 | tf_op jit(solution)/shard_map/ppermute | solution.py:65
  87.8 1.5 %collective-permute-done.24 = bf16[240,128]{1,0:T(8,128)(2,1)S(1)} collective-permute-done((bf16[240,128]{1,0:T(8,128)(2,1)S(1)}, bf16[240,128]{1,0:T(8,128)(2,1)S(1)}, u32[]{:S(2)}, u32[]{:S(2)}) %collective-permute-start.24) | collective-permute-done | bytes 61472 | tf_op jit(solution)/shard_map/ppermute | solution.py:65
  (56 shorter events, 15.9 us)
Async XLA Ops:
  3.4 19.0 %collective-permute-start.5 = (bf16[1536,128]{1,0:T(8,128)(2,1)S(1)}, bf16[1536,128]{1,0:T(8,128)(2,1)S(1)}, u32[]{:S(2)}, u32[]{:S(2)}) collective-permute-start(bf16[1536,128]{1,0:T(8,128)(2,1)S(1)} %get-tuple-element.34), channel_id=1, source_target_pairs={{0,1},{1,0},{2,3},{3,2},{4,5},{5,4},{6,7},{7,6},{8,9},{9,8},{10,11... | collective-permute-start | bytes 1179656 | tf_op jit(solution)/shard_map/ppermute | solution.py:200
  7.1 8.6 %collective-permute-start.1 = (bf16[224,128]{1,0:T(8,128)(2,1)S(1)}, bf16[224,128]{1,0:T(8,128)(2,1)S(1)}, u32[]{:S(2)}, u32[]{:S(2)}) collective-permute-start(bf16[224,128]{1,0:T(8,128)(2,1)S(1)} %get-tuple-element.71), channel_id=1, source_target_pairs={{0,16},{1,17},{2,18},{3,19},{4,20},{5,21},{6,22},{7,23},{8,24},{9,... | collective-permute-start | bytes 172040 | tf_op jit(solution)/shard_map/ppermute | solution.py:65
  9.8 12.5 %collective-permute-start.4 = (bf16[832,128]{1,0:T(8,128)(2,1)S(1)}, bf16[832,128]{1,0:T(8,128)(2,1)S(1)}, u32[]{:S(2)}, u32[]{:S(2)}) collective-permute-start(bf16[832,128]{1,0:T(8,128)(2,1)S(1)} %get-tuple-element.33), channel_id=1, source_target_pairs={{2,0},{4,2},{6,4},{8,6},{10,8},{12,10},{14,12},{16,14},{18,16},{20... | collective-permute-start | bytes 638984 | tf_op jit(solution)/shard_map/ppermute | solution.py:210
  11.1 11.2 %collective-permute-start.3 = (bf16[704,128]{1,0:T(8,128)(2,1)S(1)}, bf16[704,128]{1,0:T(8,128)(2,1)S(1)}, u32[]{:S(2)}, u32[]{:S(2)}) collective-permute-start(bf16[704,128]{1,0:T(8,128)(2,1)S(1)} %get-tuple-element.32), channel_id=1, source_target_pairs={{0,2},{2,4},{4,6},{6,8},{8,10},{10,12},{12,14},{14,16},{16,18},{18... | collective-permute-start | bytes 540680 | tf_op jit(solution)/shard_map/ppermute | solution.py:210
  14.1 4.7 %collective-permute-start = (bf16[224,128]{1,0:T(8,128)(2,1)S(1)}, bf16[224,128]{1,0:T(8,128)(2,1)S(1)}, u32[]{:S(2)}, u32[]{:S(2)}) collective-permute-start(bf16[224,128]{1,0:T(8,128)(2,1)S(1)} %get-tuple-element.71), channel_id=1, source_target_pairs={{0,8},{1,9},{2,10},{3,11},{4,12},{5,13},{6,14},{7,15},{8,0},{9,1},... | collective-permute-start | bytes 172040 | tf_op jit(solution)/shard_map/ppermute | solution.py:65
  15.8 6.5 %collective-permute-start.2 = (bf16[224,128]{1,0:T(8,128)(2,1)S(1)}, bf16[224,128]{1,0:T(8,128)(2,1)S(1)}, u32[]{:S(2)}, u32[]{:S(2)}) collective-permute-start(bf16[224,128]{1,0:T(8,128)(2,1)S(1)} %get-tuple-element.71), channel_id=1, source_target_pairs={{0,24},{1,25},{2,26},{3,27},{4,28},{5,29},{6,30},{7,31},{8,16},{9,... | collective-permute-start | bytes 172040 | tf_op jit(solution)/shard_map/ppermute | solution.py:65
  22.3 16.8 %collective-permute-start.8 = (bf16[4,224,128]{2,1,0:T(8,128)(2,1)S(1)}, bf16[4,224,128]{2,1,0:T(8,128)(2,1)S(1)}, u32[]{:S(2)}, u32[]{:S(2)}) collective-permute-start(bf16[4,224,128]{2,1,0:T(8,128)(2,1)S(1)} %pad_maximum_fusion.refs_2_), channel_id=1, source_target_pairs={{0,5},{1,4},{2,7},{3,6},{4,1},{5,0},{6,3},{7,2},{8,13},{9,12},{10,... | collective-permute-start | bytes 688136 | tf_op jit(solution)/shard_map/ppermute | solution.py:65
  23.8 15.3 %collective-permute-start.7 = (bf16[4,224,128]{2,1,0:T(8,128)(2,1)S(1)}, bf16[4,224,128]{2,1,0:T(8,128)(2,1)S(1)}, u32[]{:S(2)}, u32[]{:S(2)}) collective-permute-start(bf16[4,224,128]{2,1,0:T(8,128)(2,1)S(1)} %pad_maximum_fusion.refs_2_), channel_id=1, source_target_pairs={{0,4},{1,5},{2,6},{3,7},{4,0},{5,1},{6,2},{7,3},{8,12},{9,13},{10,... | collective-permute-start | bytes 688136 | tf_op jit(solution)/shard_map/ppermute | solution.py:65
  24.4 14.7 %collective-permute-start.6 = (bf16[4,224,128]{2,1,0:T(8,128)(2,1)S(1)}, bf16[4,224,128]{2,1,0:T(8,128)(2,1)S(1)}, u32[]{:S(2)}, u32[]{:S(2)}) collective-permute-start(bf16[4,224,128]{2,1,0:T(8,128)(2,1)S(1)} %pad_maximum_fusion.refs_2_), channel_id=1, source_target_pairs={{0,1},{1,0},{2,3},{3,2},{4,5},{5,4},{6,7},{7,6},{8,9},{9,8},{10,11... | collective-permute-start | bytes 688136 | tf_op jit(solution)/shard_map/ppermute | solution.py:65
  25.9 2.6 %collective-permute-start.9 = (bf16[464,128]{1,0:T(8,128)(2,1)S(1)}, bf16[464,128]{1,0:T(8,128)(2,1)S(1)}, u32[]{:S(2)}, u32[]{:S(2)}) collective-permute-start(bf16[464,128]{1,0:T(8,128)(2,1)S(1)} %get-tuple-element.39), channel_id=1, source_target_pairs={{0,2},{2,4},{4,6},{6,8},{8,10},{10,12},{12,14},{14,16},{16,18},{18... | collective-permute-start | bytes 356360 | tf_op jit(solution)/shard_map/ppermute | solution.py:210
  27.2 9.5 %collective-permute-start.10 = (bf16[464,128]{1,0:T(8,128)(2,1)S(1)}, bf16[464,128]{1,0:T(8,128)(2,1)S(1)}, u32[]{:S(2)}, u32[]{:S(2)}) collective-permute-start(bf16[464,128]{1,0:T(8,128)(2,1)S(1)} %get-tuple-element.40), channel_id=1, source_target_pairs={{2,0},{4,2},{6,4},{8,6},{10,8},{12,10},{14,12},{16,14},{18,16},{20... | collective-permute-start | bytes 356360 | tf_op jit(solution)/shard_map/ppermute | solution.py:210
  28.5 11.3 %collective-permute-start.11 = (bf16[4,224,128]{2,1,0:T(8,128)(2,1)S(1)}, bf16[4,224,128]{2,1,0:T(8,128)(2,1)S(1)}, u32[]{:S(2)}, u32[]{:S(2)}) collective-permute-start(bf16[4,224,128]{2,1,0:T(8,128)(2,1)S(1)} %pad_maximum_fusion.refs_2_), channel_id=1, source_target_pairs={{0,2},{1,3},{2,0},{3,1},{4,6},{5,7},{6,4},{7,5},{8,10},{9,11},{10,... | collective-permute-start | bytes 688136 | tf_op jit(solution)/shard_map/ppermute | solution.py:65
  39.3 1.7 %collective-permute-start.13 = (bf16[4,224,128]{2,1,0:T(8,128)(2,1)S(1)}, bf16[4,224,128]{2,1,0:T(8,128)(2,1)S(1)}, u32[]{:S(2)}, u32[]{:S(2)}) collective-permute-start(bf16[4,224,128]{2,1,0:T(8,128)(2,1)S(1)} %collective-permute-done.7.refs_4_), channel_id=1, source_target_pairs={{0,2},{1,3},{2,0},{3,1},{4,6},{5,7},{6,4},{7,5},{8,10},{9,11},{10,... | collective-permute-start | bytes 688136 | tf_op jit(solution)/shard_map/ppermute | solution.py:65
  57.8 2.3 %collective-permute-start.15 = (bf16[16,176,128]{2,1,0:T(8,128)(2,1)S(1)}, bf16[16,176,128]{2,1,0:T(8,128)(2,1)S(1)}, u32[]{:S(2)}, u32[]{:S(2)}) collective-permute-start(bf16[16,176,128]{2,1,0:T(8,128)(2,1)S(1)} %slice_bitcast_fusion), channel_id=1, source_target_pairs={{0,2},{1,3},{2,0},{3,1},{4,6},{5,7},{6,4},{7,5},{8,10},{9,11},{10,... | collective-permute-start | bytes 2162696 | tf_op jit(solution)/shard_map/ppermute | solution.py:65
  60.3 9.6 %collective-permute-start.16 = (bf16[4,176,128]{2,1,0:T(8,128)(2,1)S(1)}, bf16[4,176,128]{2,1,0:T(8,128)(2,1)S(1)}, u32[]{:S(2)}, u32[]{:S(2)}) collective-permute-start(bf16[4,176,128]{2,1,0:T(8,128)(2,1)S(1)} %get-tuple-element.59), channel_id=1, source_target_pairs={{0,1},{1,0},{2,3},{3,2},{4,5},{5,4},{6,7},{7,6},{8,9},{9,8},{10,11... | collective-permute-start | bytes 540680 | tf_op jit(solution)/shard_map/ppermute | solution.py:65
  61.7 11.4 %collective-permute-start.18 = (bf16[4,176,128]{2,1,0:T(8,128)(2,1)S(1)}, bf16[4,176,128]{2,1,0:T(8,128)(2,1)S(1)}, u32[]{:S(2)}, u32[]{:S(2)}) collective-permute-start(bf16[4,176,128]{2,1,0:T(8,128)(2,1)S(1)} %get-tuple-element.60), channel_id=1, source_target_pairs={{0,5},{1,4},{2,7},{3,6},{4,1},{5,0},{6,3},{7,2},{8,13},{9,12},{10,... | collective-permute-start | bytes 540680 | tf_op jit(solution)/shard_map/ppermute | solution.py:65
  64.4 10.1 %collective-permute-start.17 = (bf16[4,176,128]{2,1,0:T(8,128)(2,1)S(1)}, bf16[4,176,128]{2,1,0:T(8,128)(2,1)S(1)}, u32[]{:S(2)}, u32[]{:S(2)}) collective-permute-start(bf16[4,176,128]{2,1,0:T(8,128)(2,1)S(1)} %get-tuple-element.61), channel_id=1, source_target_pairs={{0,4},{1,5},{2,6},{3,7},{4,0},{5,1},{6,2},{7,3},{8,12},{9,13},{10,... | collective-permute-start | bytes 540680 | tf_op jit(solution)/shard_map/ppermute | solution.py:65
  69.9 4.7 %collective-permute-start.19 = (bf16[16,64,128]{2,1,0:T(8,128)(2,1)S(1)}, bf16[16,64,128]{2,1,0:T(8,128)(2,1)S(1)}, u32[]{:S(2)}, u32[]{:S(2)}) collective-permute-start(bf16[16,64,128]{2,1,0:T(8,128)(2,1)S(1)} %slice_bitcast_fusion.1), channel_id=1, source_target_pairs={{0,2},{1,3},{2,0},{3,1},{4,6},{5,7},{6,4},{7,5},{8,10},{9,11},{10,... | collective-permute-start | bytes 786440 | tf_op jit(solution)/shard_map/ppermute | solution.py:65
  74.7 4.3 %collective-permute-start.20 = (bf16[4,64,128]{2,1,0:T(8,128)(2,1)S(1)}, bf16[4,64,128]{2,1,0:T(8,128)(2,1)S(1)}, u32[]{:S(2)}, u32[]{:S(2)}) collective-permute-start(bf16[4,64,128]{2,1,0:T(8,128)(2,1)S(1)} %get-tuple-element.62), channel_id=1, source_target_pairs={{0,1},{1,0},{2,3},{3,2},{4,5},{5,4},{6,7},{7,6},{8,9},{9,8},{10,11... | collective-permute-start | bytes 196616 | tf_op jit(solution)/shard_map/ppermute | solution.py:65
  76.1 5.3 %collective-permute-start.22 = (bf16[4,64,128]{2,1,0:T(8,128)(2,1)S(1)}, bf16[4,64,128]{2,1,0:T(8,128)(2,1)S(1)}, u32[]{:S(2)}, u32[]{:S(2)}) collective-permute-start(bf16[4,64,128]{2,1,0:T(8,128)(2,1)S(1)} %get-tuple-element.63), channel_id=1, source_target_pairs={{0,5},{1,4},{2,7},{3,6},{4,1},{5,0},{6,3},{7,2},{8,13},{9,12},{10,... | collective-permute-start | bytes 196616 | tf_op jit(solution)/shard_map/ppermute | solution.py:65
  76.5 5.0 %collective-permute-start.21 = (bf16[4,64,128]{2,1,0:T(8,128)(2,1)S(1)}, bf16[4,64,128]{2,1,0:T(8,128)(2,1)S(1)}, u32[]{:S(2)}, u32[]{:S(2)}) collective-permute-start(bf16[4,64,128]{2,1,0:T(8,128)(2,1)S(1)} %get-tuple-element.64), channel_id=1, source_target_pairs={{0,4},{1,5},{2,6},{3,7},{4,0},{5,1},{6,2},{7,3},{8,12},{9,13},{10,... | collective-permute-start | bytes 196616 | tf_op jit(solution)/shard_map/ppermute | solution.py:65
  81.5 4.9 %collective-permute-start.23 = (bf16[240,128]{1,0:T(8,128)(2,1)S(1)}, bf16[240,128]{1,0:T(8,128)(2,1)S(1)}, u32[]{:S(2)}, u32[]{:S(2)}) collective-permute-start(bf16[240,128]{1,0:T(8,128)(2,1)S(1)} %get-tuple-element.65), channel_id=1, source_target_pairs={{0,8},{1,9},{2,10},{3,11},{4,12},{5,13},{6,14},{7,15},{8,0},{9,1},... | collective-permute-start | bytes 184328 | tf_op jit(solution)/shard_map/ppermute | solution.py:65
  81.6 6.2 %collective-permute-start.25 = (bf16[240,128]{1,0:T(8,128)(2,1)S(1)}, bf16[240,128]{1,0:T(8,128)(2,1)S(1)}, u32[]{:S(2)}, u32[]{:S(2)}) collective-permute-start(bf16[240,128]{1,0:T(8,128)(2,1)S(1)} %get-tuple-element.66), channel_id=1, source_target_pairs={{0,24},{1,25},{2,26},{3,27},{4,28},{5,29},{6,30},{7,31},{8,16},{9,... | collective-permute-start | bytes 184328 | tf_op jit(solution)/shard_map/ppermute | solution.py:65
  83.5 5.8 %collective-permute-start.24 = (bf16[240,128]{1,0:T(8,128)(2,1)S(1)}, bf16[240,128]{1,0:T(8,128)(2,1)S(1)}, u32[]{:S(2)}, u32[]{:S(2)}) collective-permute-start(bf16[240,128]{1,0:T(8,128)(2,1)S(1)} %get-tuple-element.67), channel_id=1, source_target_pairs={{0,16},{1,17},{2,18},{3,19},{4,20},{5,21},{6,22},{7,23},{8,24},{9,... | collective-permute-start | bytes 184328 | tf_op jit(solution)/shard_map/ppermute | solution.py:65
  (6 other events, 73.1 us)

commit v3 on v2

--- a/solution.py
+++ b/solution.py
@@ -130,7 +130,7 @@
 
 def linear(devices, line):
     far = devices.sizes[0]
-    return total_of([line[0]] + [devices.send(line[f], (f, 0, 0, 0)) for f in range(1, far)])
+    return [line[0]] + [devices.send(line[f], (f, 0, 0, 0)) for f in range(1, far)]
 
 
 WEST, EAST = 9, 10
@@ -311,12 +311,38 @@
         cot_ref[:, 128 * part : 128 * part + 128] = cots[GUARD : GUARD + size, :].astype(BF16)
 
 
+def unfold(sections, count, *refs):
+    terms, outs = refs[:count], refs[count : count + len(sections)]
+    total, k_a, k_b = refs[count + len(sections) :]
+    value = terms[0][...].astype(F32)
+    for term in terms[1:]:
+        value = value + term[...].astype(F32)
+    total[...] = value
+    for (first, n), out in zip(sections, outs):
+        half = n // 3
+        low = low_lanes(half)
+        pair = total[first + 2 * half : first + n, :]
+        turned = swapped(pair)
+        k_a[0 : 2 * half, :] = total[first : first + 2 * half, :]
+        k_b[0:half, :] = jnp.where(low, pair, turned)
+        k_b[half : 2 * half, :] = jnp.where(low, turned, pair)
+        even_a = k_a[pl.ds(0, half, stride=2), :]
+        even_b = k_b[pl.ds(0, half, stride=2), :]
+        odd_a = swapped(k_a[pl.ds(1, half, stride=2), :])
+        odd_b = k_b[pl.ds(1, half, stride=2), :]
+        out[pl.ds(0, half, stride=3), :] = even_a
+        out[pl.ds(1, half, stride=3), :] = jnp.where(low, even_b, odd_a)
+        out[pl.ds(2, half, stride=3), :] = jnp.where(low, odd_a, odd_b)
+
+
 def level(shape, devices, parts, second, names, *refs):
     rows, cols, chan_in, mid, factor, whole = shape
     refs = dict(zip(names, refs))
     x_ref, terms_ref = refs["x"], refs["terms"]
     flat, k_a, k_b, f_a, f_b = (refs[name] for name in ("flat", "k_a", "k_b", "f_a", "f_b"))
-    win_delta, t_one, t_two = (refs[name] for name in ("win_delta", "t_one", "t_two"))
+    win_delta = refs["win_delta"]
+    if second:
+        t_one, t_two = refs["t_one"], refs["t_two"]
     pitch = cols + LEFT
     height = rows + ABOVE + BELOW
     size = height * pitch
@@ -325,8 +351,12 @@
     share = [9 * c * mid // 128 // count for c in (chan_in, mid, mid)]
     begin = [0, share[0], share[0] + share[1]]
     lat_at, mine = devices.place()
-    f_a[...] = jnp.zeros_like(f_a)
-    f_b[...] = jnp.zeros_like(f_b)
+
+    def clear():
+        head, tail = GUARD + pitch, GUARD + (ABOVE + rows + 5) * pitch
+        for field in (f_a, f_b):
+            field[0:head, :] = jnp.zeros((head, 128), F32)
+            field[tail:, :] = jnp.zeros((field.shape[0] - tail, 128), F32)
 
     def unpack(which, channels):
         n = share[which]
@@ -393,6 +423,14 @@
         unpack(0, chan_in)
         refs["w_one"][:, 0:128] = k_a[0 : 9 * chan_in, :].astype(BF16)
         refs["w_one"][:, 128:256] = k_b[0 : 9 * chan_in, :].astype(BF16)
+        unpack(1, mid)
+        forward(refs["w_two"])
+        unpack(2, mid)
+        forward(refs["w_three"])
+        backward(refs["t_three"])
+
+    def load_turned():
+        unpack(0, chan_in)
         empty = jnp.zeros((chan_in, 128), F32)
         low_in = low_lanes(chan_in)
         phases = (
@@ -422,11 +460,7 @@
             for j, block in enumerate(blocks):
                 t_one[chan_in * i : chan_in * (i + 1), 128 * j : 128 * j + 128] = block.astype(BF16)
         unpack(1, mid)
-        forward(refs["w_two"])
         backward(t_two)
-        unpack(2, mid)
-        forward(refs["w_three"])
-        backward(refs["t_three"])
 
     first_row = lat_at * rows
     bottom = lax.axis_size("chip") * core * rows - first_row
@@ -446,7 +480,7 @@
         f_a[pl.ds(at, n), :] = left
         f_b[pl.ds(at, n), :] = right
 
-    def windows(target, top, under):
+    def windows(target, top, under, f_a=f_a, f_b=f_b):
         wide = -(-(under - top) * pitch // 6 // 16) * 16
 
         def one(i, _):
@@ -501,6 +535,16 @@
         return jnp.concatenate([left.T, right.T], axis=0).astype(BF16)
 
     def pack(which, channels, first=0):
+        if not whole:
+            n = share[which]
+            half = n // 3
+            low = low_lanes(half)
+            for k in range(count):
+                at = 2 * half * k
+                refs["chunk"][k, first : first + 2 * half, :] = k_a[at : at + 2 * half, :]
+                pair = jnp.where(low, k_b[at : at + half, :], k_b[at + half : at + 2 * half, :])
+                refs["chunk"][k, first + 2 * half : first + n, :] = pair
+            return
         step = 288
 
         def one(i, _):
@@ -558,7 +602,7 @@
         win_one, win_two, slope, spread, c_ref = (
             refs[name] for name in ("win_one", "win_two", "slope", "spread", "c")
         )
-        slope[...] = jnp.zeros_like(slope)
+        clear()
 
         def convolve_first():
             halo, steps = 4, 2
@@ -614,9 +658,11 @@
         convolve(win_delta, refs["t_three"], True, 1, 2, finish_delta)
         field_grad(1, win_one, 0)
         hand_over()
-        windows(win_delta, -1, rows + 3)
 
     def backward_pass():
+        load_turned()
+        windows(win_delta, -1, rows + 3, refs["d_a"], refs["d_b"])
+
         def finish_back(p, n, value):
             store(p, n, value[:, :128], value[:, 128:], True)
 
@@ -679,7 +725,7 @@
     far, near, core, lon = devices.sizes
     held = (w_first.shape[0], w_second.shape[0], w_third.shape[0])
     shard = jnp.concatenate([w_first, w_second, w_third]).reshape(-1, 128)
-    whole = any(n % 128 for n in held)
+    whole = any(n % 384 for n in held)
     if not whole:
         shard = jnp.pad(shard, ((0, -shard.shape[0] % 16), (0, 0)))
     count = 1 if whole else devices.count
@@ -757,10 +803,10 @@
     }
 
     def call(second, ins, outs, scratch):
-        scratch = {**scratch, **shared}
+        scratch = {**scratch, **{name: kind for name, kind in shared.items() if name not in outs}}
         names = list(ins) + list(outs) + list(scratch)
         results = pl.pallas_call(
-            functools.partial(level, shape, devices, () if second else parts, second, names),
+            functools.partial(level, shape, devices, parts, second, names),
             out_shape=[jax.ShapeDtypeStruct(*out) for out in outs.values()],
             in_specs=[VMEM] * len(ins),
             out_specs=[VMEM] * len(outs),
@@ -774,18 +820,16 @@
         )(*ins.values())
         return dict(zip(outs, results))
 
-    ins = {"x": padded, "c": cot}
-    for i, plane in enumerate(planes):
-        ins["plane", i] = plane
+    kernels = {("plane", i): plane for i, plane in enumerate(planes)}
+    ins = {"x": padded, "c": cot, **kernels}
     done = call(
         False,
         ins,
         {
             "features": ((rows, cols, mid), BF16),
             "terms": ((sides, count // sides, deep[0], 128), BF16),
-            "win_delta": ((size, 640), BF16),
-            "t_one": ((4 * chan_in, 768), BF16),
-            "t_two": ((256, wide), BF16),
+            "f_a": (field_shape, F32),
+            "f_b": (field_shape, F32),
         },
         {
             "chunk": ((count, deep[0], 128), F32),
@@ -797,6 +841,7 @@
             "spread": ((size, 256), F32),
             "win_one": ((size, 640), BF16),
             "win_two": ((size, 640), BF16),
+            "win_delta": ((size, 640), BF16),
         },
     )
     features = done["features"]
@@ -811,33 +856,49 @@
         return halved(devices, terms)
 
     upper = reduced(done["terms"], held[1], held[2])
-    upper, win_delta = lax.optimization_barrier((upper, done["win_delta"]))
-    done["win_delta"] = win_delta
+    upper, f_a, f_b = lax.optimization_barrier((upper, done["f_a"], done["f_b"]))
     upper = planar(devices, upper)
     done = call(
         True,
-        {"x": padded, **{name: done[name] for name in ("win_delta", "t_one", "t_two")}},
+        {"x": padded, "d_a": f_a, "d_b": f_b, **kernels},
         {
             "grad_input": ((2 * rows, 2 * cols, chan_in), BF16),
             "terms": ((sides, count // sides, deep[1], 128), BF16),
         },
         {
             "chunk": ((count, deep[1], 128), F32),
+            "t_one": ((4 * chan_in, 768), BF16),
+            "t_two": ((256, wide), BF16),
+            "win_delta": ((size, 640), BF16),
             "image": ((4 * rows * cols, 128), F32),
         },
     )
     upper, lower = lax.optimization_barrier((upper, reduced(done["terms"], held[0])))
     lower = planar(devices, lower)
-    cut = upper.shape[-2] if not whole else 0
-    total = linear(devices, jnp.concatenate([upper, lower], axis=-1 if whole else -2))
+    terms = linear(devices, jnp.concatenate([upper, lower], axis=-1 if whole else -2))
     if whole:
         grad_second, grad_third, grad_first = jnp.split(
-            total.reshape(-1), (held[1], held[1] + held[2])
+            total_of(terms).reshape(-1), (held[1], held[1] + held[2])
         )
     else:
-        grad_first = total[cut:].reshape(-1)[: held[0]]
-        total = total[:cut].reshape(-1)
-        grad_second, grad_third = total[: held[1]], total[held[1] : held[1] + held[2]]
+        depth = upper.shape[-2]
+        high = [n // 128 for n in (held[1], held[2], held[0])]
+        sections = ((0, high[0]), (high[0], high[1]), (depth, high[2]))
+        deepest = max(high)
+        totals = pl.pallas_call(
+            functools.partial(unfold, sections, len(terms)),
+            out_shape=[jax.ShapeDtypeStruct((n, 128), F32) for n in high],
+            in_specs=[VMEM] * len(terms),
+            out_specs=[VMEM] * 3,
+            scratch_shapes=[
+                pltpu.VMEM(terms[0].shape, F32),
+                pltpu.VMEM((deepest, 128), F32),
+                pltpu.VMEM((deepest, 128), F32),
+            ],
+            compiler_params=params,
+            cost_estimate=pl.CostEstimate(flops=0, bytes_accessed=2**19, transcendentals=0),
+        )(*terms)
+        grad_second, grad_third, grad_first = (total.reshape(-1) for total in totals)
     return (features, done["grad_input"], grad_first, grad_second, grad_third)
 
 

time: 90.9 us -> 88 us (0.968)
  waiting for transfers between devices: 19.7 us -> 17 us
  local copies, waits for them, and re-layouts: 3.65 us -> 2.39 us
    ppermute x21, waiting for transfers between devices: 19.7 us -> 17 us  [send(): return lax.ppermute(value, BOTH, pairs)]
    slice x2 -> x0, local copies, waits for them, and re-layouts: 1.25 us -> none  [the longest x1 0.64 us: local(): total[held[1]:held[1] + held[2]]]
    pallas_call x2 -> x3, Pallas kernels: 21.9 us -> 22.1 us  [the longest x2 21.3 us: call(): pl.pallas_call(functools.partial(level, shape, devices, parts, second, na...]
  transfers between devices with their start and end apart: 26 -> 26, of which waited for: 14 -> 13; matrix products, arithmetic and copies ran while one was open for 1% -> 1% of each run, Pallas kernels for 9% -> 10%
where the time goes in v3:
time: 88 us; the launch traced here: 87.7 us
  starting transfers between devices  41.3 us (47%)
  Pallas kernels  24.9 us (28%)
  waiting for transfers between devices  17 us (19%)
  local copies, waits for them, and re-layouts  2.39 us (3%)
  other arithmetic  1.22 us (1%)
    ppermute x21, starting transfers between devices, send(): return lax.ppermute(value, BOTH, pairs)  31.4 us
    pallas_call x2, Pallas kernels, call(): pl.pallas_call(functools.partial(level, shape, devices, parts, second, na...  21.3 us
    ppermute x21, waiting for transfers between devices, send(): return lax.ppermute(value, BOTH, pairs)  17 us
    ppermute x4, starting transfers between devices, lengthways(): return (lax.ppermute(south, LAT, down), lax.ppermute(north, LAT, up))  6.91 us
    ppermute x1, starting transfers between devices, sideways(): return lax.ppermute(packed, 'lon', east)  3 us
    pallas_call x1, Pallas kernels, local(): pl.pallas_call(functools.partial(prepare, rows, cols), out_shape=(jax.Sha...  2.36 us
    unnamed x8, local copies, waits for them, and re-layouts  2.27 us
  transfers between devices with their start and end apart: 26, of which 13 were waited for; matrix products, arithmetic and copies ran while one was open for 1% of the time, Pallas kernels for 10%

profile of v3, /device:TPU:0, one launch (start us, length us, event | category | flops | bytes accessed | tf_op | source)
XLA Modules:
  0.0 87.7 jit_solution(14759094067652294478)
XLA Ops:
  3.4 3.0 %collective-permute-start.5 = (bf16[1536,128]{1,0:T(8,128)(2,1)S(1)}, bf16[1536,128]{1,0:T(8,128)(2,1)S(1)}, u32[]{:S(2)}, u32[]{:S(2)}) collective-permute-start(bf16[1536,128]{1,0:T(8,128)(2,1)S(1)} %get-tuple-element.37), channel_id=1, source_target_pairs={{0,1},{1,0},{2,3},{3,2},{4,5},{5,4},{6,7},{7,6},{8,9},{9,8},{10,11... | collective-permute-start | bytes 1179656 | tf_op jit(solution)/shard_map/ppermute | solution.py:200
  7.1 2.7 %collective-permute-start.1 = (bf16[224,128]{1,0:T(8,128)(2,1)S(1)}, bf16[224,128]{1,0:T(8,128)(2,1)S(1)}, u32[]{:S(2)}, u32[]{:S(2)}) collective-permute-start(bf16[224,128]{1,0:T(8,128)(2,1)S(1)} %get-tuple-element.76), channel_id=1, source_target_pairs={{0,16},{1,17},{2,18},{3,19},{4,20},{5,21},{6,22},{7,23},{8,24},{9,... | collective-permute-start | bytes 172040 | tf_op jit(solution)/shard_map/ppermute | solution.py:65
  11.1 3.0 %collective-permute-start.3 = (bf16[704,128]{1,0:T(8,128)(2,1)S(1)}, bf16[704,128]{1,0:T(8,128)(2,1)S(1)}, u32[]{:S(2)}, u32[]{:S(2)}) collective-permute-start(bf16[704,128]{1,0:T(8,128)(2,1)S(1)} %get-tuple-element.35), channel_id=1, source_target_pairs={{0,2},{2,4},{4,6},{6,8},{8,10},{10,12},{12,14},{14,16},{16,18},{18... | collective-permute-start | bytes 540680 | tf_op jit(solution)/shard_map/ppermute | solution.py:210
  14.1 1.6 %collective-permute-start = (bf16[224,128]{1,0:T(8,128)(2,1)S(1)}, bf16[224,128]{1,0:T(8,128)(2,1)S(1)}, u32[]{:S(2)}, u32[]{:S(2)}) collective-permute-start(bf16[224,128]{1,0:T(8,128)(2,1)S(1)} %get-tuple-element.76), channel_id=1, source_target_pairs={{0,8},{1,9},{2,10},{3,11},{4,12},{5,13},{6,14},{7,15},{8,0},{9,1},... | collective-permute-start | bytes 172040 | tf_op jit(solution)/shard_map/ppermute | solution.py:65
  15.8 2.3 %collective-permute-start.2 = (bf16[224,128]{1,0:T(8,128)(2,1)S(1)}, bf16[224,128]{1,0:T(8,128)(2,1)S(1)}, u32[]{:S(2)}, u32[]{:S(2)}) collective-permute-start(bf16[224,128]{1,0:T(8,128)(2,1)S(1)} %get-tuple-element.76), channel_id=1, source_target_pairs={{0,24},{1,25},{2,26},{3,27},{4,28},{5,29},{6,30},{7,31},{8,16},{9,... | collective-permute-start | bytes 172040 | tf_op jit(solution)/shard_map/ppermute | solution.py:65
  18.8 3.4 %collective-permute-done.2 = bf16[224,128]{1,0:T(8,128)(2,1)S(1)} collective-permute-done((bf16[224,128]{1,0:T(8,128)(2,1)S(1)}, bf16[224,128]{1,0:T(8,128)(2,1)S(1)}, u32[]{:S(2)}, u32[]{:S(2)}) %collective-permute-start.2) | collective-permute-done | bytes 57376 | tf_op jit(solution)/shard_map/ppermute | solution.py:65
  22.3 1.5 %collective-permute-start.8 = (bf16[4,224,128]{2,1,0:T(8,128)(2,1)S(1)}, bf16[4,224,128]{2,1,0:T(8,128)(2,1)S(1)}, u32[]{:S(2)}, u32[]{:S(2)}) collective-permute-start(bf16[4,224,128]{2,1,0:T(8,128)(2,1)S(1)} %pad_maximum_fusion.refs_2_.refs_3_), channel_id=1, source_target_pairs={{0,5},{1,4},{2,7},{3,6},{4,1},{5,0},{6,3},{7,2},{8,13},{9,12},{10,... | collective-permute-start | bytes 688136 | tf_op jit(solution)/shard_map/ppermute | solution.py:65
  24.4 1.5 %collective-permute-start.6 = (bf16[4,224,128]{2,1,0:T(8,128)(2,1)S(1)}, bf16[4,224,128]{2,1,0:T(8,128)(2,1)S(1)}, u32[]{:S(2)}, u32[]{:S(2)}) collective-permute-start(bf16[4,224,128]{2,1,0:T(8,128)(2,1)S(1)} %pad_maximum_fusion.refs_2_.refs_3_), channel_id=1, source_target_pairs={{0,1},{1,0},{2,3},{3,2},{4,5},{5,4},{6,7},{7,6},{8,9},{9,8},{10,11... | collective-permute-start | bytes 688136 | tf_op jit(solution)/shard_map/ppermute | solution.py:65
  25.9 1.3 %collective-permute-start.9 = (bf16[464,128]{1,0:T(8,128)(2,1)S(1)}, bf16[464,128]{1,0:T(8,128)(2,1)S(1)}, u32[]{:S(2)}, u32[]{:S(2)}) collective-permute-start(bf16[464,128]{1,0:T(8,128)(2,1)S(1)} %get-tuple-element.42), channel_id=1, source_target_pairs={{0,2},{2,4},{4,6},{6,8},{8,10},{10,12},{12,14},{14,16},{16,18},{18... | collective-permute-start | bytes 356360 | tf_op jit(solution)/shard_map/ppermute | solution.py:210
  28.5 8.2 %collective-permute-start.11 = (bf16[4,224,128]{2,1,0:T(8,128)(2,1)S(1)}, bf16[4,224,128]{2,1,0:T(8,128)(2,1)S(1)}, u32[]{:S(2)}, u32[]{:S(2)}) collective-permute-start(bf16[4,224,128]{2,1,0:T(8,128)(2,1)S(1)} %pad_maximum_fusion.refs_2_.refs_3_), channel_id=1, source_target_pairs={{0,2},{1,3},{2,0},{3,1},{4,6},{5,7},{6,4},{7,5},{8,10},{9,11},{10,... | collective-permute-start | bytes 688136 | tf_op jit(solution)/shard_map/ppermute | solution.py:65
  36.7 2.4 %shard_map.94 = (bf16[2112,768]{1,0:T(8,128)(2,1)S(1)}, bf16[2112,256]{1,0:T(8,128)(2,1)S(1)}) custom-call(bf16[64,64,128]{2,1,0:T(8,128)(2,1)S(1)} %copy-done.1, bf16[32,32,192]{2,1,0:T(8,128)(2,1)S(1)} %copy-done.3, bf16[1536,128]{1,0:T(8,128)(2,1)S(1)} %collective-permute-done.5.side_ref, bf16[704,128]{1,0:T(8,128)(2,1)S(1)} %collective-permute-done.3.south_ref, ...), custom_call_target="tpu_custom_call" | custom-call | bytes 12582912 | tf_op jit(solution)/shard_map/pallas_call | solution.py:766
  41.3 14.8 %shard_map.95 = (bf16[32,32,192]{2,1,0:T(8,128)(2,1)}, bf16[2,16,176,128]{3,2,1,0:T(8,128)(2,1)S(1)}, f32[2128,128]{1,0:T(8,128)S(1)}, f32[2128,128]{1,0:T(8,128)S(1)}) custom-call(bf16[2112,768]{1,0:T(8,128)(2,1)S(1)} %get-tuple-element.46.refs_0_, bf16[2112,256]{1,0:T(8,128)(2,1)S(1)} %get-tuple-element.47.refs_1_, ...), custom_call_target="tpu_custom_call" | custom-call | flops 5000000000 | bytes 12582912 | tf_op jit(solution)/shard_map/pallas_call | solution.py:808
  56.4 2.0 %collective-permute-done.15 = bf16[16,176,128]{2,1,0:T(8,128)(2,1)S(1)} collective-permute-done((bf16[16,176,128]{2,1,0:T(8,128)(2,1)S(1)}, bf16[16,176,128]{2,1,0:T(8,128)(2,1)S(1)}, u32[]{:S(2)}, u32[]{:S(2)}) %collective-permute-start.15) | collective-permute-done | bytes 720928 | tf_op jit(solution)/shard_map/ppermute | solution.py:65
  58.7 1.3 %collective-permute-start.16 = (bf16[4,176,128]{2,1,0:T(8,128)(2,1)S(1)}, bf16[4,176,128]{2,1,0:T(8,128)(2,1)S(1)}, u32[]{:S(2)}, u32[]{:S(2)}) collective-permute-start(bf16[4,176,128]{2,1,0:T(8,128)(2,1)S(1)} %get-tuple-element.65), channel_id=1, source_target_pairs={{0,1},{1,0},{2,3},{3,2},{4,5},{5,4},{6,7},{7,6},{8,9},{9,8},{10,11... | collective-permute-start | bytes 540680 | tf_op jit(solution)/shard_map/ppermute | solution.py:65
  60.0 2.7 %collective-permute-start.18 = (bf16[4,176,128]{2,1,0:T(8,128)(2,1)S(1)}, bf16[4,176,128]{2,1,0:T(8,128)(2,1)S(1)}, u32[]{:S(2)}, u32[]{:S(2)}) collective-permute-start(bf16[4,176,128]{2,1,0:T(8,128)(2,1)S(1)} %get-tuple-element.66), channel_id=1, source_target_pairs={{0,5},{1,4},{2,7},{3,6},{4,1},{5,0},{6,3},{7,2},{8,13},{9,12},{10,... | collective-permute-start | bytes 540680 | tf_op jit(solution)/shard_map/ppermute | solution.py:65
  62.8 6.5 %shard_map.96 = (bf16[64,64,128]{2,1,0:T(8,128)(2,1)}, bf16[2,16,64,128]{3,2,1,0:T(8,128)(2,1)S(1)}) custom-call(bf16[2112,768]{1,0:T(8,128)(2,1)S(1)} %get-tuple-element.46.refs_0_, f32[2128,128]{1,0:T(8,128)S(1)} %get-tuple-element.55.refs_1_, f32[2128,128]{1,0:T(8,128)S(1)} %get-tuple-element.56.refs_2_, ...), custom_call_target="tpu_custom_call" | custom-call | flops 2000000000 | bytes 12582912 | tf_op jit(solution)/shard_map/pallas_call | solution.py:808
  69.4 2.1 %collective-permute-done.18 = bf16[4,176,128]{2,1,0:T(8,128)(2,1)S(1)} collective-permute-done((bf16[4,176,128]{2,1,0:T(8,128)(2,1)S(1)}, bf16[4,176,128]{2,1,0:T(8,128)(2,1)S(1)}, u32[]{:S(2)}, u32[]{:S(2)}) %collective-permute-start.18) | collective-permute-done | bytes 180256 | tf_op jit(solution)/shard_map/ppermute | solution.py:65
  71.5 1.4 %collective-permute-done.17 = bf16[4,176,128]{2,1,0:T(8,128)(2,1)S(1)} collective-permute-done((bf16[4,176,128]{2,1,0:T(8,128)(2,1)S(1)}, bf16[4,176,128]{2,1,0:T(8,128)(2,1)S(1)}, u32[]{:S(2)}, u32[]{:S(2)}) %collective-permute-start.17) | collective-permute-done | bytes 180256 | tf_op jit(solution)/shard_map/ppermute | solution.py:65
  73.0 1.4 %collective-permute-start.20 = (bf16[4,64,128]{2,1,0:T(8,128)(2,1)S(1)}, bf16[4,64,128]{2,1,0:T(8,128)(2,1)S(1)}, u32[]{:S(2)}, u32[]{:S(2)}) collective-permute-start(bf16[4,64,128]{2,1,0:T(8,128)(2,1)S(1)} %get-tuple-element.68), channel_id=1, source_target_pairs={{0,1},{1,0},{2,3},{3,2},{4,5},{5,4},{6,7},{7,6},{8,9},{9,8},{10,11... | collective-permute-start | bytes 196616 | tf_op jit(solution)/shard_map/ppermute | solution.py:65
  74.9 1.7 %collective-permute-start.21 = (bf16[4,64,128]{2,1,0:T(8,128)(2,1)S(1)}, bf16[4,64,128]{2,1,0:T(8,128)(2,1)S(1)}, u32[]{:S(2)}, u32[]{:S(2)}) collective-permute-start(bf16[4,64,128]{2,1,0:T(8,128)(2,1)S(1)} %get-tuple-element.70), channel_id=1, source_target_pairs={{0,4},{1,5},{2,6},{3,7},{4,0},{5,1},{6,2},{7,3},{8,12},{9,13},{10,... | collective-permute-start | bytes 196616 | tf_op jit(solution)/shard_map/ppermute | solution.py:65
  77.7 2.0 %collective-permute-done.22 = bf16[4,64,128]{2,1,0:T(8,128)(2,1)S(1)} collective-permute-done((bf16[4,64,128]{2,1,0:T(8,128)(2,1)S(1)}, bf16[4,64,128]{2,1,0:T(8,128)(2,1)S(1)}, u32[]{:S(2)}, u32[]{:S(2)}) %collective-permute-start.22) | collective-permute-done | bytes 65568 | tf_op jit(solution)/shard_map/ppermute | solution.py:65
  79.9 1.4 %collective-permute-start.25 = (bf16[240,128]{1,0:T(8,128)(2,1)S(1)}, bf16[240,128]{1,0:T(8,128)(2,1)S(1)}, u32[]{:S(2)}, u32[]{:S(2)}) collective-permute-start(bf16[240,128]{1,0:T(8,128)(2,1)S(1)} %get-tuple-element.71), channel_id=1, source_target_pairs={{0,24},{1,25},{2,26},{3,27},{4,28},{5,29},{6,30},{7,31},{8,16},{9,... | collective-permute-start | bytes 184328 | tf_op jit(solution)/shard_map/ppermute | solution.py:65
  81.3 3.0 %collective-permute-start.24 = (bf16[240,128]{1,0:T(8,128)(2,1)S(1)}, bf16[240,128]{1,0:T(8,128)(2,1)S(1)}, u32[]{:S(2)}, u32[]{:S(2)}) collective-permute-start(bf16[240,128]{1,0:T(8,128)(2,1)S(1)} %get-tuple-element.74), channel_id=1, source_target_pairs={{0,16},{1,17},{2,18},{3,19},{4,20},{5,21},{6,22},{7,23},{8,24},{9,... | collective-permute-start | bytes 184328 | tf_op jit(solution)/shard_map/ppermute | solution.py:65
  84.3 1.7 %collective-permute-done.25.refs_3_ = bf16[240,128]{1,0:T(8,128)(2,1)S(1)} collective-permute-done((bf16[240,128]{1,0:T(8,128)(2,1)S(1)}, bf16[240,128]{1,0:T(8,128)(2,1)S(1)}, u32[]{:S(2)}, u32[]{:S(2)}) %collective-permute-start.25) | collective-permute-done | bytes 61472 | tf_op jit(solution)/shard_map/ppermute | solution.py:65
  (54 shorter events, 13.9 us)
Async XLA Ops:
  3.4 19.0 %collective-permute-start.5 = (bf16[1536,128]{1,0:T(8,128)(2,1)S(1)}, bf16[1536,128]{1,0:T(8,128)(2,1)S(1)}, u32[]{:S(2)}, u32[]{:S(2)}) collective-permute-start(bf16[1536,128]{1,0:T(8,128)(2,1)S(1)} %get-tuple-element.37), channel_id=1, source_target_pairs={{0,1},{1,0},{2,3},{3,2},{4,5},{5,4},{6,7},{7,6},{8,9},{9,8},{10,11... | collective-permute-start | bytes 1179656 | tf_op jit(solution)/shard_map/ppermute | solution.py:200
  7.1 8.6 %collective-permute-start.1 = (bf16[224,128]{1,0:T(8,128)(2,1)S(1)}, bf16[224,128]{1,0:T(8,128)(2,1)S(1)}, u32[]{:S(2)}, u32[]{:S(2)}) collective-permute-start(bf16[224,128]{1,0:T(8,128)(2,1)S(1)} %get-tuple-element.76), channel_id=1, source_target_pairs={{0,16},{1,17},{2,18},{3,19},{4,20},{5,21},{6,22},{7,23},{8,24},{9,... | collective-permute-start | bytes 172040 | tf_op jit(solution)/shard_map/ppermute | solution.py:65
  9.8 12.5 %collective-permute-start.4 = (bf16[832,128]{1,0:T(8,128)(2,1)S(1)}, bf16[832,128]{1,0:T(8,128)(2,1)S(1)}, u32[]{:S(2)}, u32[]{:S(2)}) collective-permute-start(bf16[832,128]{1,0:T(8,128)(2,1)S(1)} %get-tuple-element.36), channel_id=1, source_target_pairs={{2,0},{4,2},{6,4},{8,6},{10,8},{12,10},{14,12},{16,14},{18,16},{20... | collective-permute-start | bytes 638984 | tf_op jit(solution)/shard_map/ppermute | solution.py:210
  11.1 11.2 %collective-permute-start.3 = (bf16[704,128]{1,0:T(8,128)(2,1)S(1)}, bf16[704,128]{1,0:T(8,128)(2,1)S(1)}, u32[]{:S(2)}, u32[]{:S(2)}) collective-permute-start(bf16[704,128]{1,0:T(8,128)(2,1)S(1)} %get-tuple-element.35), channel_id=1, source_target_pairs={{0,2},{2,4},{4,6},{6,8},{8,10},{10,12},{12,14},{14,16},{16,18},{18... | collective-permute-start | bytes 540680 | tf_op jit(solution)/shard_map/ppermute | solution.py:210
  14.1 4.7 %collective-permute-start = (bf16[224,128]{1,0:T(8,128)(2,1)S(1)}, bf16[224,128]{1,0:T(8,128)(2,1)S(1)}, u32[]{:S(2)}, u32[]{:S(2)}) collective-permute-start(bf16[224,128]{1,0:T(8,128)(2,1)S(1)} %get-tuple-element.76), channel_id=1, source_target_pairs={{0,8},{1,9},{2,10},{3,11},{4,12},{5,13},{6,14},{7,15},{8,0},{9,1},... | collective-permute-start | bytes 172040 | tf_op jit(solution)/shard_map/ppermute | solution.py:65
  15.8 6.5 %collective-permute-start.2 = (bf16[224,128]{1,0:T(8,128)(2,1)S(1)}, bf16[224,128]{1,0:T(8,128)(2,1)S(1)}, u32[]{:S(2)}, u32[]{:S(2)}) collective-permute-start(bf16[224,128]{1,0:T(8,128)(2,1)S(1)} %get-tuple-element.76), channel_id=1, source_target_pairs={{0,24},{1,25},{2,26},{3,27},{4,28},{5,29},{6,30},{7,31},{8,16},{9,... | collective-permute-start | bytes 172040 | tf_op jit(solution)/shard_map/ppermute | solution.py:65
  22.3 16.8 %collective-permute-start.8 = (bf16[4,224,128]{2,1,0:T(8,128)(2,1)S(1)}, bf16[4,224,128]{2,1,0:T(8,128)(2,1)S(1)}, u32[]{:S(2)}, u32[]{:S(2)}) collective-permute-start(bf16[4,224,128]{2,1,0:T(8,128)(2,1)S(1)} %pad_maximum_fusion.refs_2_.refs_3_), channel_id=1, source_target_pairs={{0,5},{1,4},{2,7},{3,6},{4,1},{5,0},{6,3},{7,2},{8,13},{9,12},{10,... | collective-permute-start | bytes 688136 | tf_op jit(solution)/shard_map/ppermute | solution.py:65
  23.8 15.3 %collective-permute-start.7 = (bf16[4,224,128]{2,1,0:T(8,128)(2,1)S(1)}, bf16[4,224,128]{2,1,0:T(8,128)(2,1)S(1)}, u32[]{:S(2)}, u32[]{:S(2)}) collective-permute-start(bf16[4,224,128]{2,1,0:T(8,128)(2,1)S(1)} %pad_maximum_fusion.refs_2_.refs_3_), channel_id=1, source_target_pairs={{0,4},{1,5},{2,6},{3,7},{4,0},{5,1},{6,2},{7,3},{8,12},{9,13},{10,... | collective-permute-start | bytes 688136 | tf_op jit(solution)/shard_map/ppermute | solution.py:65
  24.4 14.7 %collective-permute-start.6 = (bf16[4,224,128]{2,1,0:T(8,128)(2,1)S(1)}, bf16[4,224,128]{2,1,0:T(8,128)(2,1)S(1)}, u32[]{:S(2)}, u32[]{:S(2)}) collective-permute-start(bf16[4,224,128]{2,1,0:T(8,128)(2,1)S(1)} %pad_maximum_fusion.refs_2_.refs_3_), channel_id=1, source_target_pairs={{0,1},{1,0},{2,3},{3,2},{4,5},{5,4},{6,7},{7,6},{8,9},{9,8},{10,11... | collective-permute-start | bytes 688136 | tf_op jit(solution)/shard_map/ppermute | solution.py:65
  25.9 2.6 %collective-permute-start.9 = (bf16[464,128]{1,0:T(8,128)(2,1)S(1)}, bf16[464,128]{1,0:T(8,128)(2,1)S(1)}, u32[]{:S(2)}, u32[]{:S(2)}) collective-permute-start(bf16[464,128]{1,0:T(8,128)(2,1)S(1)} %get-tuple-element.42), channel_id=1, source_target_pairs={{0,2},{2,4},{4,6},{6,8},{8,10},{10,12},{12,14},{14,16},{16,18},{18... | collective-permute-start | bytes 356360 | tf_op jit(solution)/shard_map/ppermute | solution.py:210
  27.2 9.5 %collective-permute-start.10 = (bf16[464,128]{1,0:T(8,128)(2,1)S(1)}, bf16[464,128]{1,0:T(8,128)(2,1)S(1)}, u32[]{:S(2)}, u32[]{:S(2)}) collective-permute-start(bf16[464,128]{1,0:T(8,128)(2,1)S(1)} %get-tuple-element.43), channel_id=1, source_target_pairs={{2,0},{4,2},{6,4},{8,6},{10,8},{12,10},{14,12},{16,14},{18,16},{20... | collective-permute-start | bytes 356360 | tf_op jit(solution)/shard_map/ppermute | solution.py:210
  28.5 11.3 %collective-permute-start.11 = (bf16[4,224,128]{2,1,0:T(8,128)(2,1)S(1)}, bf16[4,224,128]{2,1,0:T(8,128)(2,1)S(1)}, u32[]{:S(2)}, u32[]{:S(2)}) collective-permute-start(bf16[4,224,128]{2,1,0:T(8,128)(2,1)S(1)} %pad_maximum_fusion.refs_2_.refs_3_), channel_id=1, source_target_pairs={{0,2},{1,3},{2,0},{3,1},{4,6},{5,7},{6,4},{7,5},{8,10},{9,11},{10,... | collective-permute-start | bytes 688136 | tf_op jit(solution)/shard_map/ppermute | solution.py:65
  39.3 1.7 %collective-permute-start.13 = (bf16[4,224,128]{2,1,0:T(8,128)(2,1)S(1)}, bf16[4,224,128]{2,1,0:T(8,128)(2,1)S(1)}, u32[]{:S(2)}, u32[]{:S(2)}) collective-permute-start(bf16[4,224,128]{2,1,0:T(8,128)(2,1)S(1)} %collective-permute-done.7.refs_4_.refs_5_), channel_id=1, source_target_pairs={{0,2},{1,3},{2,0},{3,1},{4,6},{5,7},{6,4},{7,5},{8,10},{9,11},{10,... | collective-permute-start | bytes 688136 | tf_op jit(solution)/shard_map/ppermute | solution.py:65
  56.2 2.3 %collective-permute-start.15 = (bf16[16,176,128]{2,1,0:T(8,128)(2,1)S(1)}, bf16[16,176,128]{2,1,0:T(8,128)(2,1)S(1)}, u32[]{:S(2)}, u32[]{:S(2)}) collective-permute-start(bf16[16,176,128]{2,1,0:T(8,128)(2,1)S(1)} %slice_bitcast_fusion), channel_id=1, source_target_pairs={{0,2},{1,3},{2,0},{3,1},{4,6},{5,7},{6,4},{7,5},{8,10},{9,11},{10,... | collective-permute-start | bytes 2162696 | tf_op jit(solution)/shard_map/ppermute | solution.py:65
  58.7 10.7 %collective-permute-start.16 = (bf16[4,176,128]{2,1,0:T(8,128)(2,1)S(1)}, bf16[4,176,128]{2,1,0:T(8,128)(2,1)S(1)}, u32[]{:S(2)}, u32[]{:S(2)}) collective-permute-start(bf16[4,176,128]{2,1,0:T(8,128)(2,1)S(1)} %get-tuple-element.65), channel_id=1, source_target_pairs={{0,1},{1,0},{2,3},{3,2},{4,5},{5,4},{6,7},{7,6},{8,9},{9,8},{10,11... | collective-permute-start | bytes 540680 | tf_op jit(solution)/shard_map/ppermute | solution.py:65
  60.0 11.4 %collective-permute-start.18 = (bf16[4,176,128]{2,1,0:T(8,128)(2,1)S(1)}, bf16[4,176,128]{2,1,0:T(8,128)(2,1)S(1)}, u32[]{:S(2)}, u32[]{:S(2)}) collective-permute-start(bf16[4,176,128]{2,1,0:T(8,128)(2,1)S(1)} %get-tuple-element.66), channel_id=1, source_target_pairs={{0,5},{1,4},{2,7},{3,6},{4,1},{5,0},{6,3},{7,2},{8,13},{9,12},{10,... | collective-permute-start | bytes 540680 | tf_op jit(solution)/shard_map/ppermute | solution.py:65
  62.8 10.1 %collective-permute-start.17 = (bf16[4,176,128]{2,1,0:T(8,128)(2,1)S(1)}, bf16[4,176,128]{2,1,0:T(8,128)(2,1)S(1)}, u32[]{:S(2)}, u32[]{:S(2)}) collective-permute-start(bf16[4,176,128]{2,1,0:T(8,128)(2,1)S(1)} %get-tuple-element.67), channel_id=1, source_target_pairs={{0,4},{1,5},{2,6},{3,7},{4,0},{5,1},{6,2},{7,3},{8,12},{9,13},{10,... | collective-permute-start | bytes 540680 | tf_op jit(solution)/shard_map/ppermute | solution.py:65
  69.3 3.6 %collective-permute-start.19 = (bf16[16,64,128]{2,1,0:T(8,128)(2,1)S(1)}, bf16[16,64,128]{2,1,0:T(8,128)(2,1)S(1)}, u32[]{:S(2)}, u32[]{:S(2)}) collective-permute-start(bf16[16,64,128]{2,1,0:T(8,128)(2,1)S(1)} %slice_bitcast_fusion.1), channel_id=1, source_target_pairs={{0,2},{1,3},{2,0},{3,1},{4,6},{5,7},{6,4},{7,5},{8,10},{9,11},{10,... | collective-permute-start | bytes 786440 | tf_op jit(solution)/shard_map/ppermute | solution.py:65
  73.0 4.6 %collective-permute-start.20 = (bf16[4,64,128]{2,1,0:T(8,128)(2,1)S(1)}, bf16[4,64,128]{2,1,0:T(8,128)(2,1)S(1)}, u32[]{:S(2)}, u32[]{:S(2)}) collective-permute-start(bf16[4,64,128]{2,1,0:T(8,128)(2,1)S(1)} %get-tuple-element.68), channel_id=1, source_target_pairs={{0,1},{1,0},{2,3},{3,2},{4,5},{5,4},{6,7},{7,6},{8,9},{9,8},{10,11... | collective-permute-start | bytes 196616 | tf_op jit(solution)/shard_map/ppermute | solution.py:65
  74.4 5.3 %collective-permute-start.22 = (bf16[4,64,128]{2,1,0:T(8,128)(2,1)S(1)}, bf16[4,64,128]{2,1,0:T(8,128)(2,1)S(1)}, u32[]{:S(2)}, u32[]{:S(2)}) collective-permute-start(bf16[4,64,128]{2,1,0:T(8,128)(2,1)S(1)} %get-tuple-element.69), channel_id=1, source_target_pairs={{0,5},{1,4},{2,7},{3,6},{4,1},{5,0},{6,3},{7,2},{8,13},{9,12},{10,... | collective-permute-start | bytes 196616 | tf_op jit(solution)/shard_map/ppermute | solution.py:65
  74.9 5.0 %collective-permute-start.21 = (bf16[4,64,128]{2,1,0:T(8,128)(2,1)S(1)}, bf16[4,64,128]{2,1,0:T(8,128)(2,1)S(1)}, u32[]{:S(2)}, u32[]{:S(2)}) collective-permute-start(bf16[4,64,128]{2,1,0:T(8,128)(2,1)S(1)} %get-tuple-element.70), channel_id=1, source_target_pairs={{0,4},{1,5},{2,6},{3,7},{4,0},{5,1},{6,2},{7,3},{8,12},{9,13},{10,... | collective-permute-start | bytes 196616 | tf_op jit(solution)/shard_map/ppermute | solution.py:65
  79.9 6.1 %collective-permute-start.25 = (bf16[240,128]{1,0:T(8,128)(2,1)S(1)}, bf16[240,128]{1,0:T(8,128)(2,1)S(1)}, u32[]{:S(2)}, u32[]{:S(2)}) collective-permute-start(bf16[240,128]{1,0:T(8,128)(2,1)S(1)} %get-tuple-element.71), channel_id=1, source_target_pairs={{0,24},{1,25},{2,26},{3,27},{4,28},{5,29},{6,30},{7,31},{8,16},{9,... | collective-permute-start | bytes 184328 | tf_op jit(solution)/shard_map/ppermute | solution.py:65
  81.3 5.6 %collective-permute-start.23 = (bf16[240,128]{1,0:T(8,128)(2,1)S(1)}, bf16[240,128]{1,0:T(8,128)(2,1)S(1)}, u32[]{:S(2)}, u32[]{:S(2)}) collective-permute-start(bf16[240,128]{1,0:T(8,128)(2,1)S(1)} %get-tuple-element.73), channel_id=1, source_target_pairs={{0,8},{1,9},{2,10},{3,11},{4,12},{5,13},{6,14},{7,15},{8,0},{9,1},... | collective-permute-start | bytes 184328 | tf_op jit(solution)/shard_map/ppermute | solution.py:65
  81.3 5.6 %collective-permute-start.24 = (bf16[240,128]{1,0:T(8,128)(2,1)S(1)}, bf16[240,128]{1,0:T(8,128)(2,1)S(1)}, u32[]{:S(2)}, u32[]{:S(2)}) collective-permute-start(bf16[240,128]{1,0:T(8,128)(2,1)S(1)} %get-tuple-element.74), channel_id=1, source_target_pairs={{0,16},{1,17},{2,18},{3,19},{4,20},{5,21},{6,22},{7,23},{8,24},{9,... | collective-permute-start | bytes 184328 | tf_op jit(solution)/shard_map/ppermute | solution.py:65
  (6 other events, 73.1 us)

commit v4 on v3

--- a/solution.py
+++ b/solution.py
@@ -252,7 +252,7 @@
         wide[pl.ds(pl.multiple_of(at(i, 0), 8), 2 * cols), :] = x_ref[i].astype(F32)
         return 0
 
-    lax.fori_loop(0, 2 * rows, own, 0)
+    lax.fori_loop(0, 2 * rows, own, 0, unroll=8)
     for j, place in zip(columns, side[0][0] + side[1][0]):
         strip = side_ref[place : place + 2 * rows, :].astype(F32)
         wide[pl.ds(at(0, j), 2 * rows, stride=span), :] = strip
@@ -280,7 +280,7 @@
                 windows_ref[pl.ds(pl.multiple_of(k * pitch, 16), pitch), lane : lane + 128] = cells
         return 0
 
-    lax.fori_loop(0, height, window, 0)
+    lax.fori_loop(0, height, window, 0, unroll=11)
 
     def cell(i, j):
         return GUARD + (i + ABOVE) * pitch + LEFT + j
@@ -384,7 +384,7 @@
             k_b[pl.ds(2 * at + 1, step, stride=2), :] = jnp.where(low, third_r, third)
             return 0
 
-        lax.fori_loop(0, pairs // step, one, 0)
+        lax.fori_loop(0, pairs // step, one, 0, unroll=True)
 
     def tap_rows(tap, part):
         start = (3 * tap[0] + tap[1]) * mid + 128 * part

time: 88 us -> 86.9 us (0.988)
  Pallas kernels: 24.9 us -> 23.5 us
    pallas_call x2, Pallas kernels: 21.3 us -> 20.3 us  [call(): pl.pallas_call(functools.partial(level, shape, devices, parts, second, na...]
  transfers between devices with their start and end apart: 26 -> 26, of which waited for: 13 -> 13; matrix products, arithmetic and copies ran while one was open for 1% -> 1% of each run, Pallas kernels for 10% -> 9%
where the time goes in v4:
time: 86.9 us; the launch traced here: 86.5 us
  starting transfers between devices  41.3 us (48%)
  Pallas kernels  23.5 us (27%)
  waiting for transfers between devices  17.3 us (20%)
  local copies, waits for them, and re-layouts  2.39 us (3%)
  other arithmetic  1.22 us (1%)
    ppermute x21, starting transfers between devices, send(): return lax.ppermute(value, BOTH, pairs)  31.4 us
    pallas_call x2, Pallas kernels, call(): pl.pallas_call(functools.partial(level, shape, devices, parts, second, na...  20.3 us
    ppermute x21, waiting for transfers between devices, send(): return lax.ppermute(value, BOTH, pairs)  17.3 us
    ppermute x4, starting transfers between devices, lengthways(): return (lax.ppermute(south, LAT, down), lax.ppermute(north, LAT, up))  6.91 us
    ppermute x1, starting transfers between devices, sideways(): return lax.ppermute(packed, 'lon', east)  3 us
    unnamed x8, local copies, waits for them, and re-layouts  2.27 us
    pallas_call x1, Pallas kernels, local(): pl.pallas_call(functools.partial(prepare, rows, cols), out_shape=(jax.Sha...  1.95 us
  transfers between devices with their start and end apart: 26, of which 13 were waited for; matrix products, arithmetic and copies ran while one was open for 1% of the time, Pallas kernels for 9%

profile of v4, /device:TPU:0, one launch (start us, length us, event | category | flops | bytes accessed | tf_op | source)
XLA Modules:
  0.0 86.5 jit_solution(2593212295570569147)
XLA Ops:
  3.4 3.0 %collective-permute-start.5 = (bf16[1536,128]{1,0:T(8,128)(2,1)S(1)}, bf16[1536,128]{1,0:T(8,128)(2,1)S(1)}, u32[]{:S(2)}, u32[]{:S(2)}) collective-permute-start(bf16[1536,128]{1,0:T(8,128)(2,1)S(1)} %get-tuple-element.37), channel_id=1, source_target_pairs={{0,1},{1,0},{2,3},{3,2},{4,5},{5,4},{6,7},{7,6},{8,9},{9,8},{10,11... | collective-permute-start | bytes 1179656 | tf_op jit(solution)/shard_map/ppermute | solution.py:200
  7.1 2.7 %collective-permute-start.1 = (bf16[224,128]{1,0:T(8,128)(2,1)S(1)}, bf16[224,128]{1,0:T(8,128)(2,1)S(1)}, u32[]{:S(2)}, u32[]{:S(2)}) collective-permute-start(bf16[224,128]{1,0:T(8,128)(2,1)S(1)} %get-tuple-element.76), channel_id=1, source_target_pairs={{0,16},{1,17},{2,18},{3,19},{4,20},{5,21},{6,22},{7,23},{8,24},{9,... | collective-permute-start | bytes 172040 | tf_op jit(solution)/shard_map/ppermute | solution.py:65
  11.1 3.0 %collective-permute-start.3 = (bf16[704,128]{1,0:T(8,128)(2,1)S(1)}, bf16[704,128]{1,0:T(8,128)(2,1)S(1)}, u32[]{:S(2)}, u32[]{:S(2)}) collective-permute-start(bf16[704,128]{1,0:T(8,128)(2,1)S(1)} %get-tuple-element.35), channel_id=1, source_target_pairs={{0,2},{2,4},{4,6},{6,8},{8,10},{10,12},{12,14},{14,16},{16,18},{18... | collective-permute-start | bytes 540680 | tf_op jit(solution)/shard_map/ppermute | solution.py:210
  14.1 1.6 %collective-permute-start = (bf16[224,128]{1,0:T(8,128)(2,1)S(1)}, bf16[224,128]{1,0:T(8,128)(2,1)S(1)}, u32[]{:S(2)}, u32[]{:S(2)}) collective-permute-start(bf16[224,128]{1,0:T(8,128)(2,1)S(1)} %get-tuple-element.76), channel_id=1, source_target_pairs={{0,8},{1,9},{2,10},{3,11},{4,12},{5,13},{6,14},{7,15},{8,0},{9,1},... | collective-permute-start | bytes 172040 | tf_op jit(solution)/shard_map/ppermute | solution.py:65
  15.8 2.3 %collective-permute-start.2 = (bf16[224,128]{1,0:T(8,128)(2,1)S(1)}, bf16[224,128]{1,0:T(8,128)(2,1)S(1)}, u32[]{:S(2)}, u32[]{:S(2)}) collective-permute-start(bf16[224,128]{1,0:T(8,128)(2,1)S(1)} %get-tuple-element.76), channel_id=1, source_target_pairs={{0,24},{1,25},{2,26},{3,27},{4,28},{5,29},{6,30},{7,31},{8,16},{9,... | collective-permute-start | bytes 172040 | tf_op jit(solution)/shard_map/ppermute | solution.py:65
  18.8 3.4 %collective-permute-done.2 = bf16[224,128]{1,0:T(8,128)(2,1)S(1)} collective-permute-done((bf16[224,128]{1,0:T(8,128)(2,1)S(1)}, bf16[224,128]{1,0:T(8,128)(2,1)S(1)}, u32[]{:S(2)}, u32[]{:S(2)}) %collective-permute-start.2) | collective-permute-done | bytes 57376 | tf_op jit(solution)/shard_map/ppermute | solution.py:65
  22.3 1.5 %collective-permute-start.8 = (bf16[4,224,128]{2,1,0:T(8,128)(2,1)S(1)}, bf16[4,224,128]{2,1,0:T(8,128)(2,1)S(1)}, u32[]{:S(2)}, u32[]{:S(2)}) collective-permute-start(bf16[4,224,128]{2,1,0:T(8,128)(2,1)S(1)} %pad_maximum_fusion.refs_2_.refs_3_), channel_id=1, source_target_pairs={{0,5},{1,4},{2,7},{3,6},{4,1},{5,0},{6,3},{7,2},{8,13},{9,12},{10,... | collective-permute-start | bytes 688136 | tf_op jit(solution)/shard_map/ppermute | solution.py:65
  24.4 1.5 %collective-permute-start.6 = (bf16[4,224,128]{2,1,0:T(8,128)(2,1)S(1)}, bf16[4,224,128]{2,1,0:T(8,128)(2,1)S(1)}, u32[]{:S(2)}, u32[]{:S(2)}) collective-permute-start(bf16[4,224,128]{2,1,0:T(8,128)(2,1)S(1)} %pad_maximum_fusion.refs_2_.refs_3_), channel_id=1, source_target_pairs={{0,1},{1,0},{2,3},{3,2},{4,5},{5,4},{6,7},{7,6},{8,9},{9,8},{10,11... | collective-permute-start | bytes 688136 | tf_op jit(solution)/shard_map/ppermute | solution.py:65
  25.9 1.3 %collective-permute-start.9 = (bf16[464,128]{1,0:T(8,128)(2,1)S(1)}, bf16[464,128]{1,0:T(8,128)(2,1)S(1)}, u32[]{:S(2)}, u32[]{:S(2)}) collective-permute-start(bf16[464,128]{1,0:T(8,128)(2,1)S(1)} %get-tuple-element.42), channel_id=1, source_target_pairs={{0,2},{2,4},{4,6},{6,8},{8,10},{10,12},{12,14},{14,16},{16,18},{18... | collective-permute-start | bytes 356360 | tf_op jit(solution)/shard_map/ppermute | solution.py:210
  28.5 8.2 %collective-permute-start.11 = (bf16[4,224,128]{2,1,0:T(8,128)(2,1)S(1)}, bf16[4,224,128]{2,1,0:T(8,128)(2,1)S(1)}, u32[]{:S(2)}, u32[]{:S(2)}) collective-permute-start(bf16[4,224,128]{2,1,0:T(8,128)(2,1)S(1)} %pad_maximum_fusion.refs_2_.refs_3_), channel_id=1, source_target_pairs={{0,2},{1,3},{2,0},{3,1},{4,6},{5,7},{6,4},{7,5},{8,10},{9,11},{10,... | collective-permute-start | bytes 688136 | tf_op jit(solution)/shard_map/ppermute | solution.py:65
  36.7 2.0 %shard_map.94 = (bf16[2112,768]{1,0:T(8,128)(2,1)S(1)}, bf16[2112,256]{1,0:T(8,128)(2,1)S(1)}) custom-call(bf16[64,64,128]{2,1,0:T(8,128)(2,1)S(1)} %copy-done.1, bf16[32,32,192]{2,1,0:T(8,128)(2,1)S(1)} %copy-done.3, bf16[1536,128]{1,0:T(8,128)(2,1)S(1)} %collective-permute-done.5.side_ref, bf16[704,128]{1,0:T(8,128)(2,1)S(1)} %collective-permute-done.3.south_ref, ...), custom_call_target="tpu_custom_call" | custom-call | bytes 12582912 | tf_op jit(solution)/shard_map/pallas_call | solution.py:766
  40.9 14.1 %shard_map.95 = (bf16[32,32,192]{2,1,0:T(8,128)(2,1)}, bf16[2,16,176,128]{3,2,1,0:T(8,128)(2,1)S(1)}, f32[2128,128]{1,0:T(8,128)S(1)}, f32[2128,128]{1,0:T(8,128)S(1)}) custom-call(bf16[2112,768]{1,0:T(8,128)(2,1)S(1)} %get-tuple-element.46.refs_0_, bf16[2112,256]{1,0:T(8,128)(2,1)S(1)} %get-tuple-element.47.refs_1_, ...), custom_call_target="tpu_custom_call" | custom-call | flops 5000000000 | bytes 12582912 | tf_op jit(solution)/shard_map/pallas_call | solution.py:808
  55.4 2.0 %collective-permute-done.15 = bf16[16,176,128]{2,1,0:T(8,128)(2,1)S(1)} collective-permute-done((bf16[16,176,128]{2,1,0:T(8,128)(2,1)S(1)}, bf16[16,176,128]{2,1,0:T(8,128)(2,1)S(1)}, u32[]{:S(2)}, u32[]{:S(2)}) %collective-permute-start.15) | collective-permute-done | bytes 720928 | tf_op jit(solution)/shard_map/ppermute | solution.py:65
  57.6 1.4 %collective-permute-start.16 = (bf16[4,176,128]{2,1,0:T(8,128)(2,1)S(1)}, bf16[4,176,128]{2,1,0:T(8,128)(2,1)S(1)}, u32[]{:S(2)}, u32[]{:S(2)}) collective-permute-start(bf16[4,176,128]{2,1,0:T(8,128)(2,1)S(1)} %get-tuple-element.65), channel_id=1, source_target_pairs={{0,1},{1,0},{2,3},{3,2},{4,5},{5,4},{6,7},{7,6},{8,9},{9,8},{10,11... | collective-permute-start | bytes 540680 | tf_op jit(solution)/shard_map/ppermute | solution.py:65
  59.0 2.7 %collective-permute-start.18 = (bf16[4,176,128]{2,1,0:T(8,128)(2,1)S(1)}, bf16[4,176,128]{2,1,0:T(8,128)(2,1)S(1)}, u32[]{:S(2)}, u32[]{:S(2)}) collective-permute-start(bf16[4,176,128]{2,1,0:T(8,128)(2,1)S(1)} %get-tuple-element.66), channel_id=1, source_target_pairs={{0,5},{1,4},{2,7},{3,6},{4,1},{5,0},{6,3},{7,2},{8,13},{9,12},{10,... | collective-permute-start | bytes 540680 | tf_op jit(solution)/shard_map/ppermute | solution.py:65
  61.7 6.2 %shard_map.96 = (bf16[64,64,128]{2,1,0:T(8,128)(2,1)}, bf16[2,16,64,128]{3,2,1,0:T(8,128)(2,1)S(1)}) custom-call(bf16[2112,768]{1,0:T(8,128)(2,1)S(1)} %get-tuple-element.46.refs_0_, f32[2128,128]{1,0:T(8,128)S(1)} %get-tuple-element.55.refs_1_, f32[2128,128]{1,0:T(8,128)S(1)} %get-tuple-element.56.refs_2_, ...), custom_call_target="tpu_custom_call" | custom-call | flops 2000000000 | bytes 12582912 | tf_op jit(solution)/shard_map/pallas_call | solution.py:808
  68.0 2.4 %collective-permute-done.18 = bf16[4,176,128]{2,1,0:T(8,128)(2,1)S(1)} collective-permute-done((bf16[4,176,128]{2,1,0:T(8,128)(2,1)S(1)}, bf16[4,176,128]{2,1,0:T(8,128)(2,1)S(1)}, u32[]{:S(2)}, u32[]{:S(2)}) %collective-permute-start.18) | collective-permute-done | bytes 180256 | tf_op jit(solution)/shard_map/ppermute | solution.py:65
  70.4 1.4 %collective-permute-done.17 = bf16[4,176,128]{2,1,0:T(8,128)(2,1)S(1)} collective-permute-done((bf16[4,176,128]{2,1,0:T(8,128)(2,1)S(1)}, bf16[4,176,128]{2,1,0:T(8,128)(2,1)S(1)}, u32[]{:S(2)}, u32[]{:S(2)}) %collective-permute-start.17) | collective-permute-done | bytes 180256 | tf_op jit(solution)/shard_map/ppermute | solution.py:65
  72.0 1.3 %collective-permute-start.20 = (bf16[4,64,128]{2,1,0:T(8,128)(2,1)S(1)}, bf16[4,64,128]{2,1,0:T(8,128)(2,1)S(1)}, u32[]{:S(2)}, u32[]{:S(2)}) collective-permute-start(bf16[4,64,128]{2,1,0:T(8,128)(2,1)S(1)} %get-tuple-element.68), channel_id=1, source_target_pairs={{0,1},{1,0},{2,3},{3,2},{4,5},{5,4},{6,7},{7,6},{8,9},{9,8},{10,11... | collective-permute-start | bytes 196616 | tf_op jit(solution)/shard_map/ppermute | solution.py:65
  73.8 1.7 %collective-permute-start.21 = (bf16[4,64,128]{2,1,0:T(8,128)(2,1)S(1)}, bf16[4,64,128]{2,1,0:T(8,128)(2,1)S(1)}, u32[]{:S(2)}, u32[]{:S(2)}) collective-permute-start(bf16[4,64,128]{2,1,0:T(8,128)(2,1)S(1)} %get-tuple-element.70), channel_id=1, source_target_pairs={{0,4},{1,5},{2,6},{3,7},{4,0},{5,1},{6,2},{7,3},{8,12},{9,13},{10,... | collective-permute-start | bytes 196616 | tf_op jit(solution)/shard_map/ppermute | solution.py:65
  76.3 2.3 %collective-permute-done.22 = bf16[4,64,128]{2,1,0:T(8,128)(2,1)S(1)} collective-permute-done((bf16[4,64,128]{2,1,0:T(8,128)(2,1)S(1)}, bf16[4,64,128]{2,1,0:T(8,128)(2,1)S(1)}, u32[]{:S(2)}, u32[]{:S(2)}) %collective-permute-start.22) | collective-permute-done | bytes 65568 | tf_op jit(solution)/shard_map/ppermute | solution.py:65
  78.9 1.4 %collective-permute-start.25 = (bf16[240,128]{1,0:T(8,128)(2,1)S(1)}, bf16[240,128]{1,0:T(8,128)(2,1)S(1)}, u32[]{:S(2)}, u32[]{:S(2)}) collective-permute-start(bf16[240,128]{1,0:T(8,128)(2,1)S(1)} %get-tuple-element.71), channel_id=1, source_target_pairs={{0,24},{1,25},{2,26},{3,27},{4,28},{5,29},{6,30},{7,31},{8,16},{9,... | collective-permute-start | bytes 184328 | tf_op jit(solution)/shard_map/ppermute | solution.py:65
  80.2 3.1 %collective-permute-start.24 = (bf16[240,128]{1,0:T(8,128)(2,1)S(1)}, bf16[240,128]{1,0:T(8,128)(2,1)S(1)}, u32[]{:S(2)}, u32[]{:S(2)}) collective-permute-start(bf16[240,128]{1,0:T(8,128)(2,1)S(1)} %get-tuple-element.74), channel_id=1, source_target_pairs={{0,16},{1,17},{2,18},{3,19},{4,20},{5,21},{6,22},{7,23},{8,24},{9,... | collective-permute-start | bytes 184328 | tf_op jit(solution)/shard_map/ppermute | solution.py:65
  83.3 1.7 %collective-permute-done.25.refs_3_ = bf16[240,128]{1,0:T(8,128)(2,1)S(1)} collective-permute-done((bf16[240,128]{1,0:T(8,128)(2,1)S(1)}, bf16[240,128]{1,0:T(8,128)(2,1)S(1)}, u32[]{:S(2)}, u32[]{:S(2)}) %collective-permute-start.25) | collective-permute-done | bytes 61472 | tf_op jit(solution)/shard_map/ppermute | solution.py:65
  (54 shorter events, 13.5 us)
Async XLA Ops:
  3.4 19.0 %collective-permute-start.5 = (bf16[1536,128]{1,0:T(8,128)(2,1)S(1)}, bf16[1536,128]{1,0:T(8,128)(2,1)S(1)}, u32[]{:S(2)}, u32[]{:S(2)}) collective-permute-start(bf16[1536,128]{1,0:T(8,128)(2,1)S(1)} %get-tuple-element.37), channel_id=1, source_target_pairs={{0,1},{1,0},{2,3},{3,2},{4,5},{5,4},{6,7},{7,6},{8,9},{9,8},{10,11... | collective-permute-start | bytes 1179656 | tf_op jit(solution)/shard_map/ppermute | solution.py:200
  7.1 8.6 %collective-permute-start.1 = (bf16[224,128]{1,0:T(8,128)(2,1)S(1)}, bf16[224,128]{1,0:T(8,128)(2,1)S(1)}, u32[]{:S(2)}, u32[]{:S(2)}) collective-permute-start(bf16[224,128]{1,0:T(8,128)(2,1)S(1)} %get-tuple-element.76), channel_id=1, source_target_pairs={{0,16},{1,17},{2,18},{3,19},{4,20},{5,21},{6,22},{7,23},{8,24},{9,... | collective-permute-start | bytes 172040 | tf_op jit(solution)/shard_map/ppermute | solution.py:65
  9.8 12.5 %collective-permute-start.4 = (bf16[832,128]{1,0:T(8,128)(2,1)S(1)}, bf16[832,128]{1,0:T(8,128)(2,1)S(1)}, u32[]{:S(2)}, u32[]{:S(2)}) collective-permute-start(bf16[832,128]{1,0:T(8,128)(2,1)S(1)} %get-tuple-element.36), channel_id=1, source_target_pairs={{2,0},{4,2},{6,4},{8,6},{10,8},{12,10},{14,12},{16,14},{18,16},{20... | collective-permute-start | bytes 638984 | tf_op jit(solution)/shard_map/ppermute | solution.py:210
  11.1 11.2 %collective-permute-start.3 = (bf16[704,128]{1,0:T(8,128)(2,1)S(1)}, bf16[704,128]{1,0:T(8,128)(2,1)S(1)}, u32[]{:S(2)}, u32[]{:S(2)}) collective-permute-start(bf16[704,128]{1,0:T(8,128)(2,1)S(1)} %get-tuple-element.35), channel_id=1, source_target_pairs={{0,2},{2,4},{4,6},{6,8},{8,10},{10,12},{12,14},{14,16},{16,18},{18... | collective-permute-start | bytes 540680 | tf_op jit(solution)/shard_map/ppermute | solution.py:210
  14.1 4.7 %collective-permute-start = (bf16[224,128]{1,0:T(8,128)(2,1)S(1)}, bf16[224,128]{1,0:T(8,128)(2,1)S(1)}, u32[]{:S(2)}, u32[]{:S(2)}) collective-permute-start(bf16[224,128]{1,0:T(8,128)(2,1)S(1)} %get-tuple-element.76), channel_id=1, source_target_pairs={{0,8},{1,9},{2,10},{3,11},{4,12},{5,13},{6,14},{7,15},{8,0},{9,1},... | collective-permute-start | bytes 172040 | tf_op jit(solution)/shard_map/ppermute | solution.py:65
  15.8 6.5 %collective-permute-start.2 = (bf16[224,128]{1,0:T(8,128)(2,1)S(1)}, bf16[224,128]{1,0:T(8,128)(2,1)S(1)}, u32[]{:S(2)}, u32[]{:S(2)}) collective-permute-start(bf16[224,128]{1,0:T(8,128)(2,1)S(1)} %get-tuple-element.76), channel_id=1, source_target_pairs={{0,24},{1,25},{2,26},{3,27},{4,28},{5,29},{6,30},{7,31},{8,16},{9,... | collective-permute-start | bytes 172040 | tf_op jit(solution)/shard_map/ppermute | solution.py:65
  22.3 16.4 %collective-permute-start.8 = (bf16[4,224,128]{2,1,0:T(8,128)(2,1)S(1)}, bf16[4,224,128]{2,1,0:T(8,128)(2,1)S(1)}, u32[]{:S(2)}, u32[]{:S(2)}) collective-permute-start(bf16[4,224,128]{2,1,0:T(8,128)(2,1)S(1)} %pad_maximum_fusion.refs_2_.refs_3_), channel_id=1, source_target_pairs={{0,5},{1,4},{2,7},{3,6},{4,1},{5,0},{6,3},{7,2},{8,13},{9,12},{10,... | collective-permute-start | bytes 688136 | tf_op jit(solution)/shard_map/ppermute | solution.py:65
  23.8 14.9 %collective-permute-start.7 = (bf16[4,224,128]{2,1,0:T(8,128)(2,1)S(1)}, bf16[4,224,128]{2,1,0:T(8,128)(2,1)S(1)}, u32[]{:S(2)}, u32[]{:S(2)}) collective-permute-start(bf16[4,224,128]{2,1,0:T(8,128)(2,1)S(1)} %pad_maximum_fusion.refs_2_.refs_3_), channel_id=1, source_target_pairs={{0,4},{1,5},{2,6},{3,7},{4,0},{5,1},{6,2},{7,3},{8,12},{9,13},{10,... | collective-permute-start | bytes 688136 | tf_op jit(solution)/shard_map/ppermute | solution.py:65
  24.4 14.3 %collective-permute-start.6 = (bf16[4,224,128]{2,1,0:T(8,128)(2,1)S(1)}, bf16[4,224,128]{2,1,0:T(8,128)(2,1)S(1)}, u32[]{:S(2)}, u32[]{:S(2)}) collective-permute-start(bf16[4,224,128]{2,1,0:T(8,128)(2,1)S(1)} %pad_maximum_fusion.refs_2_.refs_3_), channel_id=1, source_target_pairs={{0,1},{1,0},{2,3},{3,2},{4,5},{5,4},{6,7},{7,6},{8,9},{9,8},{10,11... | collective-permute-start | bytes 688136 | tf_op jit(solution)/shard_map/ppermute | solution.py:65
  25.9 2.6 %collective-permute-start.9 = (bf16[464,128]{1,0:T(8,128)(2,1)S(1)}, bf16[464,128]{1,0:T(8,128)(2,1)S(1)}, u32[]{:S(2)}, u32[]{:S(2)}) collective-permute-start(bf16[464,128]{1,0:T(8,128)(2,1)S(1)} %get-tuple-element.42), channel_id=1, source_target_pairs={{0,2},{2,4},{4,6},{6,8},{8,10},{10,12},{12,14},{14,16},{16,18},{18... | collective-permute-start | bytes 356360 | tf_op jit(solution)/shard_map/ppermute | solution.py:210
  27.2 9.5 %collective-permute-start.10 = (bf16[464,128]{1,0:T(8,128)(2,1)S(1)}, bf16[464,128]{1,0:T(8,128)(2,1)S(1)}, u32[]{:S(2)}, u32[]{:S(2)}) collective-permute-start(bf16[464,128]{1,0:T(8,128)(2,1)S(1)} %get-tuple-element.43), channel_id=1, source_target_pairs={{2,0},{4,2},{6,4},{8,6},{10,8},{12,10},{14,12},{16,14},{18,16},{20... | collective-permute-start | bytes 356360 | tf_op jit(solution)/shard_map/ppermute | solution.py:210
  28.5 10.9 %collective-permute-start.11 = (bf16[4,224,128]{2,1,0:T(8,128)(2,1)S(1)}, bf16[4,224,128]{2,1,0:T(8,128)(2,1)S(1)}, u32[]{:S(2)}, u32[]{:S(2)}) collective-permute-start(bf16[4,224,128]{2,1,0:T(8,128)(2,1)S(1)} %pad_maximum_fusion.refs_2_.refs_3_), channel_id=1, source_target_pairs={{0,2},{1,3},{2,0},{3,1},{4,6},{5,7},{6,4},{7,5},{8,10},{9,11},{10,... | collective-permute-start | bytes 688136 | tf_op jit(solution)/shard_map/ppermute | solution.py:65
  38.9 1.7 %collective-permute-start.13 = (bf16[4,224,128]{2,1,0:T(8,128)(2,1)S(1)}, bf16[4,224,128]{2,1,0:T(8,128)(2,1)S(1)}, u32[]{:S(2)}, u32[]{:S(2)}) collective-permute-start(bf16[4,224,128]{2,1,0:T(8,128)(2,1)S(1)} %collective-permute-done.7.refs_4_.refs_5_), channel_id=1, source_target_pairs={{0,2},{1,3},{2,0},{3,1},{4,6},{5,7},{6,4},{7,5},{8,10},{9,11},{10,... | collective-permute-start | bytes 688136 | tf_op jit(solution)/shard_map/ppermute | solution.py:65
  55.1 2.3 %collective-permute-start.15 = (bf16[16,176,128]{2,1,0:T(8,128)(2,1)S(1)}, bf16[16,176,128]{2,1,0:T(8,128)(2,1)S(1)}, u32[]{:S(2)}, u32[]{:S(2)}) collective-permute-start(bf16[16,176,128]{2,1,0:T(8,128)(2,1)S(1)} %slice_bitcast_fusion), channel_id=1, source_target_pairs={{0,2},{1,3},{2,0},{3,1},{4,6},{5,7},{6,4},{7,5},{8,10},{9,11},{10,... | collective-permute-start | bytes 2162696 | tf_op jit(solution)/shard_map/ppermute | solution.py:65
  57.6 10.4 %collective-permute-start.16 = (bf16[4,176,128]{2,1,0:T(8,128)(2,1)S(1)}, bf16[4,176,128]{2,1,0:T(8,128)(2,1)S(1)}, u32[]{:S(2)}, u32[]{:S(2)}) collective-permute-start(bf16[4,176,128]{2,1,0:T(8,128)(2,1)S(1)} %get-tuple-element.65), channel_id=1, source_target_pairs={{0,1},{1,0},{2,3},{3,2},{4,5},{5,4},{6,7},{7,6},{8,9},{9,8},{10,11... | collective-permute-start | bytes 540680 | tf_op jit(solution)/shard_map/ppermute | solution.py:65
  59.0 11.4 %collective-permute-start.18 = (bf16[4,176,128]{2,1,0:T(8,128)(2,1)S(1)}, bf16[4,176,128]{2,1,0:T(8,128)(2,1)S(1)}, u32[]{:S(2)}, u32[]{:S(2)}) collective-permute-start(bf16[4,176,128]{2,1,0:T(8,128)(2,1)S(1)} %get-tuple-element.66), channel_id=1, source_target_pairs={{0,5},{1,4},{2,7},{3,6},{4,1},{5,0},{6,3},{7,2},{8,13},{9,12},{10,... | collective-permute-start | bytes 540680 | tf_op jit(solution)/shard_map/ppermute | solution.py:65
  61.7 10.1 %collective-permute-start.17 = (bf16[4,176,128]{2,1,0:T(8,128)(2,1)S(1)}, bf16[4,176,128]{2,1,0:T(8,128)(2,1)S(1)}, u32[]{:S(2)}, u32[]{:S(2)}) collective-permute-start(bf16[4,176,128]{2,1,0:T(8,128)(2,1)S(1)} %get-tuple-element.67), channel_id=1, source_target_pairs={{0,4},{1,5},{2,6},{3,7},{4,0},{5,1},{6,2},{7,3},{8,12},{9,13},{10,... | collective-permute-start | bytes 540680 | tf_op jit(solution)/shard_map/ppermute | solution.py:65
  67.9 4.0 %collective-permute-start.19 = (bf16[16,64,128]{2,1,0:T(8,128)(2,1)S(1)}, bf16[16,64,128]{2,1,0:T(8,128)(2,1)S(1)}, u32[]{:S(2)}, u32[]{:S(2)}) collective-permute-start(bf16[16,64,128]{2,1,0:T(8,128)(2,1)S(1)} %slice_bitcast_fusion.1), channel_id=1, source_target_pairs={{0,2},{1,3},{2,0},{3,1},{4,6},{5,7},{6,4},{7,5},{8,10},{9,11},{10,... | collective-permute-start | bytes 786440 | tf_op jit(solution)/shard_map/ppermute | solution.py:65
  72.0 4.3 %collective-permute-start.20 = (bf16[4,64,128]{2,1,0:T(8,128)(2,1)S(1)}, bf16[4,64,128]{2,1,0:T(8,128)(2,1)S(1)}, u32[]{:S(2)}, u32[]{:S(2)}) collective-permute-start(bf16[4,64,128]{2,1,0:T(8,128)(2,1)S(1)} %get-tuple-element.68), channel_id=1, source_target_pairs={{0,1},{1,0},{2,3},{3,2},{4,5},{5,4},{6,7},{7,6},{8,9},{9,8},{10,11... | collective-permute-start | bytes 196616 | tf_op jit(solution)/shard_map/ppermute | solution.py:65
  73.4 5.3 %collective-permute-start.22 = (bf16[4,64,128]{2,1,0:T(8,128)(2,1)S(1)}, bf16[4,64,128]{2,1,0:T(8,128)(2,1)S(1)}, u32[]{:S(2)}, u32[]{:S(2)}) collective-permute-start(bf16[4,64,128]{2,1,0:T(8,128)(2,1)S(1)} %get-tuple-element.69), channel_id=1, source_target_pairs={{0,5},{1,4},{2,7},{3,6},{4,1},{5,0},{6,3},{7,2},{8,13},{9,12},{10,... | collective-permute-start | bytes 196616 | tf_op jit(solution)/shard_map/ppermute | solution.py:65
  73.8 5.0 %collective-permute-start.21 = (bf16[4,64,128]{2,1,0:T(8,128)(2,1)S(1)}, bf16[4,64,128]{2,1,0:T(8,128)(2,1)S(1)}, u32[]{:S(2)}, u32[]{:S(2)}) collective-permute-start(bf16[4,64,128]{2,1,0:T(8,128)(2,1)S(1)} %get-tuple-element.70), channel_id=1, source_target_pairs={{0,4},{1,5},{2,6},{3,7},{4,0},{5,1},{6,2},{7,3},{8,12},{9,13},{10,... | collective-permute-start | bytes 196616 | tf_op jit(solution)/shard_map/ppermute | solution.py:65
  78.9 6.2 %collective-permute-start.25 = (bf16[240,128]{1,0:T(8,128)(2,1)S(1)}, bf16[240,128]{1,0:T(8,128)(2,1)S(1)}, u32[]{:S(2)}, u32[]{:S(2)}) collective-permute-start(bf16[240,128]{1,0:T(8,128)(2,1)S(1)} %get-tuple-element.71), channel_id=1, source_target_pairs={{0,24},{1,25},{2,26},{3,27},{4,28},{5,29},{6,30},{7,31},{8,16},{9,... | collective-permute-start | bytes 184328 | tf_op jit(solution)/shard_map/ppermute | solution.py:65
  80.2 5.5 %collective-permute-start.23 = (bf16[240,128]{1,0:T(8,128)(2,1)S(1)}, bf16[240,128]{1,0:T(8,128)(2,1)S(1)}, u32[]{:S(2)}, u32[]{:S(2)}) collective-permute-start(bf16[240,128]{1,0:T(8,128)(2,1)S(1)} %get-tuple-element.73), channel_id=1, source_target_pairs={{0,8},{1,9},{2,10},{3,11},{4,12},{5,13},{6,14},{7,15},{8,0},{9,1},... | collective-permute-start | bytes 184328 | tf_op jit(solution)/shard_map/ppermute | solution.py:65
  80.2 5.5 %collective-permute-start.24 = (bf16[240,128]{1,0:T(8,128)(2,1)S(1)}, bf16[240,128]{1,0:T(8,128)(2,1)S(1)}, u32[]{:S(2)}, u32[]{:S(2)}) collective-permute-start(bf16[240,128]{1,0:T(8,128)(2,1)S(1)} %get-tuple-element.74), channel_id=1, source_target_pairs={{0,16},{1,17},{2,18},{3,19},{4,20},{5,21},{6,22},{7,23},{8,24},{9,... | collective-permute-start | bytes 184328 | tf_op jit(solution)/shard_map/ppermute | solution.py:65
  (6 other events, 73.1 us)

commit v5 on v4

--- a/solution.py
+++ b/solution.py
@@ -496,7 +496,7 @@
                 target[pl.ds(at, wide), 128 * j : 128 * j + 128] = value.astype(BF16)
             return 0
 
-        lax.fori_loop(0, 6, one, 0)
+        lax.fori_loop(0, 6, one, 0, unroll=2)
 
     def convolve(source, weights, turned, halo, steps, finish):
         start = (ABOVE - halo) * pitch

time: 86.9 us -> 86.8 us (level)
  no operation moved by 1% of the time
where the time goes in v5:
time: 86.8 us; the launch traced here: 86.5 us
  starting transfers between devices  41.3 us (48%)
  Pallas kernels  23.4 us (27%)
  waiting for transfers between devices  17.3 us (20%)
  local copies, waits for them, and re-layouts  2.39 us (3%)
  other arithmetic  1.22 us (1%)
    ppermute x21, starting transfers between devices, send(): return lax.ppermute(value, BOTH, pairs)  31.4 us
    pallas_call x2, Pallas kernels, call(): pl.pallas_call(functools.partial(level, shape, devices, parts, second, na...  20.2 us
    ppermute x21, waiting for transfers between devices, send(): return lax.ppermute(value, BOTH, pairs)  17.3 us
    ppermute x4, starting transfers between devices, lengthways(): return (lax.ppermute(south, LAT, down), lax.ppermute(north, LAT, up))  6.91 us
    ppermute x1, starting transfers between devices, sideways(): return lax.ppermute(packed, 'lon', east)  3 us
    unnamed x8, local copies, waits for them, and re-layouts  2.27 us
    pallas_call x1, Pallas kernels, local(): pl.pallas_call(functools.partial(prepare, rows, cols), out_shape=(jax.Sha...  1.95 us
  transfers between devices with their start and end apart: 26, of which 13 were waited for; matrix products, arithmetic and copies ran while one was open for 1% of the time, Pallas kernels for 9%

profile of v5, /device:TPU:0, one launch (start us, length us, event | category | flops | bytes accessed | tf_op | source)
XLA Modules:
  0.0 86.5 jit_solution(363811570831097461)
XLA Ops:
  3.4 3.0 %collective-permute-start.5 = (bf16[1536,128]{1,0:T(8,128)(2,1)S(1)}, bf16[1536,128]{1,0:T(8,128)(2,1)S(1)}, u32[]{:S(2)}, u32[]{:S(2)}) collective-permute-start(bf16[1536,128]{1,0:T(8,128)(2,1)S(1)} %get-tuple-element.37), channel_id=1, source_target_pairs={{0,1},{1,0},{2,3},{3,2},{4,5},{5,4},{6,7},{7,6},{8,9},{9,8},{10,11... | collective-permute-start | bytes 1179656 | tf_op jit(solution)/shard_map/ppermute | solution.py:200
  7.1 2.7 %collective-permute-start.1 = (bf16[224,128]{1,0:T(8,128)(2,1)S(1)}, bf16[224,128]{1,0:T(8,128)(2,1)S(1)}, u32[]{:S(2)}, u32[]{:S(2)}) collective-permute-start(bf16[224,128]{1,0:T(8,128)(2,1)S(1)} %get-tuple-element.76), channel_id=1, source_target_pairs={{0,16},{1,17},{2,18},{3,19},{4,20},{5,21},{6,22},{7,23},{8,24},{9,... | collective-permute-start | bytes 172040 | tf_op jit(solution)/shard_map/ppermute | solution.py:65
  11.1 3.0 %collective-permute-start.3 = (bf16[704,128]{1,0:T(8,128)(2,1)S(1)}, bf16[704,128]{1,0:T(8,128)(2,1)S(1)}, u32[]{:S(2)}, u32[]{:S(2)}) collective-permute-start(bf16[704,128]{1,0:T(8,128)(2,1)S(1)} %get-tuple-element.35), channel_id=1, source_target_pairs={{0,2},{2,4},{4,6},{6,8},{8,10},{10,12},{12,14},{14,16},{16,18},{18... | collective-permute-start | bytes 540680 | tf_op jit(solution)/shard_map/ppermute | solution.py:210
  14.1 1.6 %collective-permute-start = (bf16[224,128]{1,0:T(8,128)(2,1)S(1)}, bf16[224,128]{1,0:T(8,128)(2,1)S(1)}, u32[]{:S(2)}, u32[]{:S(2)}) collective-permute-start(bf16[224,128]{1,0:T(8,128)(2,1)S(1)} %get-tuple-element.76), channel_id=1, source_target_pairs={{0,8},{1,9},{2,10},{3,11},{4,12},{5,13},{6,14},{7,15},{8,0},{9,1},... | collective-permute-start | bytes 172040 | tf_op jit(solution)/shard_map/ppermute | solution.py:65
  15.8 2.3 %collective-permute-start.2 = (bf16[224,128]{1,0:T(8,128)(2,1)S(1)}, bf16[224,128]{1,0:T(8,128)(2,1)S(1)}, u32[]{:S(2)}, u32[]{:S(2)}) collective-permute-start(bf16[224,128]{1,0:T(8,128)(2,1)S(1)} %get-tuple-element.76), channel_id=1, source_target_pairs={{0,24},{1,25},{2,26},{3,27},{4,28},{5,29},{6,30},{7,31},{8,16},{9,... | collective-permute-start | bytes 172040 | tf_op jit(solution)/shard_map/ppermute | solution.py:65
  18.8 3.4 %collective-permute-done.2 = bf16[224,128]{1,0:T(8,128)(2,1)S(1)} collective-permute-done((bf16[224,128]{1,0:T(8,128)(2,1)S(1)}, bf16[224,128]{1,0:T(8,128)(2,1)S(1)}, u32[]{:S(2)}, u32[]{:S(2)}) %collective-permute-start.2) | collective-permute-done | bytes 57376 | tf_op jit(solution)/shard_map/ppermute | solution.py:65
  22.3 1.5 %collective-permute-start.8 = (bf16[4,224,128]{2,1,0:T(8,128)(2,1)S(1)}, bf16[4,224,128]{2,1,0:T(8,128)(2,1)S(1)}, u32[]{:S(2)}, u32[]{:S(2)}) collective-permute-start(bf16[4,224,128]{2,1,0:T(8,128)(2,1)S(1)} %pad_maximum_fusion.refs_2_.refs_3_), channel_id=1, source_target_pairs={{0,5},{1,4},{2,7},{3,6},{4,1},{5,0},{6,3},{7,2},{8,13},{9,12},{10,... | collective-permute-start | bytes 688136 | tf_op jit(solution)/shard_map/ppermute | solution.py:65
  24.4 1.5 %collective-permute-start.6 = (bf16[4,224,128]{2,1,0:T(8,128)(2,1)S(1)}, bf16[4,224,128]{2,1,0:T(8,128)(2,1)S(1)}, u32[]{:S(2)}, u32[]{:S(2)}) collective-permute-start(bf16[4,224,128]{2,1,0:T(8,128)(2,1)S(1)} %pad_maximum_fusion.refs_2_.refs_3_), channel_id=1, source_target_pairs={{0,1},{1,0},{2,3},{3,2},{4,5},{5,4},{6,7},{7,6},{8,9},{9,8},{10,11... | collective-permute-start | bytes 688136 | tf_op jit(solution)/shard_map/ppermute | solution.py:65
  25.9 1.3 %collective-permute-start.9 = (bf16[464,128]{1,0:T(8,128)(2,1)S(1)}, bf16[464,128]{1,0:T(8,128)(2,1)S(1)}, u32[]{:S(2)}, u32[]{:S(2)}) collective-permute-start(bf16[464,128]{1,0:T(8,128)(2,1)S(1)} %get-tuple-element.42), channel_id=1, source_target_pairs={{0,2},{2,4},{4,6},{6,8},{8,10},{10,12},{12,14},{14,16},{16,18},{18... | collective-permute-start | bytes 356360 | tf_op jit(solution)/shard_map/ppermute | solution.py:210
  28.5 8.2 %collective-permute-start.11 = (bf16[4,224,128]{2,1,0:T(8,128)(2,1)S(1)}, bf16[4,224,128]{2,1,0:T(8,128)(2,1)S(1)}, u32[]{:S(2)}, u32[]{:S(2)}) collective-permute-start(bf16[4,224,128]{2,1,0:T(8,128)(2,1)S(1)} %pad_maximum_fusion.refs_2_.refs_3_), channel_id=1, source_target_pairs={{0,2},{1,3},{2,0},{3,1},{4,6},{5,7},{6,4},{7,5},{8,10},{9,11},{10,... | collective-permute-start | bytes 688136 | tf_op jit(solution)/shard_map/ppermute | solution.py:65
  36.7 2.0 %shard_map.94 = (bf16[2112,768]{1,0:T(8,128)(2,1)S(1)}, bf16[2112,256]{1,0:T(8,128)(2,1)S(1)}) custom-call(bf16[64,64,128]{2,1,0:T(8,128)(2,1)S(1)} %copy-done.1, bf16[32,32,192]{2,1,0:T(8,128)(2,1)S(1)} %copy-done.3, bf16[1536,128]{1,0:T(8,128)(2,1)S(1)} %collective-permute-done.5.side_ref, bf16[704,128]{1,0:T(8,128)(2,1)S(1)} %collective-permute-done.3.south_ref, ...), custom_call_target="tpu_custom_call" | custom-call | bytes 12582912 | tf_op jit(solution)/shard_map/pallas_call | solution.py:766
  40.9 14.1 %shard_map.95 = (bf16[32,32,192]{2,1,0:T(8,128)(2,1)}, bf16[2,16,176,128]{3,2,1,0:T(8,128)(2,1)S(1)}, f32[2128,128]{1,0:T(8,128)S(1)}, f32[2128,128]{1,0:T(8,128)S(1)}) custom-call(bf16[2112,768]{1,0:T(8,128)(2,1)S(1)} %get-tuple-element.46.refs_0_, bf16[2112,256]{1,0:T(8,128)(2,1)S(1)} %get-tuple-element.47.refs_1_, ...), custom_call_target="tpu_custom_call" | custom-call | flops 5000000000 | bytes 12582912 | tf_op jit(solution)/shard_map/pallas_call | solution.py:808
  55.3 2.0 %collective-permute-done.15 = bf16[16,176,128]{2,1,0:T(8,128)(2,1)S(1)} collective-permute-done((bf16[16,176,128]{2,1,0:T(8,128)(2,1)S(1)}, bf16[16,176,128]{2,1,0:T(8,128)(2,1)S(1)}, u32[]{:S(2)}, u32[]{:S(2)}) %collective-permute-start.15) | collective-permute-done | bytes 720928 | tf_op jit(solution)/shard_map/ppermute | solution.py:65
  57.5 1.4 %collective-permute-start.16 = (bf16[4,176,128]{2,1,0:T(8,128)(2,1)S(1)}, bf16[4,176,128]{2,1,0:T(8,128)(2,1)S(1)}, u32[]{:S(2)}, u32[]{:S(2)}) collective-permute-start(bf16[4,176,128]{2,1,0:T(8,128)(2,1)S(1)} %get-tuple-element.65), channel_id=1, source_target_pairs={{0,1},{1,0},{2,3},{3,2},{4,5},{5,4},{6,7},{7,6},{8,9},{9,8},{10,11... | collective-permute-start | bytes 540680 | tf_op jit(solution)/shard_map/ppermute | solution.py:65
  58.9 2.7 %collective-permute-start.18 = (bf16[4,176,128]{2,1,0:T(8,128)(2,1)S(1)}, bf16[4,176,128]{2,1,0:T(8,128)(2,1)S(1)}, u32[]{:S(2)}, u32[]{:S(2)}) collective-permute-start(bf16[4,176,128]{2,1,0:T(8,128)(2,1)S(1)} %get-tuple-element.66), channel_id=1, source_target_pairs={{0,5},{1,4},{2,7},{3,6},{4,1},{5,0},{6,3},{7,2},{8,13},{9,12},{10,... | collective-permute-start | bytes 540680 | tf_op jit(solution)/shard_map/ppermute | solution.py:65
  61.6 6.1 %shard_map.96 = (bf16[64,64,128]{2,1,0:T(8,128)(2,1)}, bf16[2,16,64,128]{3,2,1,0:T(8,128)(2,1)S(1)}) custom-call(bf16[2112,768]{1,0:T(8,128)(2,1)S(1)} %get-tuple-element.46.refs_0_, f32[2128,128]{1,0:T(8,128)S(1)} %get-tuple-element.55.refs_1_, f32[2128,128]{1,0:T(8,128)S(1)} %get-tuple-element.56.refs_2_, ...), custom_call_target="tpu_custom_call" | custom-call | flops 2000000000 | bytes 12582912 | tf_op jit(solution)/shard_map/pallas_call | solution.py:808
  67.9 2.5 %collective-permute-done.18 = bf16[4,176,128]{2,1,0:T(8,128)(2,1)S(1)} collective-permute-done((bf16[4,176,128]{2,1,0:T(8,128)(2,1)S(1)}, bf16[4,176,128]{2,1,0:T(8,128)(2,1)S(1)}, u32[]{:S(2)}, u32[]{:S(2)}) %collective-permute-start.18) | collective-permute-done | bytes 180256 | tf_op jit(solution)/shard_map/ppermute | solution.py:65
  70.4 1.4 %collective-permute-done.17 = bf16[4,176,128]{2,1,0:T(8,128)(2,1)S(1)} collective-permute-done((bf16[4,176,128]{2,1,0:T(8,128)(2,1)S(1)}, bf16[4,176,128]{2,1,0:T(8,128)(2,1)S(1)}, u32[]{:S(2)}, u32[]{:S(2)}) %collective-permute-start.17) | collective-permute-done | bytes 180256 | tf_op jit(solution)/shard_map/ppermute | solution.py:65
  71.9 1.4 %collective-permute-start.20 = (bf16[4,64,128]{2,1,0:T(8,128)(2,1)S(1)}, bf16[4,64,128]{2,1,0:T(8,128)(2,1)S(1)}, u32[]{:S(2)}, u32[]{:S(2)}) collective-permute-start(bf16[4,64,128]{2,1,0:T(8,128)(2,1)S(1)} %get-tuple-element.68), channel_id=1, source_target_pairs={{0,1},{1,0},{2,3},{3,2},{4,5},{5,4},{6,7},{7,6},{8,9},{9,8},{10,11... | collective-permute-start | bytes 196616 | tf_op jit(solution)/shard_map/ppermute | solution.py:65
  73.7 1.7 %collective-permute-start.21 = (bf16[4,64,128]{2,1,0:T(8,128)(2,1)S(1)}, bf16[4,64,128]{2,1,0:T(8,128)(2,1)S(1)}, u32[]{:S(2)}, u32[]{:S(2)}) collective-permute-start(bf16[4,64,128]{2,1,0:T(8,128)(2,1)S(1)} %get-tuple-element.70), channel_id=1, source_target_pairs={{0,4},{1,5},{2,6},{3,7},{4,0},{5,1},{6,2},{7,3},{8,12},{9,13},{10,... | collective-permute-start | bytes 196616 | tf_op jit(solution)/shard_map/ppermute | solution.py:65
  76.3 2.3 %collective-permute-done.22 = bf16[4,64,128]{2,1,0:T(8,128)(2,1)S(1)} collective-permute-done((bf16[4,64,128]{2,1,0:T(8,128)(2,1)S(1)}, bf16[4,64,128]{2,1,0:T(8,128)(2,1)S(1)}, u32[]{:S(2)}, u32[]{:S(2)}) %collective-permute-start.22) | collective-permute-done | bytes 65568 | tf_op jit(solution)/shard_map/ppermute | solution.py:65
  78.8 1.4 %collective-permute-start.25 = (bf16[240,128]{1,0:T(8,128)(2,1)S(1)}, bf16[240,128]{1,0:T(8,128)(2,1)S(1)}, u32[]{:S(2)}, u32[]{:S(2)}) collective-permute-start(bf16[240,128]{1,0:T(8,128)(2,1)S(1)} %get-tuple-element.71), channel_id=1, source_target_pairs={{0,24},{1,25},{2,26},{3,27},{4,28},{5,29},{6,30},{7,31},{8,16},{9,... | collective-permute-start | bytes 184328 | tf_op jit(solution)/shard_map/ppermute | solution.py:65
  80.2 3.1 %collective-permute-start.24 = (bf16[240,128]{1,0:T(8,128)(2,1)S(1)}, bf16[240,128]{1,0:T(8,128)(2,1)S(1)}, u32[]{:S(2)}, u32[]{:S(2)}) collective-permute-start(bf16[240,128]{1,0:T(8,128)(2,1)S(1)} %get-tuple-element.74), channel_id=1, source_target_pairs={{0,16},{1,17},{2,18},{3,19},{4,20},{5,21},{6,22},{7,23},{8,24},{9,... | collective-permute-start | bytes 184328 | tf_op jit(solution)/shard_map/ppermute | solution.py:65
  83.2 1.7 %collective-permute-done.25.refs_3_ = bf16[240,128]{1,0:T(8,128)(2,1)S(1)} collective-permute-done((bf16[240,128]{1,0:T(8,128)(2,1)S(1)}, bf16[240,128]{1,0:T(8,128)(2,1)S(1)}, u32[]{:S(2)}, u32[]{:S(2)}) %collective-permute-start.25) | collective-permute-done | bytes 61472 | tf_op jit(solution)/shard_map/ppermute | solution.py:65
  (54 shorter events, 13.4 us)
Async XLA Ops:
  3.4 19.0 %collective-permute-start.5 = (bf16[1536,128]{1,0:T(8,128)(2,1)S(1)}, bf16[1536,128]{1,0:T(8,128)(2,1)S(1)}, u32[]{:S(2)}, u32[]{:S(2)}) collective-permute-start(bf16[1536,128]{1,0:T(8,128)(2,1)S(1)} %get-tuple-element.37), channel_id=1, source_target_pairs={{0,1},{1,0},{2,3},{3,2},{4,5},{5,4},{6,7},{7,6},{8,9},{9,8},{10,11... | collective-permute-start | bytes 1179656 | tf_op jit(solution)/shard_map/ppermute | solution.py:200
  7.1 8.6 %collective-permute-start.1 = (bf16[224,128]{1,0:T(8,128)(2,1)S(1)}, bf16[224,128]{1,0:T(8,128)(2,1)S(1)}, u32[]{:S(2)}, u32[]{:S(2)}) collective-permute-start(bf16[224,128]{1,0:T(8,128)(2,1)S(1)} %get-tuple-element.76), channel_id=1, source_target_pairs={{0,16},{1,17},{2,18},{3,19},{4,20},{5,21},{6,22},{7,23},{8,24},{9,... | collective-permute-start | bytes 172040 | tf_op jit(solution)/shard_map/ppermute | solution.py:65
  9.8 12.5 %collective-permute-start.4 = (bf16[832,128]{1,0:T(8,128)(2,1)S(1)}, bf16[832,128]{1,0:T(8,128)(2,1)S(1)}, u32[]{:S(2)}, u32[]{:S(2)}) collective-permute-start(bf16[832,128]{1,0:T(8,128)(2,1)S(1)} %get-tuple-element.36), channel_id=1, source_target_pairs={{2,0},{4,2},{6,4},{8,6},{10,8},{12,10},{14,12},{16,14},{18,16},{20... | collective-permute-start | bytes 638984 | tf_op jit(solution)/shard_map/ppermute | solution.py:210
  11.1 11.2 %collective-permute-start.3 = (bf16[704,128]{1,0:T(8,128)(2,1)S(1)}, bf16[704,128]{1,0:T(8,128)(2,1)S(1)}, u32[]{:S(2)}, u32[]{:S(2)}) collective-permute-start(bf16[704,128]{1,0:T(8,128)(2,1)S(1)} %get-tuple-element.35), channel_id=1, source_target_pairs={{0,2},{2,4},{4,6},{6,8},{8,10},{10,12},{12,14},{14,16},{16,18},{18... | collective-permute-start | bytes 540680 | tf_op jit(solution)/shard_map/ppermute | solution.py:210
  14.1 4.7 %collective-permute-start = (bf16[224,128]{1,0:T(8,128)(2,1)S(1)}, bf16[224,128]{1,0:T(8,128)(2,1)S(1)}, u32[]{:S(2)}, u32[]{:S(2)}) collective-permute-start(bf16[224,128]{1,0:T(8,128)(2,1)S(1)} %get-tuple-element.76), channel_id=1, source_target_pairs={{0,8},{1,9},{2,10},{3,11},{4,12},{5,13},{6,14},{7,15},{8,0},{9,1},... | collective-permute-start | bytes 172040 | tf_op jit(solution)/shard_map/ppermute | solution.py:65
  15.8 6.5 %collective-permute-start.2 = (bf16[224,128]{1,0:T(8,128)(2,1)S(1)}, bf16[224,128]{1,0:T(8,128)(2,1)S(1)}, u32[]{:S(2)}, u32[]{:S(2)}) collective-permute-start(bf16[224,128]{1,0:T(8,128)(2,1)S(1)} %get-tuple-element.76), channel_id=1, source_target_pairs={{0,24},{1,25},{2,26},{3,27},{4,28},{5,29},{6,30},{7,31},{8,16},{9,... | collective-permute-start | bytes 172040 | tf_op jit(solution)/shard_map/ppermute | solution.py:65
  22.3 16.4 %collective-permute-start.8 = (bf16[4,224,128]{2,1,0:T(8,128)(2,1)S(1)}, bf16[4,224,128]{2,1,0:T(8,128)(2,1)S(1)}, u32[]{:S(2)}, u32[]{:S(2)}) collective-permute-start(bf16[4,224,128]{2,1,0:T(8,128)(2,1)S(1)} %pad_maximum_fusion.refs_2_.refs_3_), channel_id=1, source_target_pairs={{0,5},{1,4},{2,7},{3,6},{4,1},{5,0},{6,3},{7,2},{8,13},{9,12},{10,... | collective-permute-start | bytes 688136 | tf_op jit(solution)/shard_map/ppermute | solution.py:65
  23.8 14.9 %collective-permute-start.7 = (bf16[4,224,128]{2,1,0:T(8,128)(2,1)S(1)}, bf16[4,224,128]{2,1,0:T(8,128)(2,1)S(1)}, u32[]{:S(2)}, u32[]{:S(2)}) collective-permute-start(bf16[4,224,128]{2,1,0:T(8,128)(2,1)S(1)} %pad_maximum_fusion.refs_2_.refs_3_), channel_id=1, source_target_pairs={{0,4},{1,5},{2,6},{3,7},{4,0},{5,1},{6,2},{7,3},{8,12},{9,13},{10,... | collective-permute-start | bytes 688136 | tf_op jit(solution)/shard_map/ppermute | solution.py:65
  24.4 14.3 %collective-permute-start.6 = (bf16[4,224,128]{2,1,0:T(8,128)(2,1)S(1)}, bf16[4,224,128]{2,1,0:T(8,128)(2,1)S(1)}, u32[]{:S(2)}, u32[]{:S(2)}) collective-permute-start(bf16[4,224,128]{2,1,0:T(8,128)(2,1)S(1)} %pad_maximum_fusion.refs_2_.refs_3_), channel_id=1, source_target_pairs={{0,1},{1,0},{2,3},{3,2},{4,5},{5,4},{6,7},{7,6},{8,9},{9,8},{10,11... | collective-permute-start | bytes 688136 | tf_op jit(solution)/shard_map/ppermute | solution.py:65
  25.9 2.6 %collective-permute-start.9 = (bf16[464,128]{1,0:T(8,128)(2,1)S(1)}, bf16[464,128]{1,0:T(8,128)(2,1)S(1)}, u32[]{:S(2)}, u32[]{:S(2)}) collective-permute-start(bf16[464,128]{1,0:T(8,128)(2,1)S(1)} %get-tuple-element.42), channel_id=1, source_target_pairs={{0,2},{2,4},{4,6},{6,8},{8,10},{10,12},{12,14},{14,16},{16,18},{18... | collective-permute-start | bytes 356360 | tf_op jit(solution)/shard_map/ppermute | solution.py:210
  27.2 9.5 %collective-permute-start.10 = (bf16[464,128]{1,0:T(8,128)(2,1)S(1)}, bf16[464,128]{1,0:T(8,128)(2,1)S(1)}, u32[]{:S(2)}, u32[]{:S(2)}) collective-permute-start(bf16[464,128]{1,0:T(8,128)(2,1)S(1)} %get-tuple-element.43), channel_id=1, source_target_pairs={{2,0},{4,2},{6,4},{8,6},{10,8},{12,10},{14,12},{16,14},{18,16},{20... | collective-permute-start | bytes 356360 | tf_op jit(solution)/shard_map/ppermute | solution.py:210
  28.5 10.9 %collective-permute-start.11 = (bf16[4,224,128]{2,1,0:T(8,128)(2,1)S(1)}, bf16[4,224,128]{2,1,0:T(8,128)(2,1)S(1)}, u32[]{:S(2)}, u32[]{:S(2)}) collective-permute-start(bf16[4,224,128]{2,1,0:T(8,128)(2,1)S(1)} %pad_maximum_fusion.refs_2_.refs_3_), channel_id=1, source_target_pairs={{0,2},{1,3},{2,0},{3,1},{4,6},{5,7},{6,4},{7,5},{8,10},{9,11},{10,... | collective-permute-start | bytes 688136 | tf_op jit(solution)/shard_map/ppermute | solution.py:65
  38.9 1.7 %collective-permute-start.13 = (bf16[4,224,128]{2,1,0:T(8,128)(2,1)S(1)}, bf16[4,224,128]{2,1,0:T(8,128)(2,1)S(1)}, u32[]{:S(2)}, u32[]{:S(2)}) collective-permute-start(bf16[4,224,128]{2,1,0:T(8,128)(2,1)S(1)} %collective-permute-done.7.refs_4_.refs_5_), channel_id=1, source_target_pairs={{0,2},{1,3},{2,0},{3,1},{4,6},{5,7},{6,4},{7,5},{8,10},{9,11},{10,... | collective-permute-start | bytes 688136 | tf_op jit(solution)/shard_map/ppermute | solution.py:65
  55.1 2.3 %collective-permute-start.15 = (bf16[16,176,128]{2,1,0:T(8,128)(2,1)S(1)}, bf16[16,176,128]{2,1,0:T(8,128)(2,1)S(1)}, u32[]{:S(2)}, u32[]{:S(2)}) collective-permute-start(bf16[16,176,128]{2,1,0:T(8,128)(2,1)S(1)} %slice_bitcast_fusion), channel_id=1, source_target_pairs={{0,2},{1,3},{2,0},{3,1},{4,6},{5,7},{6,4},{7,5},{8,10},{9,11},{10,... | collective-permute-start | bytes 2162696 | tf_op jit(solution)/shard_map/ppermute | solution.py:65
  57.5 10.3 %collective-permute-start.16 = (bf16[4,176,128]{2,1,0:T(8,128)(2,1)S(1)}, bf16[4,176,128]{2,1,0:T(8,128)(2,1)S(1)}, u32[]{:S(2)}, u32[]{:S(2)}) collective-permute-start(bf16[4,176,128]{2,1,0:T(8,128)(2,1)S(1)} %get-tuple-element.65), channel_id=1, source_target_pairs={{0,1},{1,0},{2,3},{3,2},{4,5},{5,4},{6,7},{7,6},{8,9},{9,8},{10,11... | collective-permute-start | bytes 540680 | tf_op jit(solution)/shard_map/ppermute | solution.py:65
  58.9 11.4 %collective-permute-start.18 = (bf16[4,176,128]{2,1,0:T(8,128)(2,1)S(1)}, bf16[4,176,128]{2,1,0:T(8,128)(2,1)S(1)}, u32[]{:S(2)}, u32[]{:S(2)}) collective-permute-start(bf16[4,176,128]{2,1,0:T(8,128)(2,1)S(1)} %get-tuple-element.66), channel_id=1, source_target_pairs={{0,5},{1,4},{2,7},{3,6},{4,1},{5,0},{6,3},{7,2},{8,13},{9,12},{10,... | collective-permute-start | bytes 540680 | tf_op jit(solution)/shard_map/ppermute | solution.py:65
  61.6 10.1 %collective-permute-start.17 = (bf16[4,176,128]{2,1,0:T(8,128)(2,1)S(1)}, bf16[4,176,128]{2,1,0:T(8,128)(2,1)S(1)}, u32[]{:S(2)}, u32[]{:S(2)}) collective-permute-start(bf16[4,176,128]{2,1,0:T(8,128)(2,1)S(1)} %get-tuple-element.67), channel_id=1, source_target_pairs={{0,4},{1,5},{2,6},{3,7},{4,0},{5,1},{6,2},{7,3},{8,12},{9,13},{10,... | collective-permute-start | bytes 540680 | tf_op jit(solution)/shard_map/ppermute | solution.py:65
  67.8 4.0 %collective-permute-start.19 = (bf16[16,64,128]{2,1,0:T(8,128)(2,1)S(1)}, bf16[16,64,128]{2,1,0:T(8,128)(2,1)S(1)}, u32[]{:S(2)}, u32[]{:S(2)}) collective-permute-start(bf16[16,64,128]{2,1,0:T(8,128)(2,1)S(1)} %slice_bitcast_fusion.1), channel_id=1, source_target_pairs={{0,2},{1,3},{2,0},{3,1},{4,6},{5,7},{6,4},{7,5},{8,10},{9,11},{10,... | collective-permute-start | bytes 786440 | tf_op jit(solution)/shard_map/ppermute | solution.py:65
  71.9 4.3 %collective-permute-start.20 = (bf16[4,64,128]{2,1,0:T(8,128)(2,1)S(1)}, bf16[4,64,128]{2,1,0:T(8,128)(2,1)S(1)}, u32[]{:S(2)}, u32[]{:S(2)}) collective-permute-start(bf16[4,64,128]{2,1,0:T(8,128)(2,1)S(1)} %get-tuple-element.68), channel_id=1, source_target_pairs={{0,1},{1,0},{2,3},{3,2},{4,5},{5,4},{6,7},{7,6},{8,9},{9,8},{10,11... | collective-permute-start | bytes 196616 | tf_op jit(solution)/shard_map/ppermute | solution.py:65
  73.3 5.3 %collective-permute-start.22 = (bf16[4,64,128]{2,1,0:T(8,128)(2,1)S(1)}, bf16[4,64,128]{2,1,0:T(8,128)(2,1)S(1)}, u32[]{:S(2)}, u32[]{:S(2)}) collective-permute-start(bf16[4,64,128]{2,1,0:T(8,128)(2,1)S(1)} %get-tuple-element.69), channel_id=1, source_target_pairs={{0,5},{1,4},{2,7},{3,6},{4,1},{5,0},{6,3},{7,2},{8,13},{9,12},{10,... | collective-permute-start | bytes 196616 | tf_op jit(solution)/shard_map/ppermute | solution.py:65
  73.7 5.0 %collective-permute-start.21 = (bf16[4,64,128]{2,1,0:T(8,128)(2,1)S(1)}, bf16[4,64,128]{2,1,0:T(8,128)(2,1)S(1)}, u32[]{:S(2)}, u32[]{:S(2)}) collective-permute-start(bf16[4,64,128]{2,1,0:T(8,128)(2,1)S(1)} %get-tuple-element.70), channel_id=1, source_target_pairs={{0,4},{1,5},{2,6},{3,7},{4,0},{5,1},{6,2},{7,3},{8,12},{9,13},{10,... | collective-permute-start | bytes 196616 | tf_op jit(solution)/shard_map/ppermute | solution.py:65
  78.8 6.2 %collective-permute-start.25 = (bf16[240,128]{1,0:T(8,128)(2,1)S(1)}, bf16[240,128]{1,0:T(8,128)(2,1)S(1)}, u32[]{:S(2)}, u32[]{:S(2)}) collective-permute-start(bf16[240,128]{1,0:T(8,128)(2,1)S(1)} %get-tuple-element.71), channel_id=1, source_target_pairs={{0,24},{1,25},{2,26},{3,27},{4,28},{5,29},{6,30},{7,31},{8,16},{9,... | collective-permute-start | bytes 184328 | tf_op jit(solution)/shard_map/ppermute | solution.py:65
  80.2 5.5 %collective-permute-start.23 = (bf16[240,128]{1,0:T(8,128)(2,1)S(1)}, bf16[240,128]{1,0:T(8,128)(2,1)S(1)}, u32[]{:S(2)}, u32[]{:S(2)}) collective-permute-start(bf16[240,128]{1,0:T(8,128)(2,1)S(1)} %get-tuple-element.73), channel_id=1, source_target_pairs={{0,8},{1,9},{2,10},{3,11},{4,12},{5,13},{6,14},{7,15},{8,0},{9,1},... | collective-permute-start | bytes 184328 | tf_op jit(solution)/shard_map/ppermute | solution.py:65
  80.2 5.5 %collective-permute-start.24 = (bf16[240,128]{1,0:T(8,128)(2,1)S(1)}, bf16[240,128]{1,0:T(8,128)(2,1)S(1)}, u32[]{:S(2)}, u32[]{:S(2)}) collective-permute-start(bf16[240,128]{1,0:T(8,128)(2,1)S(1)} %get-tuple-element.74), channel_id=1, source_target_pairs={{0,16},{1,17},{2,18},{3,19},{4,20},{5,21},{6,22},{7,23},{8,24},{9,... | collective-permute-start | bytes 184328 | tf_op jit(solution)/shard_map/ppermute | solution.py:65
  (6 other events, 73.1 us)
